TPU v7x, 512 devices: a whole 4x8x8 slice. The times are simulated.
512 devices in a mesh: rows: 16 (over z, core), protos: 32 (over x, y).
Axes of the slice: x: 4, y: 8, z: 8, core: 2. Of those that a mesh axis runs over, the one named last changes fastest.
Arguments:
- student_patches: bfloat16 [128, 256, 256], P('rows'), may hold values from -120 to 120
- teacher_patches: bfloat16 [128, 256, 256], P('rows'), may hold values from -120 to 120
- mask_index: int32 [128, 128], P('rows'), may hold values from 0 to 255, as said below
- student_weight: bfloat16 [256, 65536], P(None, 'protos'), may hold values from -140 to 140
- teacher_weight: bfloat16 [256, 65536], P(None, 'protos'), may hold values from -140 to 140
Outputs:
- grad_patches: float32 [128, 256, 256], P('rows', 'protos')
- grad_weight: float32 [256, 65536], P('rows', 'protos')
Inputs may be any that keep to these rules, and one draw needn't show every extreme that they name: `mask_index`: each image's 128 entries are distinct patch positions in increasing order.
All inputs are finite; a program needn't handle non-finite values.
Results may differ from a plain program's by a relative error of at most 0.0029.
Values sent between devices are 32-bit elements; how exact they have to be, the bound alone decides.
No kernel may reach another device: no remote copies, remote signals or barrier semaphores. Data moves between devices by JAX's collectives and lax.ppermute only.
A program may use at most 128 MiB of HBM per device.

v0:
```python
import jax
import jax.numpy as jnp
from jax import lax
from jax.sharding import PartitionSpec as P

PROTOS = 65536
SK_ITERS = 3


epsilon = 1e-06
temp_student = 0.1
temp_teacher = 0.07


def unit_rows(values):
    values = values.astype(jnp.float32)
    length = jnp.sqrt(jnp.sum(values * values, axis=-1, keepdims=True) + epsilon)
    return (values / length, length)


def unit_columns(values):
    values = values.astype(jnp.float32)
    length = jnp.sqrt(jnp.sum(values * values, axis=0, keepdims=True) + epsilon)
    return (values / length, length)


def teacher_rows(row_part):
    return lax.psum(row_part, "protos")


def place_rows(values, mask_index, patches):
    images, masked, feature_width = values.shape
    image_index = lax.broadcasted_iota(jnp.int32, (images, masked), 0)
    return (
        jnp.zeros((images, patches, feature_width), jnp.float32)
        .at[image_index, mask_index]
        .set(values)
    )


def local(student_patches, teacher_patches, mask_index, student_weight, teacher_weight):
    images, patches, feature_width = student_patches.shape
    masked = mask_index.shape[1]
    local_rows = images * masked
    total_rows = local_rows * lax.axis_size("rows")
    local_protos = student_weight.shape[1]
    selector = mask_index[:, :, None]
    picked_student = jnp.take_along_axis(student_patches, selector, axis=1).reshape(
        local_rows, feature_width
    )
    picked_teacher = jnp.take_along_axis(teacher_patches, selector, axis=1).reshape(
        local_rows, feature_width
    )
    unit_student, norm_student = unit_rows(picked_student)
    student_unit = unit_student.astype(jnp.bfloat16)
    teacher_unit = unit_rows(picked_teacher)[0].astype(jnp.bfloat16)
    unit_weight, weight_norm = unit_columns(student_weight)
    weight_bf = unit_weight.astype(jnp.bfloat16)
    teacher_bf = unit_columns(teacher_weight)[0].astype(jnp.bfloat16)
    teacher_exp = jnp.exp(
        jnp.dot(teacher_unit, teacher_bf, preferred_element_type=jnp.float32) * (1.0 / temp_teacher)
    )
    logits = jnp.dot(student_unit, weight_bf, preferred_element_type=jnp.float32) * (
        1.0 / temp_student
    )
    student_part = jnp.sum(jnp.exp(logits), axis=1)
    student_total = lax.psum(student_part, "protos")
    row_scale = jnp.ones((local_rows,), jnp.float32)
    col_scale = jnp.ones((local_protos,), jnp.float32)

    def column_update(row_scale, col_scale):
        column_part = col_scale * jnp.dot(row_scale, teacher_exp, precision=lax.Precision.HIGHEST)
        column_sums = lax.psum(column_part, "rows")
        updated = col_scale / (column_sums * PROTOS)
        row_part = row_scale * jnp.dot(teacher_exp, updated, precision=lax.Precision.HIGHEST)
        return (updated, row_part)

    for sweep in range(SK_ITERS - 1):
        col_scale, row_part = column_update(row_scale, col_scale)
        row_scale = row_scale / (teacher_rows(row_part) * total_rows)
    col_scale, row_part = column_update(row_scale, col_scale)
    row_sums = teacher_rows(row_part)
    row_scale = row_scale / (row_sums * total_rows)
    target = teacher_exp * row_scale[:, None] * (col_scale * total_rows)[None, :]
    probabilities = jnp.exp(logits) / student_total[:, None]
    score_grad = ((probabilities - target) * (1.0 / temp_student)).astype(jnp.bfloat16)
    feature_part = lax.dot_general(
        score_grad, weight_bf, (((1,), (1,)), ((), ())), preferred_element_type=jnp.float32
    )
    proto_index = lax.axis_index("protos")
    patch_count = patches // lax.axis_size("protos")
    feature_sum = lax.psum(feature_part, "protos")
    projection = jnp.sum(unit_student * feature_sum, axis=1, keepdims=True)
    masked_grad = ((feature_sum - unit_student * projection) / norm_student).reshape(
        images, masked, feature_width
    )
    placed = place_rows(masked_grad, mask_index, patches)
    grad_patches = lax.dynamic_slice_in_dim(placed, proto_index * patch_count, patch_count, 1)
    share_rows = feature_width // lax.axis_size("rows")
    rows_index = lax.axis_index("rows")
    weight_share = lax.psum_scatter(
        lax.dot_general(
            student_unit, score_grad, (((0,), (0,)), ((), ())), preferred_element_type=jnp.float32
        ),
        "rows",
        scatter_dimension=0,
        tiled=True,
    )
    unit_share = lax.dynamic_slice_in_dim(unit_weight, rows_index * share_rows, share_rows, 0)
    column_dots = lax.psum(jnp.sum(unit_share * weight_share, axis=0), "rows")
    grad_weight = (weight_share - unit_share * column_dots[None, :]) / weight_norm
    return (grad_patches, grad_weight)


def solution(mesh):
    placed = (
        P("rows", None, None),
        P("rows", None, None),
        P("rows", None),
        P(None, "protos"),
        P(None, "protos"),
    )
    return jax.shard_map(
        local,
        mesh=mesh,
        in_specs=placed,
        out_specs=(P("rows", "protos", None), P("rows", "protos")),
        check_vma=False,
    )
```

profile of v0, /device:TPU:1, one launch (start us, length us, event | category | flops | bytes accessed | tf_op | source)
XLA Modules:
  0.0 590.5 jit_solution(545025184698509232)
XLA Ops:
  9.6 5.8 gather_fusion.1
  15.4 13.5 %gather_fusion = bf16[1024,256]{1,0:T(8,128)(2,1)S(1)} fusion(bf16[8,256,256]{2,1,0:T(8,128)(2,1)} %param.7, s32[1024]{0:T(1024)S(1)} %or_bitcast_fusion), kind=kCustom, calls=%fused_computation.clone | custom fusion | bytes 1056768 | tf_op jit(solution)/shard_map/jit(take_along_axis)/gather | solution.py:48
  31.9 3.2 copy-done.1
  35.1 4.0 fusion.22
  39.1 31.1 %psum.64 = f32[2048]{0:T(1024)S(1)} all-reduce(f32[2048]{0:T(1024)S(1)} %bitcast.64), channel_id=1, replica_groups=mesh['rows'=16,'protos'=32] {'rows'}, use_global_device_ids=true, to_apply=%region_6.0 | all-reduce | flops 2048 | bytes 16384 | tf_op jit(solution)/shard_map/psum | solution.py:73
  70.2 9.4 %fusion.27 = f32[1,1024]{1,0:T(1,128)S(1)} fusion(f32[1024,2048]{1,0:T(8,128)} %copy-done.1, f32[2048,1]{0,1:T(1,128)S(1)} %bitcast.65), kind=kOutput, calls=%fused_computation.67 | convolution fusion | flops 25165824 | bytes 8400896 | tf_op jit(solution)/shard_map/dot_general | solution.py:75
  79.6 61.3 %psum.65 = f32[1024]{0:T(1024)S(1)} all-reduce(f32[1024]{0:T(1024)S(1)} %bitcast.68), channel_id=1, replica_groups=mesh['rows'=16,'protos'=32] {'protos'}, use_global_device_ids=true, to_apply=%region_7.0 | all-reduce | flops 1024 | bytes 8192 | tf_op jit(solution)/shard_map/psum | solution.py:28
  140.9 6.3 %fusion.28 = f32[1,2048]{1,0:T(1,128)S(1)} fusion(f32[1024,1]{0,1:T(1,128)S(1)} %bitcast.69, f32[1024,2048]{1,0:T(8,128)} %copy-done.1), kind=kOutput, calls=%fused_computation.68 | convolution fusion | flops 25165824 | bytes 8400896 | tf_op jit(solution)/shard_map/dot_general | solution.py:72
  147.3 40.5 %psum.66 = f32[2048]{0:T(1024)S(1)} all-reduce(f32[2048]{0:T(1024)S(1)} %fusion.26), channel_id=1, replica_groups=mesh['rows'=16,'protos'=32] {'rows'}, use_global_device_ids=true, to_apply=%region_8.0 | all-reduce | flops 2048 | bytes 16384 | tf_op jit(solution)/shard_map/psum | solution.py:73
  187.8 9.4 %fusion.29 = f32[1,1024]{1,0:T(1,128)S(1)} fusion(f32[1024,2048]{1,0:T(8,128)} %copy-done.1, f32[2048,1]{0,1:T(1,128)S(1)} %bitcast.59), kind=kOutput, calls=%fused_computation.69 | convolution fusion | flops 25165824 | bytes 8400896 | tf_op jit(solution)/shard_map/dot_general | solution.py:75
  197.2 55.7 %psum.67 = f32[1024]{0:T(1024)S(1)} all-reduce(f32[1024]{0:T(1024)S(1)} %fusion.25), channel_id=1, replica_groups=mesh['rows'=16,'protos'=32] {'protos'}, use_global_device_ids=true, to_apply=%region_9.0 | all-reduce | flops 1024 | bytes 8192 | tf_op jit(solution)/shard_map/psum | solution.py:28
  252.9 6.4 %fusion.30 = f32[1,2048]{1,0:T(1,128)S(1)} fusion(f32[1024,1]{0,1:T(1,128)S(1)} %bitcast.60, f32[1024,2048]{1,0:T(8,128)} %copy-done.1), kind=kOutput, calls=%fused_computation.70 | convolution fusion | flops 25165824 | bytes 8400896 | tf_op jit(solution)/shard_map/dot_general | solution.py:72
  259.3 38.2 %psum.68 = f32[2048]{0:T(1024)S(1)} all-reduce(f32[2048]{0:T(1024)S(1)} %mul.119), channel_id=1, replica_groups=mesh['rows'=16,'protos'=32] {'rows'}, use_global_device_ids=true, to_apply=%region_10.0 | all-reduce | flops 2048 | bytes 16384 | tf_op jit(solution)/shard_map/psum | solution.py:73
  297.6 9.4 %fusion.31 = f32[1,1024]{1,0:T(1,128)S(1)} fusion(f32[1024,2048]{1,0:T(8,128)} %copy-done.1, f32[2048,1]{0,1:T(1,128)S(1)} %bitcast.61), kind=kOutput, calls=%fused_computation.71 | convolution fusion | flops 25165824 | bytes 8400896 | tf_op jit(solution)/shard_map/dot_general | solution.py:75
  307.2 4.7 fusion
  311.9 58.4 %all-reduce = (f32[1024]{0:T(1024)S(1)}, f32[1024]{0:T(1024)S(1)}) all-reduce(f32[1024]{0:T(1024)S(1)} %mul.121, f32[1024]{0:T(1024)S(1)} %get-tuple-element.11), channel_id=1, replica_groups=mesh['rows'=16,'protos'=32] {'protos'}, use_global_device_ids=true, to_apply=%region_11.0 | all-reduce | flops 2048 | bytes 16384 | tf_op jit(solution)/shard_map/psum | solution.py:28
  370.4 7.1 %multiply_convert_fusion = bf16[1024,2048]{1,0:T(8,128)(2,1)S(1)} fusion(f32[1024,2048]{1,0:T(8,128)} %copy-done.1, f32[1024,2048]{1,0:T(8,128)} %get-tuple-element.12, f32[2048]{0:T(1024)S(1)} %get-tuple-element.7, f32[1024]{0:T(1024)S(1)} %multiply_divide_fusion.2, f32[1024]{0:T(1024)S(1)} %get-tuple-element.6), kind=kLoop, calls=%fused_computation.3 | loop fusion | flops 14680064 | bytes 20987904 | tf_op jit(solution)/shard_map/convert_element_type | solution.py:86
  377.5 1.9 copy-done.2
  379.4 2.3 fusion.13
  381.8 4.8 fusion.18
  388.5 152.2 %all-reduce.3.cloned.1.call-done = f32[1024,256]{1,0:T(8,128)} async-done(((f32[1024,256]{1,0:T(8,128)}), f32[1024,256]{1,0:T(8,128)}) %all-reduce.3.cloned.1.call-update) | async-done | bytes 1048592 | tf_op jit(solution)/shard_map/psum | solution.py:92
  542.1 7.2 %scatter_custom_fusion = f32[2048,256]{1,0:T(8,128)} fusion(s32[1024]{0:T(1024)S(1)} %select_bitcast_fusion, f32[]{:T(128)} %constant.22.clone.1, f32[1024,256]{1,0:T(8,128)} %all-reduce.3.cloned.1.call-done, f32[1024,256]{1,0:T(8,128)S(1)} %get-tuple-element.14, f32[1024]{0:T(1024)S(1)} %multiply_reduce_fusion, f32[1024]{0:T(1024)S(1)} %sqrt_bitcast_fusion.1), kind=kCustom, calls=%fused_computation.17 | custom fusion | flops 786432 | bytes 4202500
  551.7 29.7 %psum.71 = f32[2048]{0:T(1024)S(1)} all-reduce(f32[2048]{0:T(1024)S(1)} %multiply_reduce_fusion.3), channel_id=1, replica_groups=mesh['rows'=16,'protos'=32] {'rows'}, use_global_device_ids=true, to_apply=%region_17.0 | all-reduce | flops 2048 | bytes 16384 | tf_op jit(solution)/shard_map/psum | solution.py:110
  581.4 1.7 subtract_divide_fusion
  (50 shorter events, 10.6 us)
Async XLA Ops:
  8.0 1.6 copy-start
  8.0 21.9 %copy-start.4 = (bf16[256,2048]{1,0:T(8,128)(2,1)S(1)}, bf16[256,2048]{1,0:T(8,128)(2,1)}, u32[]{:S(2)}) copy-start(bf16[256,2048]{1,0:T(8,128)(2,1)} %param.11) | copy-start | bytes 3145732
  8.0 532.6 %all-reduce.3.cloned.1.call-start = ((), (), s32[]{:S(2)}) async-start(), calls=%async_computation.1 | async-start | bytes 2097152 | tf_op jit(solution)/shard_map/psum | solution.py:92
  31.8 3.2 copy-start.1
  252.9 54.1 %copy-start.3 = (bf16[256,2048]{1,0:T(8,128)(2,1)S(1)}, bf16[256,2048]{1,0:T(8,128)(2,1)}, u32[]{:S(2)}) copy-start(bf16[256,2048]{1,0:T(8,128)(2,1)} %param.10) | copy-start | bytes 3145732
  377.5 1.9 copy-start.2
  381.8 4.9 copy-start.5
  381.8 4.9 copy-start.7
  381.8 5.0 copy-start.6
  381.8 169.0 %reduce-scatter.2.cloned.1.call-start = ((), (), s32[]{:S(2)}) async-start(), calls=%async_computation.2 | async-start | bytes 2228224 | tf_op jit(solution)/shard_map/reduce_scatter | solution.py:101
Sparse Core Ops, SparseCore 0:
  381.9 158.6 all-reduce.2
Sparse Core Ops, SparseCore 1:
  386.7 63.0 reduce-scatter.1
where the time goes:
time: 591 us
  blocking collectives  315 us (53%)
  waiting for transfers between devices  152 us (26%)
  matrix products  58.1 us (10%)
  local copies, waits for them, and re-layouts  25.9 us (4%)
  other arithmetic  23.6 us (4%)
  between operations  15.8 us (3%)
    psum x3, blocking collectives, teacher_rows(): return lax.psum(row_part, 'protos')  175 us
    psum x1, waiting for transfers between devices, local(): feature_sum = lax.psum(feature_part, 'protos')  152 us
    psum x3, blocking collectives, column_update(): column_sums = lax.psum(column_part, 'rows')  110 us
    psum x1, blocking collectives, local(): column_dots = lax.psum(jnp.sum(unit_share * weight_share, axis=0), 'rows')  29.7 us
    dot_general x3, matrix products, column_update(): jnp.dot(teacher_exp, updated, precision=lax.Precision.HIGHEST)  28.2 us
    dot_general x3, matrix products, column_update(): jnp.dot(row_scale, teacher_exp, precision=lax.Precision.HIGHEST)  16.8 us
    gather x1, local copies, waits for them, and re-layouts, local(): jnp.take_along_axis(student_patches, selector, axis=1)  13.5 us
  transfers between devices with their start and end apart: 2, of which 1 were waited for; matrix products, arithmetic and copies ran while one was open for 3% of the time, Pallas kernels for 0%

commit v1 on v0

v1 whole, which is shorter than its diff:
```python
import functools
import math

import jax
import jax.numpy as jnp
from jax import lax
from jax.experimental import pallas as pl
from jax.experimental.pallas import tpu as pltpu
from jax.sharding import PartitionSpec as P

PROTOS = 65536
SK_ITERS = 3
LANES = 128

epsilon = 1e-06
temp_student = 0.1
temp_teacher = 0.07

f32 = jnp.float32
bf16 = jnp.bfloat16


def call(body, outs, ins, scratch=(), limit=8, flops=0, moved=0):
    return pl.pallas_call(
        body,
        out_shape=[pltpu.VMEM(s, d) for s, d in outs],
        in_specs=[pl.BlockSpec(memory_space=pltpu.VMEM)] * len(ins),
        out_specs=[pl.BlockSpec(memory_space=pltpu.VMEM)] * len(outs),
        scratch_shapes=list(scratch),
        compiler_params=pltpu.CompilerParams(vmem_limit_bytes=limit * 2**20),
        cost_estimate=pl.CostEstimate(flops=flops, bytes_accessed=moved, transcendentals=0),
    )(*ins)


def selector(mask_ref, image, patches):
    wanted = mask_ref[pl.ds(image, 1), :]
    masked = wanted.shape[1]
    return lax.broadcasted_iota(jnp.int32, (patches, masked), 0) == wanted


def pick(patches_ref, mask_ref, image):
    patches = patches_ref.shape[1]
    chosen = selector(mask_ref, image, patches).astype(bf16)
    return lax.dot_general(
        chosen, patches_ref[image], (((0,), (0,)), ((), ())), preferred_element_type=f32
    )


def lanes_of_rows(parts):
    return jnp.sum(parts.T, axis=0, keepdims=True)


def fold_lanes(values):
    total = values[:, :LANES]
    for start in range(LANES, values.shape[1], LANES):
        total = total + values[:, start : start + LANES]
    return total


def rows_on_sublanes(line):
    pieces = [
        jnp.broadcast_to(line[:, s : s + LANES], (LANES, LANES)).T
        for s in range(0, line.shape[1], LANES)
    ]
    return jnp.concatenate(pieces, axis=0)


def spread(column, width):
    return jnp.concatenate([column] * (width // LANES), axis=1)


def unit_columns(weight_ref, cols):
    weight = weight_ref[:, cols].astype(f32)
    length = jnp.sqrt(jnp.sum(weight * weight, axis=0, keepdims=True) + epsilon)
    return weight / length, length


TILE = 256


def teacher_body(patches_ref, mask_ref, weight_ref, exp_ref, cols_ref, unit_ref):
    images, masked = mask_ref.shape

    def one_image(image, _):
        picked = pick(patches_ref, mask_ref, image)
        length = jnp.sqrt(jnp.sum(picked * picked, axis=1, keepdims=True) + epsilon)
        unit_ref[pl.ds(image * masked, masked), :] = (picked / length).astype(bf16)
        return 0

    lax.fori_loop(0, images, one_image, 0)

    def one_tile(tile, _):
        cols = pl.ds(pl.multiple_of(tile * TILE, TILE), TILE)
        unit = unit_columns(weight_ref, cols)[0].astype(bf16)
        products = jnp.dot(unit_ref[...], unit, preferred_element_type=f32)
        exps = jnp.exp(products * (1.0 / temp_teacher))
        exp_ref[:, cols] = exps
        line = jnp.sum(exps, axis=0, keepdims=True)
        cols_ref[:, :, cols] = jnp.broadcast_to(line[None], (cols_ref.shape[0], 1, TILE))
        return 0

    lax.fori_loop(0, weight_ref.shape[1] // TILE, one_tile, 0)


def student_body(
    patches_ref, mask_ref, weight_ref,
    exp_ref, rows_ref, unit_ref, inverse_ref, turned_ref, back_ref, length_ref, unit_bf_ref, parts_ref,
):
    images, masked = mask_ref.shape

    def one_image(image, _):
        picked = pick(patches_ref, mask_ref, image)
        length = jnp.sqrt(jnp.sum(picked * picked, axis=1, keepdims=True) + epsilon)
        unit = picked / length
        rows = pl.ds(pl.multiple_of(image * masked, masked), masked)
        unit_ref[rows, :] = unit
        unit_bf_ref[rows, :] = unit.astype(bf16)
        turned_ref[:, rows] = unit.T.astype(bf16)
        inverse_ref[rows, :] = jnp.broadcast_to(1.0 / length, (masked, LANES))
        return 0

    lax.fori_loop(0, images, one_image, 0)
    parts_ref[...] = jnp.zeros_like(parts_ref)

    def one_tile(tile, _):
        cols = pl.ds(pl.multiple_of(tile * TILE, TILE), TILE)
        unit, length = unit_columns(weight_ref, cols)
        length_ref[:, cols] = length
        back_ref[cols, :] = unit.T.astype(bf16)
        products = jnp.dot(unit_bf_ref[...], unit.astype(bf16), preferred_element_type=f32)
        exps = jnp.exp(products * (1.0 / temp_student))
        exp_ref[:, cols] = exps
        parts_ref[...] += fold_lanes(exps)
        return 0

    lax.fori_loop(0, weight_ref.shape[1] // TILE, one_tile, 0)
    store_copies(rows_ref, lanes_of_rows(parts_ref[...]))


def store_copies(out_ref, line):
    out_ref[...] = jnp.broadcast_to(line[None], out_ref.shape)


def sum_parts(refs):
    total = None
    for ref in refs:
        line = jnp.sum(ref[...], axis=0)
        total = line if total is None else total + line
    return total


def columns_body(*refs):
    *sums, exp_ref, scale_ref, rows_ref, parts_ref = refs
    scale = 1.0 / (sum_parts(sums) * PROTOS)
    scale_ref[...] = scale
    step = 64

    def block(index, _):
        rows = pl.ds(pl.multiple_of(index * step, step), step)
        total = exp_ref[rows, :LANES] * scale[:, :LANES]
        for start in range(LANES, exp_ref.shape[1], LANES):
            total = total + exp_ref[rows, start : start + LANES] * scale[:, start : start + LANES]
        parts_ref[rows, :] = total
        return 0

    lax.fori_loop(0, exp_ref.shape[0] // step, block, 0)
    store_copies(rows_ref, lanes_of_rows(parts_ref[...]))


def rows_body(total_rows, *refs):
    *sums, exp_ref, cols_ref, scale_ref, parts_ref = refs
    line = 1.0 / (sum_parts(sums)[:, : exp_ref.shape[0]] * total_rows)
    scale_ref[...] = rows_on_sublanes(line)
    width = exp_ref.shape[1]
    parts_ref[...] = jnp.zeros_like(parts_ref)
    step = 64

    def block(index, _):
        rows = pl.ds(pl.multiple_of(index * step, step), step)
        scale = scale_ref[rows, :]
        for start in range(0, width, LANES):
            product = exp_ref[rows, start : start + LANES] * scale
            total = product[0:8]
            for r in range(8, step, 8):
                total = total + product[r : r + 8]
            parts_ref[:, start : start + LANES] += total
        return 0

    lax.fori_loop(0, exp_ref.shape[0] // step, block, 0)
    store_copies(cols_ref, jnp.sum(parts_ref[...], axis=0, keepdims=True))


def placing(mask_ref, image, order, share, patches):
    place = lax.broadcasted_iota(jnp.int32, (patches, mask_ref.shape[1]), 0)
    patch = order(place // share) * share + place % share
    return (patch == mask_ref[pl.ds(image, 1), :]).astype(bf16)


def three_pieces(values):
    high = values.astype(bf16)
    rest = values - high.astype(f32)
    middle = rest.astype(bf16)
    return high, middle, (rest - middle.astype(f32)).astype(bf16)


def feature_body(total_rows, grid, *refs):
    (
        *sums, student_ref, cols_ref, teacher_exp_ref, student_exp_ref, back_ref, unit_ref, inverse_ref, mask_ref,
        first_ref, second_ref, score_ref, row_ref, total_ref, sum_ref,
    ) = refs
    row_ref[...] = rows_on_sublanes(1.0 / (sum_parts(sums) * total_rows))
    total_ref[...] = rows_on_sublanes(1.0 / jnp.sum(student_ref[...], axis=0)[:, teacher_exp_ref.shape[0] :])
    sum_ref[...] = jnp.zeros_like(sum_ref)

    def one_tile(tile, _):
        cols = pl.ds(pl.multiple_of(tile * TILE, TILE), TILE)
        target = teacher_exp_ref[:, cols] * spread(row_ref[...], TILE) * (cols_ref[:, cols] * total_rows)
        probabilities = student_exp_ref[:, cols] * spread(total_ref[...], TILE)
        score = ((probabilities - target) * (1.0 / temp_student)).astype(bf16)
        score_ref[:, cols] = score
        sum_ref[...] += jnp.dot(score, back_ref[cols, :], preferred_element_type=f32)
        return 0

    lax.fori_loop(0, teacher_exp_ref.shape[1] // TILE, one_tile, 0)
    images, masked = mask_ref.shape
    width = unit_ref.shape[1]
    half = width // 2
    size_x, size_y = grid
    shares = size_x * size_y
    patches = first_ref.shape[0] * first_ref.shape[1] // images
    share = patches // shares
    me = lax.axis_index("protos")
    my_x, my_y = me // size_y, me % size_y

    def x_first(place):
        return (place // size_y + my_x) % size_x * size_y + (place % size_y + my_y) % size_y

    def y_first(place):
        return (place % size_x + my_x) % size_x * size_y + (place // size_x + my_y) % size_y

    def one_image(image, _):
        rows = pl.ds(pl.multiple_of(image * masked, masked), masked)
        unit = unit_ref[rows, :]
        total = sum_ref[rows, :]
        projection = jnp.sum(unit * total, axis=1, keepdims=True)
        pieces = three_pieces((total - unit * projection) * spread(inverse_ref[rows, :], width))
        for out_ref, order, lanes in (
            (first_ref, x_first, slice(0, half)),
            (second_ref, y_first, slice(half, width)),
        ):
            chosen = placing(mask_ref, image, order, share, patches)
            placed = sum(jnp.dot(chosen, piece[:, lanes], preferred_element_type=f32) for piece in pieces)
            out_ref[:, pl.ds(pl.multiple_of(image * share, share), share), :] = placed.reshape(
                shares, share, half
            )
        return 0

    lax.fori_loop(0, images, one_image, 0)


def weight_body(shares, score_ref, turned_ref, weight_ref, length_ref, mine_ref, other_ref):
    depth = weight_ref.shape[0]
    share = depth // shares
    levels = shares // 2
    me = lax.axis_index("rows")
    core, level = me % 2, me // 2

    def one_tile(tile, _):
        cols = pl.ds(pl.multiple_of(tile * TILE, TILE), TILE)
        total = jnp.dot(turned_ref[...], score_ref[:, cols], preferred_element_type=f32)
        inverse = 1.0 / length_ref[:, cols]
        unit = weight_ref[:, cols].astype(f32) * inverse
        dots = jnp.sum(unit * total, axis=0, keepdims=True)
        gradient = (total - unit * dots) * inverse
        for z in range(levels):
            even = gradient[2 * z * share : (2 * z + 1) * share]
            odd = gradient[(2 * z + 1) * share : (2 * z + 2) * share]
            place = (z + levels - level) % levels
            mine_ref[pl.ds(place, 1), :, cols] = jnp.where(core == 0, even, odd)[None]
            other_ref[pl.ds(place, 1), :, cols] = jnp.where(core == 0, odd, even)[None]
        return 0

    lax.fori_loop(0, weight_ref.shape[1] // TILE, one_tile, 0)


def add_body(*refs):
    *parts, out_ref = refs
    total = parts[0][...]
    for part in parts[1:]:
        total = total + part[...]
    out_ref[...] = total


def add(*parts):
    (total,) = call(add_body, [(parts[0].shape, f32)], parts, limit=4)
    return total


def moves(axis, size, to):
    return axis, [(i, to(i)) for i in range(size)]


def shift_z(by):
    size = lax.axis_size("rows")
    return moves("rows", size, lambda i: (i + 2 * by) % size)


def swap_rows(bit):
    return moves("rows", lax.axis_size("rows"), lambda i: i ^ bit)


def shift_x(by):
    size = lax.axis_size("protos")
    length = grid_of(size)[1]
    return moves("protos", size, lambda i: (i + length * by) % size)


def shift_y(by):
    size = lax.axis_size("protos")
    length = grid_of(size)[1]
    return moves("protos", size, lambda i: i // length * length + (i + by) % length)


def swap_protos(bit):
    return moves("protos", lax.axis_size("protos"), lambda i: i ^ bit)


def send(values, move):
    axis, pairs = move
    return lax.ppermute(values, axis, pairs)


def grid_of(size):
    return (4, 8) if size == 32 else (2, size // 2)


def by_doubling(line, swaps):
    for move in swaps[:-1]:
        line = add(line, send(line, move))
    return [line, send(line, swaps[-1])]


def all_along(line, shift, size):
    return [line] + [send(line, shift(by)) for by in range(1, size)]


def ring_share(parts, shift, size):
    last = size // 2
    up = parts[last]
    for k in range(last - 1, 0, -1):
        up = send(up, shift(1)) + parts[k]
    up = send(up, shift(1))
    total = parts[0] + up
    if size > 2:
        down = parts[last + 1]
        for k in range(last + 2, size):
            down = send(down, shift(-1)) + parts[k]
        total = total + send(down, shift(-1))
    return total


def everyones(copies, axis):
    return lax.all_to_all(copies, axis, 0, 0, tiled=True)


def local(student_patches, teacher_patches, mask_index, student_weight, teacher_weight):
    images, patches, depth = student_patches.shape
    masked = mask_index.shape[1]
    rows = images * masked
    row_devices = lax.axis_size("rows")
    proto_devices = lax.axis_size("protos")
    total_rows = float(rows * row_devices)
    protos = student_weight.shape[1]
    work = 2 * rows * protos * depth

    teacher_exp, column_part = call(
        teacher_body,
        [((rows, protos), f32), ((row_devices, 1, protos), f32)],
        (teacher_patches, mask_index, teacher_weight),
        [pltpu.VMEM((rows, depth), bf16)],
        flops=work, moved=2**23,
    )
    column_sums = [everyones(column_part, "rows")]
    student_exp, student_part, unit, inverse, turned, back, length = call(
        student_body,
        [
            ((rows, protos), f32),
            ((proto_devices, 1, rows), f32),
            ((rows, depth), f32),
            ((rows, LANES), f32),
            ((depth, rows), bf16),
            ((protos, depth), bf16),
            ((1, protos), f32),
        ],
        (student_patches, mask_index, student_weight),
        [pltpu.VMEM((rows, depth), bf16), pltpu.VMEM((rows, LANES), f32)],
        flops=work, moved=2**23,
    )
    levels = row_devices // 2
    grid = grid_of(proto_devices)
    student_sums = None
    for sweep in range(SK_ITERS):
        col_scale, row_part = call(
            columns_body,
            [((1, protos), f32), ((proto_devices if sweep == 0 else 1, 1, rows), f32)],
            (*column_sums, teacher_exp),
            [pltpu.VMEM((rows, LANES), f32)],
            flops=2 * rows * protos, moved=2**23,
        )
        if sweep == 0:
            student_sums = everyones(jnp.concatenate([row_part, student_part], axis=2), "protos")
            row_sums = [student_sums]
        elif sweep == 1:
            row_sums = all_along(add(*all_along(row_part, shift_x, grid[0])), shift_y, grid[1])
        else:
            row_sums = by_doubling(
                row_part, [swap_protos(1 << bit) for bit in range((proto_devices - 1).bit_length())]
            )
        if sweep < SK_ITERS - 1:
            (column_part,) = call(
                functools.partial(rows_body, total_rows),
                [((1, 1, protos), f32)],
                (*row_sums, teacher_exp),
                [pltpu.VMEM((rows, LANES), f32), pltpu.VMEM((8, protos), f32)],
                flops=2 * rows * protos, moved=2**23,
            )
            if sweep == 0:
                column_sums = all_along(add(column_part, send(column_part, swap_rows(1))), shift_z, levels)
            else:
                column_sums = by_doubling(
                    column_part, [swap_rows(1 << bit) for bit in range((row_devices - 1).bit_length())]
                )
    share = patches // proto_devices
    half = depth // 2
    first, second, score = call(
        functools.partial(feature_body, total_rows, grid),
        [((proto_devices, images * share, half), f32)] * 2 + [((rows, protos), bf16)],
        (*row_sums, student_sums, col_scale, teacher_exp, student_exp, back, unit, inverse, mask_index),
        [
            pltpu.VMEM((rows, LANES), f32),
            pltpu.VMEM((rows, LANES), f32),
            pltpu.VMEM((rows, depth), f32),
        ],
        flops=work, moved=2**24,
    )
    first = first.reshape(grid[0], grid[1], images * share, half)
    second = second.reshape(grid[1], grid[0], images * share, half)
    first = ring_share(ring_share(first, shift_x, grid[0]), shift_y, grid[1])
    second = ring_share(ring_share(second, shift_y, grid[1]), shift_x, grid[0])
    mine, other = call(
        functools.partial(weight_body, row_devices),
        [((levels, depth // row_devices, protos), f32)] * 2,
        (score, turned, student_weight, length),
        flops=work, moved=2**23,
    )
    grad_weight = ring_share(mine + send(other, swap_rows(1)), shift_z, levels)
    grad_patches = jnp.concatenate([first, second], axis=1).reshape(images, share, depth)
    return (grad_patches, grad_weight)


def solution(mesh):
    placed = (
        P("rows", None, None),
        P("rows", None, None),
        P("rows", None),
        P(None, "protos"),
        P(None, "protos"),
    )
    return jax.shard_map(
        local,
        mesh=mesh,
        in_specs=placed,
        out_specs=(P("rows", "protos", None), P("rows", "protos")),
        check_vma=False,
    )
```

time: 591 us -> 325 us (0.55)
  the two profiles are of different devices: /device:TPU:1 before, /device:TPU:2 now
where the time goes in v1:
time: 325 us; the launch traced here: 323 us
  starting transfers between devices  195 us (60%)
  waiting for transfers between devices  55.9 us (17%)
  Pallas kernels  29.6 us (9%)
  blocking collectives  21.9 us (7%)
  local copies, waits for them, and re-layouts  16.4 us (5%)
    ppermute x55, starting transfers between devices, send(): return lax.ppermute(values, axis, pairs)  185 us
    ppermute x55, waiting for transfers between devices, send(): return lax.ppermute(values, axis, pairs)  55.9 us
    pallas_call x18, Pallas kernels, call(): pl.pallas_call(body, out_shape=[pltpu.VMEM(s, d) for s, d in outs], in_sp...  29.6 us
    all_to_all x1, blocking collectives, everyones(): return lax.all_to_all(copies, axis, 0, 0, tiled=True)  21.9 us
    unnamed x28, local copies, waits for them, and re-layouts  16.4 us
    all_to_all x1, starting transfers between devices, everyones(): return lax.all_to_all(copies, axis, 0, 0, tiled=True)  10.4 us
  transfers between devices with their start and end apart: 56, of which 22 were waited for; matrix products, arithmetic and copies ran while one was open for 0% of the time, Pallas kernels for 3%

profile of v1, /device:TPU:2, one launch (start us, length us, event | category | flops | bytes accessed | tf_op | source)
XLA Modules:
  0.0 322.6 jit_solution(3609664639236536959)
XLA Ops:
  3.8 6.5 %shard_map.68 = (f32[1024,2048]{1,0:T(8,128)S(1)}, f32[16,1,2048]{2,1,0:T(1,128)}) custom-call(bf16[8,256,256]{2,1,0:T(8,128)(2,1)S(1)} %copy-done.9, s32[8,128]{1,0:T(8,128)S(1)} %copy-done.6, bf16[256,2048]{1,0:T(8,128)(2,1)S(1)} %copy-done.10), custom_call_target="tpu_custom_call" | custom-call | flops 1073741824 | bytes 8388608 | tf_op jit(solution)/shard_map/pallas_call | solution.py:24
  13.6 10.4 %all-to-all-start = ((f32[16,1,2048]{2,1,0:T(1,128)}), f32[16,1,2048]{2,1,0:T(1,128)S(1)}, u32[]{:S(2)}, u32[]{:S(2)}) async-start(f32[16,1,2048]{2,1,0:T(1,128)} %get-tuple-element.20), calls=%async_computation | async-start | bytes 262144 | tf_op jit(solution)/shard_map/all_to_all | solution.py:363
  27.2 6.3 %shard_map.70 = (f32[1024,2048]{1,0:T(8,128)S(1)}, f32[32,1,1024]{2,1,0:T(1,128)S(1)}, f32[1024,256]{1,0:T(8,128)S(1)}, f32[1024,128]{1,0:T(8,128)S(1)}, bf16[25...) custom-call(bf16[8,256,256]{2,1,0:T(8,128)(2,1)S(1)} %copy-done.11, ...), custom_call_target="tpu_custom_call" | custom-call | flops 1073741824 | bytes 8388608 | tf_op jit(solution)/shard_map/pallas_call | solution.py:24
  41.9 21.9 %all_to_all.10.refs_0_.refs_2_ = f32[32,1,2048]{2,1,0:T(1,128)S(1)} all-to-all(f32[32,1,2048]{2,1,0:T(1,128)S(1)} %pad_maximum_fusion), channel_id=1, replica_groups=mesh['rows'=16,'protos'=32] {'protos'}, dimensions={0} | all-to-all | bytes 524288 | tf_op jit(solution)/shard_map/all_to_all | solution.py:363
  67.8 4.9 %collective-permute-start.7 = (f32[1,1,2048]{2,1,0:T(1,128)S(1)}, f32[1,1,2048]{2,1,0:T(1,128)S(1)}, u32[]{:S(2)}, u32[]{:S(2)}) collective-permute-start(f32[1,1,2048]{2,1,0:T(1,128)S(1)} %shard_map.72.refs_0_), channel_id=1, source_target_pairs={{0,448},{32,480},{64,0},{96,32},{128,64},{160,96},{192,128},{224,1... | collective-permute-start | bytes 24584 | tf_op jit(solution)/shard_map/ppermute | solution.py:330
  80.4 5.5 %collective-permute-start.4 = (f32[1,1,2048]{2,1,0:T(1,128)S(1)}, f32[1,1,2048]{2,1,0:T(1,128)S(1)}, u32[]{:S(2)}, u32[]{:S(2)}) collective-permute-start(f32[1,1,2048]{2,1,0:T(1,128)S(1)} %shard_map.72.refs_0_), channel_id=1, source_target_pairs={{0,256},{32,288},{64,320},{96,352},{128,384},{160,416},{192,448},{... | collective-permute-start | bytes 24584 | tf_op jit(solution)/shard_map/ppermute | solution.py:330
  88.1 5.5 %collective-permute-start.2 = (f32[1,1,2048]{2,1,0:T(1,128)S(1)}, f32[1,1,2048]{2,1,0:T(1,128)S(1)}, u32[]{:S(2)}, u32[]{:S(2)}) collective-permute-start(f32[1,1,2048]{2,1,0:T(1,128)S(1)} %shard_map.72.refs_0_), channel_id=1, source_target_pairs={{0,128},{32,160},{64,192},{96,224},{128,256},{160,288},{192,320},{... | collective-permute-start | bytes 24584 | tf_op jit(solution)/shard_map/ppermute | solution.py:330
  119.1 6.1 %collective-permute-start.15 = (f32[1,1,1024]{2,1,0:T(1,128)S(1)}, f32[1,1,1024]{2,1,0:T(1,128)S(1)}, u32[]{:S(2)}, u32[]{:S(2)}) collective-permute-start(f32[1,1,1024]{2,1,0:T(1,128)S(1)} %shard_map.74.refs_0_), channel_id=1, source_target_pairs={{0,5},{1,6},{2,7},{3,0},{4,1},{5,2},{6,3},{7,4},{8,13},{9,14},{10,... | collective-permute-start | bytes 12296 | tf_op jit(solution)/shard_map/ppermute | solution.py:330
  160.4 4.6 %collective-permute-start.21 = (f32[1,1,2048]{2,1,0:T(1,128)S(1)}, f32[1,1,2048]{2,1,0:T(1,128)S(1)}, u32[]{:S(2)}, u32[]{:S(2)}) collective-permute-start(f32[1,1,2048]{2,1,0:T(1,128)S(1)} %shard_map.78.refs_0_), channel_id=1, source_target_pairs={{0,256},{32,288},{64,320},{96,352},{128,384},{160,416},{192,448},{... | collective-permute-start | bytes 24584 | tf_op jit(solution)/shard_map/ppermute | solution.py:330
  165.0 4.9 %collective-permute-done.21.refs_1_ = f32[1,1,2048]{2,1,0:T(1,128)S(1)} collective-permute-done((f32[1,1,2048]{2,1,0:T(1,128)S(1)}, f32[1,1,2048]{2,1,0:T(1,128)S(1)}, u32[]{:S(2)}, u32[]{:S(2)}) %collective-permute-start.21) | collective-permute-done | bytes 8224 | tf_op jit(solution)/shard_map/ppermute | solution.py:330
  182.7 4.5 %collective-permute-start.24 = (f32[1,1,1024]{2,1,0:T(1,128)S(1)}, f32[1,1,1024]{2,1,0:T(1,128)S(1)}, u32[]{:S(2)}, u32[]{:S(2)}) collective-permute-start(f32[1,1,1024]{2,1,0:T(1,128)S(1)} %shard_map.81.refs_0_), channel_id=1, source_target_pairs={{0,4},{1,5},{2,6},{3,7},{4,0},{5,1},{6,2},{7,3},{8,12},{9,13},{10,... | collective-permute-start | bytes 12296 | tf_op jit(solution)/shard_map/ppermute | solution.py:330
  187.2 4.9 %collective-permute-done.24.refs_1_ = f32[1,1,1024]{2,1,0:T(1,128)S(1)} collective-permute-done((f32[1,1,1024]{2,1,0:T(1,128)S(1)}, f32[1,1,1024]{2,1,0:T(1,128)S(1)}, u32[]{:S(2)}, u32[]{:S(2)}) %collective-permute-start.24) | collective-permute-done | bytes 4128 | tf_op jit(solution)/shard_map/ppermute | solution.py:330
  192.1 5.1 %collective-permute-start.25 = (f32[1,1,1024]{2,1,0:T(1,128)S(1)}, f32[1,1,1024]{2,1,0:T(1,128)S(1)}, u32[]{:S(2)}, u32[]{:S(2)}) collective-permute-start(f32[1,1,1024]{2,1,0:T(1,128)S(1)} %shard_map.82.refs_0_), channel_id=1, source_target_pairs={{0,8},{1,9},{2,10},{3,11},{4,12},{5,13},{6,14},{7,15},{8,0},{9,1},... | collective-permute-start | bytes 12296 | tf_op jit(solution)/shard_map/ppermute | solution.py:330
  205.8 8.1 %shard_map.84 = (f32[32,64,128]{2,1,0:T(8,128)S(1)}, f32[32,64,128]{2,1,0:T(8,128)S(1)}, bf16[1024,2048]{1,0:T(8,128)(2,1)S(1)}) custom-call(f32[1,1,1024]{2,1,0:T(1,128)S(1)} %shard_map.83.refs_0_, f32[1,1,1024]{2,1,0:T(1,128)S(1)} %collective-permute-done.26.refs_1_, f32[32,1,2048]{2,1,0:T(1,128)S(1)} %all_to_all.10.refs_0_.refs_2_, ...), custom_call_target="tpu_custom_call" | custom-call | flops 1073741824 | bytes 16777216 | tf_op jit(solution)/shard_map/pallas_call | solution.py:24
  215.9 6.1 %collective-permute-done.37 = f32[4,64,128]{2,1,0:T(8,128)S(1)} collective-permute-done((f32[4,64,128]{2,1,0:T(8,128)S(1)}, f32[4,64,128]{2,1,0:T(8,128)S(1)}, u32[]{:S(2)}, u32[]{:S(2)}) %collective-permute-start.37) | collective-permute-done | bytes 131104 | tf_op jit(solution)/shard_map/ppermute | solution.py:330
  224.0 5.1 %collective-permute-start.41 = (f32[4,64,128]{2,1,0:T(8,128)S(1)}, f32[4,64,128]{2,1,0:T(8,128)S(1)}, u32[]{:S(2)}, u32[]{:S(2)}) collective-permute-start(f32[4,64,128]{2,1,0:T(8,128)S(1)} %get-tuple-element.51), channel_id=1, source_target_pairs={{0,7},{1,0},{2,1},{3,2},{4,3},{5,4},{6,5},{7,6},{8,15},{9,8},{10,9... | collective-permute-start | bytes 393224 | tf_op jit(solution)/shard_map/ppermute | solution.py:330
  233.6 5.6 %collective-permute-start.42 = (f32[4,64,128]{2,1,0:T(8,128)S(1)}, f32[4,64,128]{2,1,0:T(8,128)S(1)}, u32[]{:S(2)}, u32[]{:S(2)}) collective-permute-start(f32[4,64,128]{2,1,0:T(8,128)S(1)} %get-tuple-element.49), channel_id=1, source_target_pairs={{0,7},{1,0},{2,1},{3,2},{4,3},{5,4},{6,5},{7,6},{8,15},{9,8},{10,9... | collective-permute-start | bytes 393224 | tf_op jit(solution)/shard_map/ppermute | solution.py:330
  248.8 5.1 %collective-permute-start.43 = (f32[4,64,128]{2,1,0:T(8,128)S(1)}, f32[4,64,128]{2,1,0:T(8,128)S(1)}, u32[]{:S(2)}, u32[]{:S(2)}) collective-permute-start(f32[4,64,128]{2,1,0:T(8,128)S(1)} %get-tuple-element.47), channel_id=1, source_target_pairs={{0,7},{1,0},{2,1},{3,2},{4,3},{5,4},{6,5},{7,6},{8,15},{9,8},{10,9... | collective-permute-start | bytes 393224 | tf_op jit(solution)/shard_map/ppermute | solution.py:330
  270.0 5.1 %collective-permute-start.34 = (f32[64,128]{1,0:T(8,128)S(1)}, f32[64,128]{1,0:T(8,128)S(1)}, u32[]{:S(2)}, u32[]{:S(2)}) collective-permute-start(f32[64,128]{1,0:T(8,128)S(1)} %get-tuple-element.57), channel_id=1, source_target_pairs={{0,7},{1,0},{2,1},{3,2},{4,3},{5,4},{6,5},{7,6},{8,15},{9,8},{10,9... | collective-permute-start | bytes 98312 | tf_op jit(solution)/shard_map/ppermute | solution.py:330
  283.2 4.9 %collective-permute-start.52 = (f32[16,2048]{1,0:T(8,128)S(1)}, f32[16,2048]{1,0:T(8,128)S(1)}, u32[]{:S(2)}, u32[]{:S(2)}) collective-permute-start(f32[16,2048]{1,0:T(8,128)S(1)} %get-tuple-element.43), channel_id=1, source_target_pairs={{0,448},{32,480},{64,0},{96,32},{128,64},{160,96},{192,128},{224,1... | collective-permute-start | bytes 393224 | tf_op jit(solution)/shard_map/ppermute | solution.py:330
  293.0 5.1 %collective-permute-start.35 = (f32[64,128]{1,0:T(8,128)S(1)}, f32[64,128]{1,0:T(8,128)S(1)}, u32[]{:S(2)}, u32[]{:S(2)}) collective-permute-start(f32[64,128]{1,0:T(8,128)S(1)} %get-tuple-element.55), channel_id=1, source_target_pairs={{0,7},{1,0},{2,1},{3,2},{4,3},{5,4},{6,5},{7,6},{8,15},{9,8},{10,9... | collective-permute-start | bytes 98312 | tf_op jit(solution)/shard_map/ppermute | solution.py:330
  300.1 5.1 %collective-permute-start.53 = (f32[16,2048]{1,0:T(8,128)S(1)}, f32[16,2048]{1,0:T(8,128)S(1)}, u32[]{:S(2)}, u32[]{:S(2)}) collective-permute-start(f32[16,2048]{1,0:T(8,128)S(1)} %get-tuple-element.41), channel_id=1, source_target_pairs={{0,448},{32,480},{64,0},{96,32},{128,64},{160,96},{192,128},{224,1... | collective-permute-start | bytes 393224 | tf_op jit(solution)/shard_map/ppermute | solution.py:330
  307.2 5.1 %collective-permute-start.36 = (f32[64,128]{1,0:T(8,128)S(1)}, f32[64,128]{1,0:T(8,128)S(1)}, u32[]{:S(2)}, u32[]{:S(2)}) collective-permute-start(f32[64,128]{1,0:T(8,128)S(1)} %get-tuple-element.53), channel_id=1, source_target_pairs={{0,7},{1,0},{2,1},{3,2},{4,3},{5,4},{6,5},{7,6},{8,15},{9,8},{10,9... | collective-permute-start | bytes 98312 | tf_op jit(solution)/shard_map/ppermute | solution.py:330
  314.3 5.1 %collective-permute-start.54 = (f32[16,2048]{1,0:T(8,128)S(1)}, f32[16,2048]{1,0:T(8,128)S(1)}, u32[]{:S(2)}, u32[]{:S(2)}) collective-permute-start(f32[16,2048]{1,0:T(8,128)S(1)} %get-tuple-element.39), channel_id=1, source_target_pairs={{0,448},{32,480},{64,0},{96,32},{128,64},{160,96},{192,128},{224,1... | collective-permute-start | bytes 393224 | tf_op jit(solution)/shard_map/ppermute | solution.py:330
  (160 shorter events, 169.5 us)
Async XLA Ops:
  13.6 23.2 %all-to-all-start = ((f32[16,1,2048]{2,1,0:T(1,128)}), f32[16,1,2048]{2,1,0:T(1,128)S(1)}, u32[]{:S(2)}, u32[]{:S(2)}) async-start(f32[16,1,2048]{2,1,0:T(1,128)} %get-tuple-element.20), calls=%async_computation | async-start | bytes 262144 | tf_op jit(solution)/shard_map/all_to_all | solution.py:363
  67.8 20.2 %collective-permute-start.7 = (f32[1,1,2048]{2,1,0:T(1,128)S(1)}, f32[1,1,2048]{2,1,0:T(1,128)S(1)}, u32[]{:S(2)}, u32[]{:S(2)}) collective-permute-start(f32[1,1,2048]{2,1,0:T(1,128)S(1)} %shard_map.72.refs_0_), channel_id=1, source_target_pairs={{0,448},{32,480},{64,0},{96,32},{128,64},{160,96},{192,128},{224,1... | collective-permute-start | bytes 24584 | tf_op jit(solution)/shard_map/ppermute | solution.py:330
  72.7 20.8 %collective-permute-start.6 = (f32[1,1,2048]{2,1,0:T(1,128)S(1)}, f32[1,1,2048]{2,1,0:T(1,128)S(1)}, u32[]{:S(2)}, u32[]{:S(2)}) collective-permute-start(f32[1,1,2048]{2,1,0:T(1,128)S(1)} %shard_map.72.refs_0_), channel_id=1, source_target_pairs={{0,384},{32,416},{64,448},{96,480},{128,0},{160,32},{192,64},{224,... | collective-permute-start | bytes 24584 | tf_op jit(solution)/shard_map/ppermute | solution.py:330
  77.0 19.9 %collective-permute-start.5 = (f32[1,1,2048]{2,1,0:T(1,128)S(1)}, f32[1,1,2048]{2,1,0:T(1,128)S(1)}, u32[]{:S(2)}, u32[]{:S(2)}) collective-permute-start(f32[1,1,2048]{2,1,0:T(1,128)S(1)} %shard_map.72.refs_0_), channel_id=1, source_target_pairs={{0,320},{32,352},{64,384},{96,416},{128,448},{160,480},{192,0},{22... | collective-permute-start | bytes 24584 | tf_op jit(solution)/shard_map/ppermute | solution.py:330
  80.4 16.6 %collective-permute-start.4 = (f32[1,1,2048]{2,1,0:T(1,128)S(1)}, f32[1,1,2048]{2,1,0:T(1,128)S(1)}, u32[]{:S(2)}, u32[]{:S(2)}) collective-permute-start(f32[1,1,2048]{2,1,0:T(1,128)S(1)} %shard_map.72.refs_0_), channel_id=1, source_target_pairs={{0,256},{32,288},{64,320},{96,352},{128,384},{160,416},{192,448},{... | collective-permute-start | bytes 24584 | tf_op jit(solution)/shard_map/ppermute | solution.py:330
  113.3 20.1 %collective-permute-start.17 = (f32[1,1,1024]{2,1,0:T(1,128)S(1)}, f32[1,1,1024]{2,1,0:T(1,128)S(1)}, u32[]{:S(2)}, u32[]{:S(2)}) collective-permute-start(f32[1,1,1024]{2,1,0:T(1,128)S(1)} %shard_map.74.refs_0_), channel_id=1, source_target_pairs={{0,7},{1,0},{2,1},{3,2},{4,3},{5,4},{6,5},{7,6},{8,15},{9,8},{10,9... | collective-permute-start | bytes 12296 | tf_op jit(solution)/shard_map/ppermute | solution.py:330
  116.5 20.9 %collective-permute-start.16 = (f32[1,1,1024]{2,1,0:T(1,128)S(1)}, f32[1,1,1024]{2,1,0:T(1,128)S(1)}, u32[]{:S(2)}, u32[]{:S(2)}) collective-permute-start(f32[1,1,1024]{2,1,0:T(1,128)S(1)} %shard_map.74.refs_0_), channel_id=1, source_target_pairs={{0,6},{1,7},{2,0},{3,1},{4,2},{5,3},{6,4},{7,5},{8,14},{9,15},{10,... | collective-permute-start | bytes 12296 | tf_op jit(solution)/shard_map/ppermute | solution.py:330
  119.1 20.3 %collective-permute-start.15 = (f32[1,1,1024]{2,1,0:T(1,128)S(1)}, f32[1,1,1024]{2,1,0:T(1,128)S(1)}, u32[]{:S(2)}, u32[]{:S(2)}) collective-permute-start(f32[1,1,1024]{2,1,0:T(1,128)S(1)} %shard_map.74.refs_0_), channel_id=1, source_target_pairs={{0,5},{1,6},{2,7},{3,0},{4,1},{5,2},{6,3},{7,4},{8,13},{9,14},{10,... | collective-permute-start | bytes 12296 | tf_op jit(solution)/shard_map/ppermute | solution.py:330
  125.2 14.2 %collective-permute-start.14 = (f32[1,1,1024]{2,1,0:T(1,128)S(1)}, f32[1,1,1024]{2,1,0:T(1,128)S(1)}, u32[]{:S(2)}, u32[]{:S(2)}) collective-permute-start(f32[1,1,1024]{2,1,0:T(1,128)S(1)} %shard_map.74.refs_0_), channel_id=1, source_target_pairs={{0,4},{1,5},{2,6},{3,7},{4,0},{5,1},{6,2},{7,3},{8,12},{9,13},{10,... | collective-permute-start | bytes 12296 | tf_op jit(solution)/shard_map/ppermute | solution.py:330
  231.6 15.2 %collective-permute-start.39 = (f32[4,64,128]{2,1,0:T(8,128)S(1)}, f32[4,64,128]{2,1,0:T(8,128)S(1)}, u32[]{:S(2)}, u32[]{:S(2)}) collective-permute-start(f32[4,64,128]{2,1,0:T(8,128)S(1)} %get-tuple-element.48), channel_id=1, source_target_pairs={{0,1},{1,2},{2,3},{3,4},{4,5},{5,6},{6,7},{7,0},{8,9},{9,10},{10,1... | collective-permute-start | bytes 393224 | tf_op jit(solution)/shard_map/ppermute | solution.py:330
  233.6 13.2 %collective-permute-start.42 = (f32[4,64,128]{2,1,0:T(8,128)S(1)}, f32[4,64,128]{2,1,0:T(8,128)S(1)}, u32[]{:S(2)}, u32[]{:S(2)}) collective-permute-start(f32[4,64,128]{2,1,0:T(8,128)S(1)} %get-tuple-element.49), channel_id=1, source_target_pairs={{0,7},{1,0},{2,1},{3,2},{4,3},{5,4},{6,5},{7,6},{8,15},{9,8},{10,9... | collective-permute-start | bytes 393224 | tf_op jit(solution)/shard_map/ppermute | solution.py:330
  239.2 14.8 %collective-permute-start.27 = (f32[8,64,128]{2,1,0:T(8,128)S(1)}, f32[8,64,128]{2,1,0:T(8,128)S(1)}, u32[]{:S(2)}, u32[]{:S(2)}) collective-permute-start(f32[8,64,128]{2,1,0:T(8,128)S(1)} %slice.109), channel_id=1, source_target_pairs={{0,8},{1,9},{2,10},{3,11},{4,12},{5,13},{6,14},{7,15},{8,16},{9,17... | collective-permute-start | bytes 786440 | tf_op jit(solution)/shard_map/ppermute | solution.py:330
  244.9 35.9 %collective-permute-start.47 = (f32[8,16,2048]{2,1,0:T(8,128)S(1)}, f32[8,16,2048]{2,1,0:T(8,128)S(1)}, u32[]{:S(2)}, u32[]{:S(2)}) collective-permute-start(f32[8,16,2048]{2,1,0:T(8,128)S(1)} %get-tuple-element.37), channel_id=1, source_target_pairs={{0,32},{32,0},{64,96},{96,64},{128,160},{160,128},{192,224},{224,1... | collective-permute-start | bytes 3145736 | tf_op jit(solution)/shard_map/ppermute | solution.py:330
  246.9 13.0 %collective-permute-start.40 = (f32[4,64,128]{2,1,0:T(8,128)S(1)}, f32[4,64,128]{2,1,0:T(8,128)S(1)}, u32[]{:S(2)}, u32[]{:S(2)}) collective-permute-start(f32[4,64,128]{2,1,0:T(8,128)S(1)} %get-tuple-element.46), channel_id=1, source_target_pairs={{0,1},{1,2},{2,3},{3,4},{4,5},{5,6},{6,7},{7,0},{8,9},{9,10},{10,1... | collective-permute-start | bytes 393224 | tf_op jit(solution)/shard_map/ppermute | solution.py:330
  259.9 15.2 %collective-permute-start.44 = (f32[64,128]{1,0:T(8,128)S(1)}, f32[64,128]{1,0:T(8,128)S(1)}, u32[]{:S(2)}, u32[]{:S(2)}) collective-permute-start(f32[64,128]{1,0:T(8,128)S(1)} %get-tuple-element.58), channel_id=1, source_target_pairs={{0,8},{1,9},{2,10},{3,11},{4,12},{5,13},{6,14},{7,15},{8,16},{9,17... | collective-permute-start | bytes 98312 | tf_op jit(solution)/shard_map/ppermute | solution.py:330
  263.7 19.4 %collective-permute-start.46 = (f32[64,128]{1,0:T(8,128)S(1)}, f32[64,128]{1,0:T(8,128)S(1)}, u32[]{:S(2)}, u32[]{:S(2)}) collective-permute-start(f32[64,128]{1,0:T(8,128)S(1)} %get-tuple-element.59), channel_id=1, source_target_pairs={{0,24},{1,25},{2,26},{3,27},{4,28},{5,29},{6,30},{7,31},{8,0},{9,1... | collective-permute-start | bytes 98312 | tf_op jit(solution)/shard_map/ppermute | solution.py:330
  270.0 21.0 %collective-permute-start.34 = (f32[64,128]{1,0:T(8,128)S(1)}, f32[64,128]{1,0:T(8,128)S(1)}, u32[]{:S(2)}, u32[]{:S(2)}) collective-permute-start(f32[64,128]{1,0:T(8,128)S(1)} %get-tuple-element.57), channel_id=1, source_target_pairs={{0,7},{1,0},{2,1},{3,2},{4,3},{5,4},{6,5},{7,6},{8,15},{9,8},{10,9... | collective-permute-start | bytes 98312 | tf_op jit(solution)/shard_map/ppermute | solution.py:330
  283.2 14.9 %collective-permute-start.52 = (f32[16,2048]{1,0:T(8,128)S(1)}, f32[16,2048]{1,0:T(8,128)S(1)}, u32[]{:S(2)}, u32[]{:S(2)}) collective-permute-start(f32[16,2048]{1,0:T(8,128)S(1)} %get-tuple-element.43), channel_id=1, source_target_pairs={{0,448},{32,480},{64,0},{96,32},{128,64},{160,96},{192,128},{224,1... | collective-permute-start | bytes 393224 | tf_op jit(solution)/shard_map/ppermute | solution.py:330
  291.0 14.2 %collective-permute-start.32 = (f32[64,128]{1,0:T(8,128)S(1)}, f32[64,128]{1,0:T(8,128)S(1)}, u32[]{:S(2)}, u32[]{:S(2)}) collective-permute-start(f32[64,128]{1,0:T(8,128)S(1)} %get-tuple-element.54), channel_id=1, source_target_pairs={{0,1},{1,2},{2,3},{3,4},{4,5},{5,6},{6,7},{7,0},{8,9},{9,10},{10,1... | collective-permute-start | bytes 98312 | tf_op jit(solution)/shard_map/ppermute | solution.py:330
  293.0 12.3 %collective-permute-start.35 = (f32[64,128]{1,0:T(8,128)S(1)}, f32[64,128]{1,0:T(8,128)S(1)}, u32[]{:S(2)}, u32[]{:S(2)}) collective-permute-start(f32[64,128]{1,0:T(8,128)S(1)} %get-tuple-element.55), channel_id=1, source_target_pairs={{0,7},{1,0},{2,1},{3,2},{4,3},{5,4},{6,5},{7,6},{8,15},{9,8},{10,9... | collective-permute-start | bytes 98312 | tf_op jit(solution)/shard_map/ppermute | solution.py:330
  298.2 14.2 %collective-permute-start.50 = (f32[16,2048]{1,0:T(8,128)S(1)}, f32[16,2048]{1,0:T(8,128)S(1)}, u32[]{:S(2)}, u32[]{:S(2)}) collective-permute-start(f32[16,2048]{1,0:T(8,128)S(1)} %get-tuple-element.40), channel_id=1, source_target_pairs={{0,64},{32,96},{64,128},{96,160},{128,192},{160,224},{192,256},{22... | collective-permute-start | bytes 393224 | tf_op jit(solution)/shard_map/ppermute | solution.py:330
  300.1 12.3 %collective-permute-start.53 = (f32[16,2048]{1,0:T(8,128)S(1)}, f32[16,2048]{1,0:T(8,128)S(1)}, u32[]{:S(2)}, u32[]{:S(2)}) collective-permute-start(f32[16,2048]{1,0:T(8,128)S(1)} %get-tuple-element.41), channel_id=1, source_target_pairs={{0,448},{32,480},{64,0},{96,32},{128,64},{160,96},{192,128},{224,1... | collective-permute-start | bytes 393224 | tf_op jit(solution)/shard_map/ppermute | solution.py:330
  305.3 14.2 %collective-permute-start.33 = (f32[64,128]{1,0:T(8,128)S(1)}, f32[64,128]{1,0:T(8,128)S(1)}, u32[]{:S(2)}, u32[]{:S(2)}) collective-permute-start(f32[64,128]{1,0:T(8,128)S(1)} %get-tuple-element.52), channel_id=1, source_target_pairs={{0,1},{1,2},{2,3},{3,4},{4,5},{5,6},{6,7},{7,0},{8,9},{9,10},{10,1... | collective-permute-start | bytes 98312 | tf_op jit(solution)/shard_map/ppermute | solution.py:330
  307.2 12.3 %collective-permute-start.36 = (f32[64,128]{1,0:T(8,128)S(1)}, f32[64,128]{1,0:T(8,128)S(1)}, u32[]{:S(2)}, u32[]{:S(2)}) collective-permute-start(f32[64,128]{1,0:T(8,128)S(1)} %get-tuple-element.53), channel_id=1, source_target_pairs={{0,7},{1,0},{2,1},{3,2},{4,3},{5,4},{6,5},{7,6},{8,15},{9,8},{10,9... | collective-permute-start | bytes 98312 | tf_op jit(solution)/shard_map/ppermute | solution.py:330
  (46 other events, 570.6 us)

commit v2 on v1

v2 whole, which is shorter than its diff:
```python
import functools
import math

import jax
import jax.numpy as jnp
from jax import lax
from jax.experimental import pallas as pl
from jax.experimental.pallas import tpu as pltpu
from jax.sharding import PartitionSpec as P

PROTOS = 65536
SK_ITERS = 3
LANES = 128

epsilon = 1e-06
temp_student = 0.1
temp_teacher = 0.07

f32 = jnp.float32
bf16 = jnp.bfloat16


def call(body, outs, ins, scratch=(), limit=8, hbm=0, flops=0, moved=0):
    held = [pltpu.with_memory_space_constraint(array, pltpu.HBM) for array in ins[:hbm]]
    spaces = [pltpu.HBM] * hbm + [pltpu.VMEM] * (len(ins) - hbm)
    return pl.pallas_call(
        body,
        out_shape=[pltpu.VMEM(s, d) for s, d in outs],
        in_specs=[pl.BlockSpec(memory_space=space) for space in spaces],
        out_specs=[pl.BlockSpec(memory_space=pltpu.VMEM)] * len(outs),
        scratch_shapes=list(scratch),
        compiler_params=pltpu.CompilerParams(vmem_limit_bytes=limit * 2**20),
        cost_estimate=pl.CostEstimate(flops=flops, bytes_accessed=moved, transcendentals=0),
    )(*held, *ins[hbm:])


def selector(mask_ref, image, patches):
    wanted = mask_ref[pl.ds(image, 1), :]
    masked = wanted.shape[1]
    return lax.broadcasted_iota(jnp.int32, (patches, masked), 0) == wanted


def pick(patches_ref, mask_ref, image):
    patches = patches_ref.shape[1]
    chosen = selector(mask_ref, image, patches).astype(bf16)
    return lax.dot_general(
        chosen, patches_ref[image], (((0,), (0,)), ((), ())), preferred_element_type=f32
    )


def lanes_of_rows(parts):
    return jnp.sum(parts.T, axis=0, keepdims=True)


def fold_lanes(values):
    total = values[:, :LANES]
    for start in range(LANES, values.shape[1], LANES):
        total = total + values[:, start : start + LANES]
    return total


def rows_on_sublanes(line):
    pieces = [
        jnp.broadcast_to(line[:, s : s + LANES], (LANES, LANES)).T
        for s in range(0, line.shape[1], LANES)
    ]
    return jnp.concatenate(pieces, axis=0)


def spread(column, width):
    return jnp.concatenate([column] * (width // LANES), axis=1)


def unit_columns(weight_ref, cols):
    weight = weight_ref[:, cols].astype(f32)
    length = jnp.sqrt(jnp.sum(weight * weight, axis=0, keepdims=True) + epsilon)
    return weight / length, length


TILE = 256
LOG2_E = math.log2(math.e)


def first_body(
    teacher_hbm, teacher_weight_hbm, student_hbm, student_weight_hbm, mask_ref,
    teacher_exp_ref, cols_ref, student_exp_ref, student_rows_ref, unit_ref, inverse_ref, turned_ref, back_ref,
    length_ref,
    teacher_ref, teacher_weight_ref, student_ref, student_weight_ref, teacher_bf_ref, student_bf_ref, parts_ref, sems,
):
    images, masked = mask_ref.shape
    protos = teacher_exp_ref.shape[1]
    loads = [
        pltpu.make_async_copy(source, target, sems.at[index])
        for index, (source, target) in enumerate(
            (
                (teacher_hbm, teacher_ref),
                (teacher_weight_hbm, teacher_weight_ref),
                (student_hbm, student_ref),
                (student_weight_hbm, student_weight_ref),
            )
        )
    ]
    for load in loads:
        load.start()
    loads[0].wait()

    def teacher_image(image, _):
        picked = pick(teacher_ref, mask_ref, image)
        length = jnp.sqrt(jnp.sum(picked * picked, axis=1, keepdims=True) + epsilon)
        rows = pl.ds(pl.multiple_of(image * masked, masked), masked)
        teacher_bf_ref[rows, :] = (picked / length).astype(bf16)
        return 0

    lax.fori_loop(0, images, teacher_image, 0)
    loads[1].wait()

    def teacher_tile(tile, _):
        cols = pl.ds(pl.multiple_of(tile * TILE, TILE), TILE)
        unit = unit_columns(teacher_weight_ref, cols)[0].astype(bf16)
        products = jnp.dot(teacher_bf_ref[...], unit, preferred_element_type=f32)
        exps = jnp.exp2(products * (LOG2_E / temp_teacher))
        teacher_exp_ref[:, cols] = exps
        line = jnp.sum(exps, axis=0, keepdims=True)
        cols_ref[:, :, cols] = jnp.broadcast_to(line[None], (cols_ref.shape[0], 1, TILE))
        return 0

    lax.fori_loop(0, protos // TILE, teacher_tile, 0)
    loads[2].wait()

    def student_image(image, _):
        picked = pick(student_ref, mask_ref, image)
        length = jnp.sqrt(jnp.sum(picked * picked, axis=1, keepdims=True) + epsilon)
        unit = picked / length
        rows = pl.ds(pl.multiple_of(image * masked, masked), masked)
        unit_ref[rows, :] = unit
        student_bf_ref[rows, :] = unit.astype(bf16)
        turned_ref[:, rows] = unit.T.astype(bf16)
        inverse_ref[rows, :] = jnp.broadcast_to(1.0 / length, (masked, LANES))
        return 0

    lax.fori_loop(0, images, student_image, 0)
    parts_ref[...] = jnp.zeros_like(parts_ref)
    loads[3].wait()

    def student_tile(tile, _):
        cols = pl.ds(pl.multiple_of(tile * TILE, TILE), TILE)
        unit, length = unit_columns(student_weight_ref, cols)
        length_ref[:, cols] = length
        back_ref[cols, :] = unit.T.astype(bf16)
        products = jnp.dot(student_bf_ref[...], unit.astype(bf16), preferred_element_type=f32)
        exps = jnp.exp2(products * (LOG2_E / temp_student))
        student_exp_ref[:, cols] = exps
        parts_ref[...] += fold_lanes(exps)
        return 0

    lax.fori_loop(0, protos // TILE, student_tile, 0)
    student_rows_ref[...] = lanes_of_rows(parts_ref[...])


def store_copies(out_ref, line):
    out_ref[...] = jnp.broadcast_to(line[None], out_ref.shape)


def columns_body(sums_ref, exp_ref, *refs):
    *student, scale_ref, rows_ref, parts_ref = refs
    scale = 1.0 / (jnp.sum(sums_ref[...], axis=0) * PROTOS)
    scale_ref[...] = scale
    step = 64

    def block(index, _):
        rows = pl.ds(pl.multiple_of(index * step, step), step)
        total = exp_ref[rows, :LANES] * scale[:, :LANES]
        for start in range(LANES, exp_ref.shape[1], LANES):
            total = total + exp_ref[rows, start : start + LANES] * scale[:, start : start + LANES]
        parts_ref[rows, :] = total
        return 0

    lax.fori_loop(0, exp_ref.shape[0] // step, block, 0)
    line = lanes_of_rows(parts_ref[...])
    if student:
        line = jnp.concatenate([line, student[0][...]], axis=1)
    store_copies(rows_ref, line)


def rows_body(total_rows, sums_ref, exp_ref, cols_ref, scale_ref, parts_ref):
    line = 1.0 / (jnp.sum(sums_ref[...], axis=0)[:, : exp_ref.shape[0]] * total_rows)
    scale_ref[...] = rows_on_sublanes(line)
    width = exp_ref.shape[1]
    parts_ref[...] = jnp.zeros_like(parts_ref)
    step = 64

    def block(index, _):
        rows = pl.ds(pl.multiple_of(index * step, step), step)
        scale = scale_ref[rows, :]
        for start in range(0, width, LANES):
            product = exp_ref[rows, start : start + LANES] * scale
            total = product[0:8]
            for r in range(8, step, 8):
                total = total + product[r : r + 8]
            parts_ref[:, start : start + LANES] += total
        return 0

    lax.fori_loop(0, exp_ref.shape[0] // step, block, 0)
    store_copies(cols_ref, jnp.sum(parts_ref[...], axis=0, keepdims=True))


def three_pieces(values):
    high = values.astype(bf16)
    rest = values - high.astype(f32)
    middle = rest.astype(bf16)
    return high, middle, (rest - middle.astype(f32)).astype(bf16)


def gradient_body(
    total_rows, shares,
    sums_ref, student_ref, cols_ref, teacher_exp_ref, student_exp_ref, back_ref, turned_ref, unit_ref, inverse_ref,
    mask_ref, weight_ref, length_ref,
    placed_ref, weight_out_ref, row_ref, total_ref, sum_ref,
):
    rows = teacher_exp_ref.shape[0]
    row_ref[...] = rows_on_sublanes(1.0 / (jnp.sum(sums_ref[...], axis=0) * total_rows))
    total_ref[...] = rows_on_sublanes((1.0 / temp_student) / jnp.sum(student_ref[...], axis=0)[:, rows:])
    sum_ref[...] = jnp.zeros_like(sum_ref)

    def one_tile(tile, _):
        cols = pl.ds(pl.multiple_of(tile * TILE, TILE), TILE)
        target = teacher_exp_ref[:, cols] * spread(row_ref[...], TILE)
        target = target * (cols_ref[:, cols] * (total_rows / temp_student))
        score = (student_exp_ref[:, cols] * spread(total_ref[...], TILE) - target).astype(bf16)
        total = jnp.dot(turned_ref[...], score, preferred_element_type=f32)
        inverse = 1.0 / length_ref[:, cols]
        unit = weight_ref[:, cols].astype(f32) * inverse
        dots = jnp.sum(unit * total, axis=0, keepdims=True)
        weight_out_ref[:, cols] = (total - unit * dots) * inverse
        sum_ref[...] += jnp.dot(score, back_ref[cols, :], preferred_element_type=f32)
        return 0

    lax.fori_loop(0, teacher_exp_ref.shape[1] // TILE, one_tile, 0)
    images, masked = mask_ref.shape
    width = unit_ref.shape[1]
    patches = placed_ref.shape[0] * placed_ref.shape[1] // images
    share = patches // shares

    def one_image(image, _):
        rows = pl.ds(pl.multiple_of(image * masked, masked), masked)
        unit = unit_ref[rows, :]
        total = sum_ref[rows, :]
        projection = jnp.sum(unit * total, axis=1, keepdims=True)
        pieces = three_pieces((total - unit * projection) * spread(inverse_ref[rows, :], width))
        chosen = selector(mask_ref, image, patches).astype(bf16)
        placed = sum(jnp.dot(chosen, piece, preferred_element_type=f32) for piece in pieces)
        placed_ref[:, pl.ds(pl.multiple_of(image * share, share), share), :] = placed.reshape(
            shares, share, width
        )
        return 0

    lax.fori_loop(0, images, one_image, 0)


def everyones(copies, axis):
    return lax.all_to_all(copies, axis, 0, 0, tiled=True)


def share_of_sum(parts, axis):
    return jnp.sum(lax.all_to_all(parts, axis, 0, 0, tiled=True), axis=0)


def local(student_patches, teacher_patches, mask_index, student_weight, teacher_weight):
    images, patches, depth = student_patches.shape
    masked = mask_index.shape[1]
    rows = images * masked
    row_devices = lax.axis_size("rows")
    proto_devices = lax.axis_size("protos")
    total_rows = float(rows * row_devices)
    protos = student_weight.shape[1]
    work = 2 * rows * protos * depth

    teacher_exp, column_part, student_exp, student_part, unit, inverse, turned, back, length = call(
        first_body,
        [
            ((rows, protos), f32),
            ((row_devices, 1, protos), f32),
            ((rows, protos), f32),
            ((1, rows), f32),
            ((rows, depth), f32),
            ((rows, LANES), f32),
            ((depth, rows), bf16),
            ((protos, depth), bf16),
            ((1, protos), f32),
        ],
        (teacher_patches, teacher_weight, student_patches, student_weight, mask_index),
        [
            pltpu.VMEM(teacher_patches.shape, bf16),
            pltpu.VMEM(teacher_weight.shape, bf16),
            pltpu.VMEM(student_patches.shape, bf16),
            pltpu.VMEM(student_weight.shape, bf16),
            pltpu.VMEM((rows, depth), bf16),
            pltpu.VMEM((rows, depth), bf16),
            pltpu.VMEM((rows, LANES), f32),
            pltpu.SemaphoreType.DMA((4,)),
        ],
        limit=12, hbm=4, flops=2 * work, moved=2**23,
    )
    for sweep in range(SK_ITERS):
        column_sums = everyones(column_part, "rows")
        student = (student_part,) if sweep == 0 else ()
        col_scale, row_part = call(
            columns_body,
            [((1, protos), f32), ((proto_devices, 1, rows * (1 + len(student))), f32)],
            (column_sums, teacher_exp, *student),
            [pltpu.VMEM((rows, LANES), f32)],
            flops=2 * rows * protos, moved=2**23,
        )
        row_sums = everyones(row_part, "protos")
        if sweep == 0:
            student_sums = row_sums
        if sweep < SK_ITERS - 1:
            (column_part,) = call(
                functools.partial(rows_body, total_rows),
                [((row_devices, 1, protos), f32)],
                (row_sums, teacher_exp),
                [pltpu.VMEM((rows, LANES), f32), pltpu.VMEM((8, protos), f32)],
                flops=2 * rows * protos, moved=2**23,
            )
    share = patches // proto_devices
    placed, columns = call(
        functools.partial(gradient_body, total_rows, proto_devices),
        [((proto_devices, images * share, depth), f32), ((depth, protos), f32)],
        (
            row_sums, student_sums, col_scale, teacher_exp, student_exp, back, turned, unit, inverse, mask_index,
            student_weight, length,
        ),
        [
            pltpu.VMEM((rows, LANES), f32),
            pltpu.VMEM((rows, LANES), f32),
            pltpu.VMEM((rows, depth), f32),
        ],
        flops=2 * work, moved=2**24,
    )
    grad_weight = lax.psum_scatter(columns, "rows", scatter_dimension=0, tiled=True)
    grad_patches = share_of_sum(placed, "protos").reshape(images, share, depth)
    return (grad_patches, grad_weight)


def solution(mesh):
    placed = (
        P("rows", None, None),
        P("rows", None, None),
        P("rows", None),
        P(None, "protos"),
        P(None, "protos"),
    )
    return jax.shard_map(
        local,
        mesh=mesh,
        in_specs=placed,
        out_specs=(P("rows", "protos", None), P("rows", "protos")),
        check_vma=False,
    )
```

time: 325 us -> 196 us (0.60)
  the two profiles are of different devices: /device:TPU:2 before, /device:TPU:8 now
where the time goes in v2:
time: 196 us; the launch traced here: 195 us
  blocking collectives  150 us (77%)
  Pallas kernels  28.4 us (14%)
  between operations  14.1 us (7%)
  other arithmetic  2.36 us (1%)
    all_to_all x6, blocking collectives, everyones(): return lax.all_to_all(copies, axis, 0, 0, tiled=True)  94.7 us
    all_to_all x1, blocking collectives, share_of_sum(): return jnp.sum(lax.all_to_all(parts, axis, 0, 0, tiled=True), axis=0)  55.1 us
    pallas_call x7, Pallas kernels, call(): pl.pallas_call(body, out_shape=[pltpu.VMEM(s, d) for s, d in outs], in_sp...  28.4 us
  transfers between devices with their start and end apart: 1, of which 0 were waited for; matrix products, arithmetic and copies ran while one was open for 1% of the time, Pallas kernels for 0%

profile of v2, /device:TPU:8, one launch (start us, length us, event | category | flops | bytes accessed | tf_op | source)
XLA Modules:
  0.0 195.3 jit_solution(12986914961911664381)
XLA Ops:
  7.2 0.0 reduce-scatter.2.cloned.1.call-start
  7.2 0.0 copy-start.1
  7.2 0.7 copy-done.1
  7.9 13.3 %shard_map.68 = (f32[1024,2048]{1,0:T(8,128)S(1)}, f32[16,1,2048]{2,1,0:T(1,128)S(1)}, f32[1024,2048]{1,0:T(8,128)S(1)}, f32[1,1024]{1,0:T(1,128)S(1)}, f32[1024...) custom-call(bf16[8,256,256]{2,1,0:T(8,128)(2,1)} %teacher_hbm.1, ...), custom_call_target="tpu_custom_call" | custom-call | flops 2147483648 | bytes 8388608 | tf_op jit(solution)/shard_map/pallas_call | solution.py:26
  21.2 19.0 %all_to_all.35.sums_ref = f32[16,1,2048]{2,1,0:T(1,128)S(1)} all-to-all(f32[16,1,2048]{2,1,0:T(1,128)S(1)} %get-tuple-element.17), channel_id=1, replica_groups=mesh['rows'=16,'protos'=32] {'rows'}, dimensions={0} | all-to-all | bytes 262144 | tf_op jit(solution)/shard_map/all_to_all | solution.py:261
  40.1 1.6 shard_map.69
  41.7 23.1 %all_to_all.36.sums_ref.student_ref = f32[32,1,2048]{2,1,0:T(1,128)S(1)} all-to-all(f32[32,1,2048]{2,1,0:T(1,128)S(1)} %get-tuple-element.20), channel_id=1, replica_groups=mesh['rows'=16,'protos'=32] {'protos'}, dimensions={0} | all-to-all | bytes 524288 | tf_op jit(solution)/shard_map/all_to_all | solution.py:261
  64.8 1.0 shard_map.70
  65.9 11.3 %all_to_all.37.sums_ref = f32[16,1,2048]{2,1,0:T(1,128)S(1)} all-to-all(f32[16,1,2048]{2,1,0:T(1,128)S(1)} %shard_map.70), channel_id=1, replica_groups=mesh['rows'=16,'protos'=32] {'rows'}, dimensions={0} | all-to-all | bytes 262144 | tf_op jit(solution)/shard_map/all_to_all | solution.py:261
  77.2 1.4 shard_map.71
  78.6 15.1 %all_to_all.38.sums_ref = f32[32,1,1024]{2,1,0:T(1,128)S(1)} all-to-all(f32[32,1,1024]{2,1,0:T(1,128)S(1)} %get-tuple-element.21), channel_id=1, replica_groups=mesh['rows'=16,'protos'=32] {'protos'}, dimensions={0} | all-to-all | bytes 262144 | tf_op jit(solution)/shard_map/all_to_all | solution.py:261
  93.7 1.0 shard_map.72
  94.8 11.3 %all_to_all.39.sums_ref = f32[16,1,2048]{2,1,0:T(1,128)S(1)} all-to-all(f32[16,1,2048]{2,1,0:T(1,128)S(1)} %shard_map.72), channel_id=1, replica_groups=mesh['rows'=16,'protos'=32] {'rows'}, dimensions={0} | all-to-all | bytes 262144 | tf_op jit(solution)/shard_map/all_to_all | solution.py:261
  106.1 0.0 copy-start
  106.1 0.0 copy-start.2
  106.1 1.1 shard_map.73
  107.2 14.8 %all_to_all.40.sums_ref = f32[32,1,1024]{2,1,0:T(1,128)S(1)} all-to-all(f32[32,1,1024]{2,1,0:T(1,128)S(1)} %get-tuple-element.22), channel_id=1, replica_groups=mesh['rows'=16,'protos'=32] {'protos'}, dimensions={0} | all-to-all | bytes 262144 | tf_op jit(solution)/shard_map/all_to_all | solution.py:261
  122.0 0.0 copy-done
  122.0 0.0 copy-done.2
  122.0 9.0 %shard_map.74 = (f32[32,64,256]{2,1,0:T(8,128)S(1)}, f32[256,2048]{1,0:T(8,128)}) custom-call(f32[32,1,1024]{2,1,0:T(1,128)S(1)} %all_to_all.40.sums_ref, f32[32,1,2048]{2,1,0:T(1,128)S(1)} %all_to_all.36.sums_ref.student_ref, f32[1,2048]{1,0:T(1,128)S(1)} %get-tuple-element.23.cols_ref, f32[1024,2048]{1,0:T(8,128)S(1)} %get-tuple-element.18.exp_ref.teacher_exp_ref, ...), custom_call_target="tpu_custom_call" | custom-call | flops 2147483648 | bytes 16777216 | tf_op jit(solution)/shard_map/pallas_call | solution.py:26
  131.0 0.0 reduce-scatter.2.cloned.1.call-update
  131.0 55.1 %all_to_all.41 = f32[32,64,256]{2,1,0:T(8,128)} all-to-all(f32[32,64,256]{2,1,0:T(8,128)S(1)} %get-tuple-element.30), channel_id=1, replica_groups=mesh['rows'=16,'protos'=32] {'protos'}, dimensions={0} | all-to-all | bytes 4194304 | tf_op jit(solution)/shard_map/all_to_all | solution.py:265
  186.1 2.4 %reduce_sum.9 = f32[64,256]{1,0:T(8,128)} reduce(f32[32,64,256]{2,1,0:T(8,128)} %all_to_all.41, f32[]{:T(128)} %constant.0.clone.1), dimensions={0}, to_apply=%region_0.0 | reduce | flops 507904 | bytes 2162692 | tf_op jit(solution)/shard_map/reduce_sum | solution.py:265
  188.5 0.0 reduce-scatter.2.cloned.1.call-done
Async XLA Ops:
  7.2 181.3 %reduce-scatter.2.cloned.1.call-start = ((), (), s32[]{:S(2)}) async-start(), calls=%async_computation.8 | async-start | bytes 2228224 | tf_op jit(solution)/shard_map/reduce_scatter | solution.py:340
  7.2 0.7 copy-start.1
  106.1 15.9 %copy-start = (bf16[256,2048]{1,0:T(8,128)(2,1)S(1)}, bf16[256,2048]{1,0:T(8,128)(2,1)}, u32[]{:S(2)}) copy-start(bf16[256,2048]{1,0:T(8,128)(2,1)} %weight_ref.1) | copy-start | bytes 3145732
  106.1 15.9 %copy-start.2 = (s32[8,128]{1,0:T(8,128)S(1)}, s32[8,128]{1,0:T(8,128)}, u32[]{:S(2)}) copy-start(s32[8,128]{1,0:T(8,128)} %mask_ref.3) | copy-start | bytes 12292
Sparse Core Ops, SparseCore 0:
  131.1 55.4 reduce-scatter.1

commit v3 on v2

--- a/solution.py
+++ b/solution.py
@@ -74,7 +74,7 @@
 def unit_columns(weight_ref, cols):
     weight = weight_ref[:, cols].astype(f32)
     length = jnp.sqrt(jnp.sum(weight * weight, axis=0, keepdims=True) + epsilon)
-    return weight / length, length
+    return weight * (1.0 / length), length
 
 
 TILE = 256
@@ -108,10 +108,10 @@
         picked = pick(teacher_ref, mask_ref, image)
         length = jnp.sqrt(jnp.sum(picked * picked, axis=1, keepdims=True) + epsilon)
         rows = pl.ds(pl.multiple_of(image * masked, masked), masked)
-        teacher_bf_ref[rows, :] = (picked / length).astype(bf16)
-        return 0
-
-    lax.fori_loop(0, images, teacher_image, 0)
+        teacher_bf_ref[rows, :] = (picked * (1.0 / length)).astype(bf16)
+        return 0
+
+    lax.fori_loop(0, images, teacher_image, 0, unroll=2)
     loads[1].wait()
 
     def teacher_tile(tile, _):
@@ -124,21 +124,22 @@
         cols_ref[:, :, cols] = jnp.broadcast_to(line[None], (cols_ref.shape[0], 1, TILE))
         return 0
 
-    lax.fori_loop(0, protos // TILE, teacher_tile, 0)
+    lax.fori_loop(0, protos // TILE, teacher_tile, 0, unroll=2)
     loads[2].wait()
 
     def student_image(image, _):
         picked = pick(student_ref, mask_ref, image)
         length = jnp.sqrt(jnp.sum(picked * picked, axis=1, keepdims=True) + epsilon)
-        unit = picked / length
+        inverse = 1.0 / length
+        unit = picked * inverse
         rows = pl.ds(pl.multiple_of(image * masked, masked), masked)
         unit_ref[rows, :] = unit
         student_bf_ref[rows, :] = unit.astype(bf16)
         turned_ref[:, rows] = unit.T.astype(bf16)
-        inverse_ref[rows, :] = jnp.broadcast_to(1.0 / length, (masked, LANES))
-        return 0
-
-    lax.fori_loop(0, images, student_image, 0)
+        inverse_ref[rows, :] = jnp.broadcast_to(inverse, (masked, LANES))
+        return 0
+
+    lax.fori_loop(0, images, student_image, 0, unroll=2)
     parts_ref[...] = jnp.zeros_like(parts_ref)
     loads[3].wait()
 
@@ -153,7 +154,7 @@
         parts_ref[...] += fold_lanes(exps)
         return 0
 
-    lax.fori_loop(0, protos // TILE, student_tile, 0)
+    lax.fori_loop(0, protos // TILE, student_tile, 0, unroll=2)
     student_rows_ref[...] = lanes_of_rows(parts_ref[...])
 
 
@@ -175,7 +176,7 @@
         parts_ref[rows, :] = total
         return 0
 
-    lax.fori_loop(0, exp_ref.shape[0] // step, block, 0)
+    lax.fori_loop(0, exp_ref.shape[0] // step, block, 0, unroll=2)
     line = lanes_of_rows(parts_ref[...])
     if student:
         line = jnp.concatenate([line, student[0][...]], axis=1)
@@ -200,7 +201,7 @@
             parts_ref[:, start : start + LANES] += total
         return 0
 
-    lax.fori_loop(0, exp_ref.shape[0] // step, block, 0)
+    lax.fori_loop(0, exp_ref.shape[0] // step, block, 0, unroll=2)
     store_copies(cols_ref, jnp.sum(parts_ref[...], axis=0, keepdims=True))
 
 
@@ -215,12 +216,14 @@
     total_rows, shares,
     sums_ref, student_ref, cols_ref, teacher_exp_ref, student_exp_ref, back_ref, turned_ref, unit_ref, inverse_ref,
     mask_ref, weight_ref, length_ref,
-    placed_ref, weight_out_ref, row_ref, total_ref, sum_ref,
+    placed_ref, mine_ref, other_ref, row_ref, total_ref, sum_ref, score_ref,
 ):
     rows = teacher_exp_ref.shape[0]
     row_ref[...] = rows_on_sublanes(1.0 / (jnp.sum(sums_ref[...], axis=0) * total_rows))
     total_ref[...] = rows_on_sublanes((1.0 / temp_student) / jnp.sum(student_ref[...], axis=0)[:, rows:])
-    sum_ref[...] = jnp.zeros_like(sum_ref)
+    levels, depth_share = mine_ref.shape[:2]
+    me = lax.axis_index("rows")
+    core, level = me % 2, me // 2
 
     def one_tile(tile, _):
         cols = pl.ds(pl.multiple_of(tile * TILE, TILE), TILE)
@@ -231,11 +234,16 @@
         inverse = 1.0 / length_ref[:, cols]
         unit = weight_ref[:, cols].astype(f32) * inverse
         dots = jnp.sum(unit * total, axis=0, keepdims=True)
-        weight_out_ref[:, cols] = (total - unit * dots) * inverse
-        sum_ref[...] += jnp.dot(score, back_ref[cols, :], preferred_element_type=f32)
-        return 0
-
-    lax.fori_loop(0, teacher_exp_ref.shape[1] // TILE, one_tile, 0)
+        gradient = ((total - unit * dots) * inverse).reshape(levels, 2, depth_share, TILE)
+        for z in range(levels):
+            place = pl.ds((z + levels - level) % levels, 1)
+            mine_ref[place, :, cols] = jnp.where(core == 0, gradient[z, 0], gradient[z, 1])[None]
+            other_ref[place, :, cols] = jnp.where(core == 0, gradient[z, 1], gradient[z, 0])[None]
+        score_ref[:, cols] = score
+        return 0
+
+    lax.fori_loop(0, teacher_exp_ref.shape[1] // TILE, one_tile, 0, unroll=2)
+    sum_ref[...] = jnp.dot(score_ref[...], back_ref[...], preferred_element_type=f32)
     images, masked = mask_ref.shape
     width = unit_ref.shape[1]
     patches = placed_ref.shape[0] * placed_ref.shape[1] // images
@@ -254,7 +262,7 @@
         )
         return 0
 
-    lax.fori_loop(0, images, one_image, 0)
+    lax.fori_loop(0, images, one_image, 0, unroll=2)
 
 
 def everyones(copies, axis):
@@ -263,6 +271,10 @@
 
 def share_of_sum(parts, axis):
     return jnp.sum(lax.all_to_all(parts, axis, 0, 0, tiled=True), axis=0)
+
+
+def send_rows(values, to):
+    return lax.ppermute(values, "rows", [(i, to(i)) for i in range(lax.axis_size("rows"))])
 
 
 def local(student_patches, teacher_patches, mask_index, student_weight, teacher_weight):
@@ -323,9 +335,10 @@
                 flops=2 * rows * protos, moved=2**23,
             )
     share = patches // proto_devices
-    placed, columns = call(
+    levels = row_devices // 2
+    placed, mine, other = call(
         functools.partial(gradient_body, total_rows, proto_devices),
-        [((proto_devices, images * share, depth), f32), ((depth, protos), f32)],
+        [((proto_devices, images * share, depth), f32)] + [((levels, depth // row_devices, protos), f32)] * 2,
         (
             row_sums, student_sums, col_scale, teacher_exp, student_exp, back, turned, unit, inverse, mask_index,
             student_weight, length,
@@ -334,10 +347,14 @@
             pltpu.VMEM((rows, LANES), f32),
             pltpu.VMEM((rows, LANES), f32),
             pltpu.VMEM((rows, depth), f32),
+            pltpu.VMEM((rows, protos), bf16),
         ],
-        flops=2 * work, moved=2**24,
-    )
-    grad_weight = lax.psum_scatter(columns, "rows", scatter_dimension=0, tiled=True)
+        limit=12, flops=2 * work, moved=2**24,
+    )
+    levels_parts = mine + send_rows(other, lambda i: i ^ 1)
+    grad_weight = levels_parts[0]
+    for ahead in range(1, levels):
+        grad_weight = grad_weight + send_rows(levels_parts[ahead], lambda i: (i + 2 * ahead) % row_devices)
     grad_patches = share_of_sum(placed, "protos").reshape(images, share, depth)
     return (grad_patches, grad_weight)
 

time: 196 us -> 177 us (0.903)
  the two profiles are of different devices: /device:TPU:8 before, /device:TPU:1 now
where the time goes in v3:
time: 177 us; the launch traced here: 176 us
  blocking collectives  94.7 us (54%)
  starting transfers between devices  32.1 us (18%)
  Pallas kernels  23.2 us (13%)
  waiting for transfers between devices  21.1 us (12%)
  other arithmetic  3.18 us (2%)
    all_to_all x6, blocking collectives, everyones(): return lax.all_to_all(copies, axis, 0, 0, tiled=True)  94.7 us
    ppermute x8, starting transfers between devices, send_rows(): lax.ppermute(values, 'rows', [(i, to(i)) for i in range(lax.axis_size('ro...  27.3 us
    pallas_call x7, Pallas kernels, call(): pl.pallas_call(body, out_shape=[pltpu.VMEM(s, d) for s, d in outs], in_sp...  23.2 us
    ppermute x8, waiting for transfers between devices, send_rows(): lax.ppermute(values, 'rows', [(i, to(i)) for i in range(lax.axis_size('ro...  16.2 us
    all_to_all x1, waiting for transfers between devices, share_of_sum(): return jnp.sum(lax.all_to_all(parts, axis, 0, 0, tiled=True), axis=0)  4.92 us
    all_to_all x1, starting transfers between devices, share_of_sum(): return jnp.sum(lax.all_to_all(parts, axis, 0, 0, tiled=True), axis=0)  4.77 us
  transfers between devices with their start and end apart: 9, of which 5 were waited for; matrix products, arithmetic and copies ran while one was open for 1% of the time, Pallas kernels for 0%

profile of v3, /device:TPU:1, one launch (start us, length us, event | category | flops | bytes accessed | tf_op | source)
XLA Modules:
  0.0 175.8 jit_solution(15940461100877216141)
XLA Ops:
  1.3 9.3 %shard_map.68 = (f32[1024,2048]{1,0:T(8,128)S(1)}, f32[16,1,2048]{2,1,0:T(1,128)S(1)}, f32[1024,2048]{1,0:T(8,128)S(1)}, f32[1,1024]{1,0:T(1,128)S(1)}, f32[1024...) custom-call(bf16[8,256,256]{2,1,0:T(8,128)(2,1)} %teacher_hbm.1, ...), custom_call_target="tpu_custom_call" | custom-call | flops 2147483648 | bytes 8388608 | tf_op jit(solution)/shard_map/pallas_call | solution.py:26
  10.7 20.8 %all_to_all.35.sums_ref = f32[16,1,2048]{2,1,0:T(1,128)S(1)} all-to-all(f32[16,1,2048]{2,1,0:T(1,128)S(1)} %get-tuple-element.18), channel_id=1, replica_groups=mesh['rows'=16,'protos'=32] {'rows'}, dimensions={0} | all-to-all | bytes 262144 | tf_op jit(solution)/shard_map/all_to_all | solution.py:269
  31.4 1.5 shard_map.69
  32.9 20.2 %all_to_all.36.sums_ref.student_ref = f32[32,1,2048]{2,1,0:T(1,128)S(1)} all-to-all(f32[32,1,2048]{2,1,0:T(1,128)S(1)} %get-tuple-element.21), channel_id=1, replica_groups=mesh['rows'=16,'protos'=32] {'protos'}, dimensions={0} | all-to-all | bytes 524288 | tf_op jit(solution)/shard_map/all_to_all | solution.py:269
  54.0 13.9 %all_to_all.37.sums_ref = f32[16,1,2048]{2,1,0:T(1,128)S(1)} all-to-all(f32[16,1,2048]{2,1,0:T(1,128)S(1)} %shard_map.70), channel_id=1, replica_groups=mesh['rows'=16,'protos'=32] {'rows'}, dimensions={0} | all-to-all | bytes 262144 | tf_op jit(solution)/shard_map/all_to_all | solution.py:269
  69.1 13.7 %all_to_all.38.sums_ref = f32[32,1,1024]{2,1,0:T(1,128)S(1)} all-to-all(f32[32,1,1024]{2,1,0:T(1,128)S(1)} %get-tuple-element.22), channel_id=1, replica_groups=mesh['rows'=16,'protos'=32] {'protos'}, dimensions={0} | all-to-all | bytes 262144 | tf_op jit(solution)/shard_map/all_to_all | solution.py:269
  83.7 13.4 %all_to_all.39.sums_ref = f32[16,1,2048]{2,1,0:T(1,128)S(1)} all-to-all(f32[16,1,2048]{2,1,0:T(1,128)S(1)} %shard_map.72), channel_id=1, replica_groups=mesh['rows'=16,'protos'=32] {'rows'}, dimensions={0} | all-to-all | bytes 262144 | tf_op jit(solution)/shard_map/all_to_all | solution.py:269
  98.1 12.7 %all_to_all.40.sums_ref = f32[32,1,1024]{2,1,0:T(1,128)S(1)} all-to-all(f32[32,1,1024]{2,1,0:T(1,128)S(1)} %get-tuple-element.23), channel_id=1, replica_groups=mesh['rows'=16,'protos'=32] {'protos'}, dimensions={0} | all-to-all | bytes 262144 | tf_op jit(solution)/shard_map/all_to_all | solution.py:269
  110.8 8.4 %shard_map.74 = (f32[32,64,256]{2,1,0:T(8,128)}, f32[8,16,2048]{2,1,0:T(8,128)S(1)}, f32[8,16,2048]{2,1,0:T(8,128)S(1)}) custom-call(f32[32,1,1024]{2,1,0:T(1,128)S(1)} %all_to_all.40.sums_ref, f32[32,1,2048]{2,1,0:T(1,128)S(1)} %all_to_all.36.sums_ref.student_ref, f32[1,2048]{1,0:T(1,128)S(1)} %get-tuple-element.24.cols_ref, ...), custom_call_target="tpu_custom_call" | custom-call | flops 2147483648 | bytes 16777216 | tf_op jit(solution)/shard_map/pallas_call | solution.py:26
  119.3 4.8 %all-to-all-start.6 = ((f32[32,64,256]{2,1,0:T(8,128)}), f32[32,64,256]{2,1,0:T(8,128)}, u32[]{:S(2)}, u32[]{:S(2)}) async-start(f32[32,64,256]{2,1,0:T(8,128)} %get-tuple-element.31), calls=%async_computation.6 | async-start | bytes 4194304 | tf_op jit(solution)/shard_map/all_to_all | solution.py:273
  124.0 3.7 %collective-permute-start = (f32[8,16,2048]{2,1,0:T(8,128)S(1)}, f32[8,16,2048]{2,1,0:T(8,128)S(1)}, u32[]{:S(2)}, u32[]{:S(2)}) collective-permute-start(f32[8,16,2048]{2,1,0:T(8,128)S(1)} %get-tuple-element.33), channel_id=1, source_target_pairs={{0,32},{32,0},{64,96},{96,64},{128,160},{160,128},{192,224},{224,1... | collective-permute-start | bytes 3145736 | tf_op jit(solution)/shard_map/ppermute | solution.py:277
  127.8 2.3 %collective-permute-done = f32[8,16,2048]{2,1,0:T(8,128)S(1)} collective-permute-done((f32[8,16,2048]{2,1,0:T(8,128)S(1)}, f32[8,16,2048]{2,1,0:T(8,128)S(1)}, u32[]{:S(2)}, u32[]{:S(2)}) %collective-permute-start) | collective-permute-done | bytes 1048608 | tf_op jit(solution)/shard_map/ppermute | solution.py:277
  130.2 2.0 %collective-permute-start.1 = (f32[16,2048]{1,0:T(8,128)S(1)}, f32[16,2048]{1,0:T(8,128)S(1)}, u32[]{:S(2)}, u32[]{:S(2)}) collective-permute-start(f32[16,2048]{1,0:T(8,128)S(1)} %get-tuple-element.34), channel_id=1, source_target_pairs={{0,64},{32,96},{64,128},{96,160},{128,192},{160,224},{192,256},{22... | collective-permute-start | bytes 393224 | tf_op jit(solution)/shard_map/ppermute | solution.py:277
  132.2 4.5 %collective-permute-start.7 = (f32[16,2048]{1,0:T(8,128)S(1)}, f32[16,2048]{1,0:T(8,128)S(1)}, u32[]{:S(2)}, u32[]{:S(2)}) collective-permute-start(f32[16,2048]{1,0:T(8,128)S(1)} %get-tuple-element.35), channel_id=1, source_target_pairs={{0,448},{32,480},{64,0},{96,32},{128,64},{160,96},{192,128},{224,1... | collective-permute-start | bytes 393224 | tf_op jit(solution)/shard_map/ppermute | solution.py:277
  136.7 1.9 %collective-permute-start.6 = (f32[16,2048]{1,0:T(8,128)S(1)}, f32[16,2048]{1,0:T(8,128)S(1)}, u32[]{:S(2)}, u32[]{:S(2)}) collective-permute-start(f32[16,2048]{1,0:T(8,128)S(1)} %get-tuple-element.36), channel_id=1, source_target_pairs={{0,384},{32,416},{64,448},{96,480},{128,0},{160,32},{192,64},{224,... | collective-permute-start | bytes 393224 | tf_op jit(solution)/shard_map/ppermute | solution.py:277
  138.7 3.6 %collective-permute-start.5 = (f32[16,2048]{1,0:T(8,128)S(1)}, f32[16,2048]{1,0:T(8,128)S(1)}, u32[]{:S(2)}, u32[]{:S(2)}) collective-permute-start(f32[16,2048]{1,0:T(8,128)S(1)} %get-tuple-element.37), channel_id=1, source_target_pairs={{0,320},{32,352},{64,384},{96,416},{128,448},{160,480},{192,0},{22... | collective-permute-start | bytes 393224 | tf_op jit(solution)/shard_map/ppermute | solution.py:277
  142.3 5.5 %collective-permute-start.4 = (f32[16,2048]{1,0:T(8,128)S(1)}, f32[16,2048]{1,0:T(8,128)S(1)}, u32[]{:S(2)}, u32[]{:S(2)}) collective-permute-start(f32[16,2048]{1,0:T(8,128)S(1)} %get-tuple-element.38), channel_id=1, source_target_pairs={{0,256},{32,288},{64,320},{96,352},{128,384},{160,416},{192,448},{... | collective-permute-start | bytes 393224 | tf_op jit(solution)/shard_map/ppermute | solution.py:277
  147.9 2.2 %collective-permute-start.3 = (f32[16,2048]{1,0:T(8,128)S(1)}, f32[16,2048]{1,0:T(8,128)S(1)}, u32[]{:S(2)}, u32[]{:S(2)}) collective-permute-start(f32[16,2048]{1,0:T(8,128)S(1)} %get-tuple-element.39), channel_id=1, source_target_pairs={{0,192},{32,224},{64,256},{96,288},{128,320},{160,352},{192,384},{... | collective-permute-start | bytes 393224 | tf_op jit(solution)/shard_map/ppermute | solution.py:277
  150.1 3.8 %collective-permute-start.2 = (f32[16,2048]{1,0:T(8,128)S(1)}, f32[16,2048]{1,0:T(8,128)S(1)}, u32[]{:S(2)}, u32[]{:S(2)}) collective-permute-start(f32[16,2048]{1,0:T(8,128)S(1)} %get-tuple-element.40), channel_id=1, source_target_pairs={{0,128},{32,160},{64,192},{96,224},{128,256},{160,288},{192,320},{... | collective-permute-start | bytes 393224 | tf_op jit(solution)/shard_map/ppermute | solution.py:277
  153.9 1.3 collective-permute-done.4
  155.2 6.7 %collective-permute-done.3 = f32[16,2048]{1,0:T(8,128)S(1)} collective-permute-done((f32[16,2048]{1,0:T(8,128)S(1)}, f32[16,2048]{1,0:T(8,128)S(1)}, u32[]{:S(2)}, u32[]{:S(2)}) %collective-permute-start.3) | collective-permute-done | bytes 131104 | tf_op jit(solution)/shard_map/ppermute | solution.py:277
  161.8 6.0 %collective-permute-done.2 = f32[16,2048]{1,0:T(8,128)S(1)} collective-permute-done((f32[16,2048]{1,0:T(8,128)S(1)}, f32[16,2048]{1,0:T(8,128)S(1)}, u32[]{:S(2)}, u32[]{:S(2)}) %collective-permute-start.2) | collective-permute-done | bytes 131104 | tf_op jit(solution)/shard_map/ppermute | solution.py:277
  168.5 4.9 %all-to-all-done.6 = f32[32,64,256]{2,1,0:T(8,128)} async-done(((f32[32,64,256]{2,1,0:T(8,128)}), f32[32,64,256]{2,1,0:T(8,128)}, u32[]{:S(2)}, u32[]{:S(2)}) %all-to-all-start.6) | async-done | bytes 2097184 | tf_op jit(solution)/shard_map/all_to_all | solution.py:273
  173.5 2.3 %reduce_sum.9 = f32[64,256]{1,0:T(8,128)} reduce(f32[32,64,256]{2,1,0:T(8,128)} %all-to-all-done.6, f32[]{:T(128)} %constant.0.clone.1), dimensions={0}, to_apply=%region_0.0 | reduce | flops 507904 | bytes 2162692 | tf_op jit(solution)/shard_map/reduce_sum | solution.py:273
  (17 shorter events, 5.6 us)
Async XLA Ops:
  0.6 0.7 copy-start.1
  82.8 28.0 %copy-start = (bf16[256,2048]{1,0:T(8,128)(2,1)S(1)}, bf16[256,2048]{1,0:T(8,128)(2,1)}, u32[]{:S(2)}) copy-start(bf16[256,2048]{1,0:T(8,128)(2,1)} %weight_ref.1) | copy-start | bytes 3145732
  82.8 28.0 %copy-start.2 = (s32[8,128]{1,0:T(8,128)S(1)}, s32[8,128]{1,0:T(8,128)}, u32[]{:S(2)}) copy-start(s32[8,128]{1,0:T(8,128)} %mask_ref.3) | copy-start | bytes 12292
  119.3 54.2 %all-to-all-start.6 = ((f32[32,64,256]{2,1,0:T(8,128)}), f32[32,64,256]{2,1,0:T(8,128)}, u32[]{:S(2)}, u32[]{:S(2)}) async-start(f32[32,64,256]{2,1,0:T(8,128)} %get-tuple-element.31), calls=%async_computation.6 | async-start | bytes 4194304 | tf_op jit(solution)/shard_map/all_to_all | solution.py:273
  124.0 6.0 %collective-permute-start = (f32[8,16,2048]{2,1,0:T(8,128)S(1)}, f32[8,16,2048]{2,1,0:T(8,128)S(1)}, u32[]{:S(2)}, u32[]{:S(2)}) collective-permute-start(f32[8,16,2048]{2,1,0:T(8,128)S(1)} %get-tuple-element.33), channel_id=1, source_target_pairs={{0,32},{32,0},{64,96},{96,64},{128,160},{160,128},{192,224},{224,1... | collective-permute-start | bytes 3145736 | tf_op jit(solution)/shard_map/ppermute | solution.py:277
  130.2 17.6 %collective-permute-start.1 = (f32[16,2048]{1,0:T(8,128)S(1)}, f32[16,2048]{1,0:T(8,128)S(1)}, u32[]{:S(2)}, u32[]{:S(2)}) collective-permute-start(f32[16,2048]{1,0:T(8,128)S(1)} %get-tuple-element.34), channel_id=1, source_target_pairs={{0,64},{32,96},{64,128},{96,160},{128,192},{160,224},{192,256},{22... | collective-permute-start | bytes 393224 | tf_op jit(solution)/shard_map/ppermute | solution.py:277
  132.2 17.9 %collective-permute-start.7 = (f32[16,2048]{1,0:T(8,128)S(1)}, f32[16,2048]{1,0:T(8,128)S(1)}, u32[]{:S(2)}, u32[]{:S(2)}) collective-permute-start(f32[16,2048]{1,0:T(8,128)S(1)} %get-tuple-element.35), channel_id=1, source_target_pairs={{0,448},{32,480},{64,0},{96,32},{128,64},{160,96},{192,128},{224,1... | collective-permute-start | bytes 393224 | tf_op jit(solution)/shard_map/ppermute | solution.py:277
  136.7 17.1 %collective-permute-start.6 = (f32[16,2048]{1,0:T(8,128)S(1)}, f32[16,2048]{1,0:T(8,128)S(1)}, u32[]{:S(2)}, u32[]{:S(2)}) collective-permute-start(f32[16,2048]{1,0:T(8,128)S(1)} %get-tuple-element.36), channel_id=1, source_target_pairs={{0,384},{32,416},{64,448},{96,480},{128,0},{160,32},{192,64},{224,... | collective-permute-start | bytes 393224 | tf_op jit(solution)/shard_map/ppermute | solution.py:277
  138.7 15.2 %collective-permute-start.5 = (f32[16,2048]{1,0:T(8,128)S(1)}, f32[16,2048]{1,0:T(8,128)S(1)}, u32[]{:S(2)}, u32[]{:S(2)}) collective-permute-start(f32[16,2048]{1,0:T(8,128)S(1)} %get-tuple-element.37), channel_id=1, source_target_pairs={{0,320},{32,352},{64,384},{96,416},{128,448},{160,480},{192,0},{22... | collective-permute-start | bytes 393224 | tf_op jit(solution)/shard_map/ppermute | solution.py:277
  142.3 12.8 %collective-permute-start.4 = (f32[16,2048]{1,0:T(8,128)S(1)}, f32[16,2048]{1,0:T(8,128)S(1)}, u32[]{:S(2)}, u32[]{:S(2)}) collective-permute-start(f32[16,2048]{1,0:T(8,128)S(1)} %get-tuple-element.38), channel_id=1, source_target_pairs={{0,256},{32,288},{64,320},{96,352},{128,384},{160,416},{192,448},{... | collective-permute-start | bytes 393224 | tf_op jit(solution)/shard_map/ppermute | solution.py:277
  147.9 13.9 %collective-permute-start.3 = (f32[16,2048]{1,0:T(8,128)S(1)}, f32[16,2048]{1,0:T(8,128)S(1)}, u32[]{:S(2)}, u32[]{:S(2)}) collective-permute-start(f32[16,2048]{1,0:T(8,128)S(1)} %get-tuple-element.39), channel_id=1, source_target_pairs={{0,192},{32,224},{64,256},{96,288},{128,320},{160,352},{192,384},{... | collective-permute-start | bytes 393224 | tf_op jit(solution)/shard_map/ppermute | solution.py:277
  150.1 17.7 %collective-permute-start.2 = (f32[16,2048]{1,0:T(8,128)S(1)}, f32[16,2048]{1,0:T(8,128)S(1)}, u32[]{:S(2)}, u32[]{:S(2)}) collective-permute-start(f32[16,2048]{1,0:T(8,128)S(1)} %get-tuple-element.40), channel_id=1, source_target_pairs={{0,128},{32,160},{64,192},{96,224},{128,256},{160,288},{192,320},{... | collective-permute-start | bytes 393224 | tf_op jit(solution)/shard_map/ppermute | solution.py:277

commit v4 on v3

--- a/solution.py
+++ b/solution.py
@@ -34,22 +34,23 @@
     )(*held, *ins[hbm:])
 
 
-def selector(mask_ref, image, patches):
-    wanted = mask_ref[pl.ds(image, 1), :]
-    masked = wanted.shape[1]
-    return lax.broadcasted_iota(jnp.int32, (patches, masked), 0) == wanted
-
-
-def pick(patches_ref, mask_ref, image):
+def pick(patches_ref, positions, image):
     patches = patches_ref.shape[1]
-    chosen = selector(mask_ref, image, patches).astype(bf16)
-    return lax.dot_general(
-        chosen, patches_ref[image], (((0,), (0,)), ((), ())), preferred_element_type=f32
-    )
+    masked = positions.shape[0]
+    column = lax.broadcasted_iota(jnp.int32, (masked, patches), 1).astype(f32)
+    chosen = (column == positions[:, image : image + 1]).astype(bf16)
+    return jnp.dot(chosen, patches_ref[image], preferred_element_type=f32)
 
 
 def lanes_of_rows(parts):
-    return jnp.sum(parts.T, axis=0, keepdims=True)
+    groups = parts.shape[0] // LANES
+    lane = lax.broadcasted_iota(jnp.int32, (LANES, LANES), 1)
+    table = jnp.zeros((LANES, LANES), f32)
+    for group in range(groups):
+        column = jnp.sum(parts[group * LANES : (group + 1) * LANES], axis=1, keepdims=True)
+        table = jnp.where(lane == group, column, table)
+    table = table.T
+    return jnp.concatenate([table[group : group + 1] for group in range(groups)], axis=1)
 
 
 def fold_lanes(values):
@@ -60,10 +61,9 @@
 
 
 def rows_on_sublanes(line):
-    pieces = [
-        jnp.broadcast_to(line[:, s : s + LANES], (LANES, LANES)).T
-        for s in range(0, line.shape[1], LANES)
-    ]
+    groups = line.shape[1] // LANES
+    table = jnp.concatenate([line[:, g * LANES : (g + 1) * LANES] for g in range(groups)], axis=0).T
+    pieces = [jnp.broadcast_to(table[:, g : g + 1], (LANES, LANES)) for g in range(groups)]
     return jnp.concatenate(pieces, axis=0)
 
 
@@ -82,10 +82,10 @@
 
 
 def first_body(
-    teacher_hbm, teacher_weight_hbm, student_hbm, student_weight_hbm, mask_ref,
-    teacher_exp_ref, cols_ref, student_exp_ref, student_rows_ref, unit_ref, inverse_ref, turned_ref, back_ref,
+    teacher_hbm, teacher_weight_hbm, student_hbm, student_weight_hbm, mask_hbm,
+    teacher_exp_ref, cols_ref, student_exp_ref, student_rows_ref, unit_ref, inverse_ref, turned_ref, unit_weight_ref,
     length_ref,
-    teacher_ref, teacher_weight_ref, student_ref, student_weight_ref, teacher_bf_ref, student_bf_ref, parts_ref, sems,
+    teacher_ref, teacher_weight_ref, student_ref, student_weight_ref, mask_ref, teacher_bf_ref, student_bf_ref, parts_ref, sems,
 ):
     images, masked = mask_ref.shape
     protos = teacher_exp_ref.shape[1]
@@ -93,6 +93,7 @@
         pltpu.make_async_copy(source, target, sems.at[index])
         for index, (source, target) in enumerate(
             (
+                (mask_hbm, mask_ref),
                 (teacher_hbm, teacher_ref),
                 (teacher_weight_hbm, teacher_weight_ref),
                 (student_hbm, student_ref),
@@ -103,16 +104,14 @@
     for load in loads:
         load.start()
     loads[0].wait()
-
-    def teacher_image(image, _):
-        picked = pick(teacher_ref, mask_ref, image)
+    positions = mask_ref[...].astype(f32).T
+    loads[1].wait()
+    for image in range(images):
+        picked = pick(teacher_ref, positions, image)
         length = jnp.sqrt(jnp.sum(picked * picked, axis=1, keepdims=True) + epsilon)
-        rows = pl.ds(pl.multiple_of(image * masked, masked), masked)
+        rows = slice(image * masked, (image + 1) * masked)
         teacher_bf_ref[rows, :] = (picked * (1.0 / length)).astype(bf16)
-        return 0
-
-    lax.fori_loop(0, images, teacher_image, 0, unroll=2)
-    loads[1].wait()
+    loads[2].wait()
 
     def teacher_tile(tile, _):
         cols = pl.ds(pl.multiple_of(tile * TILE, TILE), TILE)
@@ -124,37 +123,34 @@
         cols_ref[:, :, cols] = jnp.broadcast_to(line[None], (cols_ref.shape[0], 1, TILE))
         return 0
 
-    lax.fori_loop(0, protos // TILE, teacher_tile, 0, unroll=2)
-    loads[2].wait()
-
-    def student_image(image, _):
-        picked = pick(student_ref, mask_ref, image)
-        length = jnp.sqrt(jnp.sum(picked * picked, axis=1, keepdims=True) + epsilon)
-        inverse = 1.0 / length
+    lax.fori_loop(0, protos // TILE, teacher_tile, 0, unroll=4)
+    loads[3].wait()
+
+    for image in range(images):
+        picked = pick(student_ref, positions, image)
+        inverse = 1.0 / jnp.sqrt(jnp.sum(picked * picked, axis=1, keepdims=True) + epsilon)
         unit = picked * inverse
-        rows = pl.ds(pl.multiple_of(image * masked, masked), masked)
+        rows = slice(image * masked, (image + 1) * masked)
         unit_ref[rows, :] = unit
         student_bf_ref[rows, :] = unit.astype(bf16)
         turned_ref[:, rows] = unit.T.astype(bf16)
         inverse_ref[rows, :] = jnp.broadcast_to(inverse, (masked, LANES))
-        return 0
-
-    lax.fori_loop(0, images, student_image, 0, unroll=2)
     parts_ref[...] = jnp.zeros_like(parts_ref)
-    loads[3].wait()
+    loads[4].wait()
 
     def student_tile(tile, _):
         cols = pl.ds(pl.multiple_of(tile * TILE, TILE), TILE)
         unit, length = unit_columns(student_weight_ref, cols)
         length_ref[:, cols] = length
-        back_ref[cols, :] = unit.T.astype(bf16)
-        products = jnp.dot(student_bf_ref[...], unit.astype(bf16), preferred_element_type=f32)
+        unit = unit.astype(bf16)
+        unit_weight_ref[:, cols] = unit
+        products = jnp.dot(student_bf_ref[...], unit, preferred_element_type=f32)
         exps = jnp.exp2(products * (LOG2_E / temp_student))
         student_exp_ref[:, cols] = exps
         parts_ref[...] += fold_lanes(exps)
         return 0
 
-    lax.fori_loop(0, protos // TILE, student_tile, 0, unroll=2)
+    lax.fori_loop(0, protos // TILE, student_tile, 0, unroll=4)
     student_rows_ref[...] = lanes_of_rows(parts_ref[...])
 
 
@@ -163,7 +159,7 @@
 
 
 def columns_body(sums_ref, exp_ref, *refs):
-    *student, scale_ref, rows_ref, parts_ref = refs
+    *rider, scale_ref, rows_ref, parts_ref = refs
     scale = 1.0 / (jnp.sum(sums_ref[...], axis=0) * PROTOS)
     scale_ref[...] = scale
     step = 64
@@ -178,13 +174,23 @@
 
     lax.fori_loop(0, exp_ref.shape[0] // step, block, 0, unroll=2)
     line = lanes_of_rows(parts_ref[...])
-    if student:
-        line = jnp.concatenate([line, student[0][...]], axis=1)
-    store_copies(rows_ref, line)
-
-
-def rows_body(total_rows, sums_ref, exp_ref, cols_ref, scale_ref, parts_ref):
-    line = 1.0 / (jnp.sum(sums_ref[...], axis=0)[:, : exp_ref.shape[0]] * total_rows)
+    peers, _, width = rows_ref.shape
+    rows = line.shape[1]
+    rows_ref[:, :, :rows] = jnp.broadcast_to(line[None], (peers, 1, rows))
+    if rider:
+        groups = rider[0].shape[1] // LANES
+        for group in range(groups):
+            lanes = rider[0][:, group * LANES : (group + 1) * LANES]
+            some = slice(group * peers // groups, (group + 1) * peers // groups)
+            rows_ref[some, :, rows:] = jnp.broadcast_to(lanes[None], (peers // groups, 1, LANES))
+
+
+def rows_body(total_rows, sums_ref, exp_ref, cols_ref, *refs):
+    *rider, scale_ref, parts_ref = refs
+    sums = jnp.sum(sums_ref[...], axis=0)
+    line = 1.0 / (sums[:, : exp_ref.shape[0]] * total_rows)
+    if rider:
+        rider[0][...] = sums[:, exp_ref.shape[0] :]
     scale_ref[...] = rows_on_sublanes(line)
     width = exp_ref.shape[1]
     parts_ref[...] = jnp.zeros_like(parts_ref)
@@ -213,14 +219,18 @@
 
 
 def gradient_body(
-    total_rows, shares,
-    sums_ref, student_ref, cols_ref, teacher_exp_ref, student_exp_ref, back_ref, turned_ref, unit_ref, inverse_ref,
+    total_rows,
+    sums_ref, student_ref, cols_ref, teacher_exp_ref, student_exp_ref, unit_weight_ref, turned_ref, unit_ref, inverse_ref,
     mask_ref, weight_ref, length_ref,
-    placed_ref, mine_ref, other_ref, row_ref, total_ref, sum_ref, score_ref,
+    placed_ref, mine_ref, other_ref,
+    row_ref, total_ref, sum_ref, score_ref,
 ):
     rows = teacher_exp_ref.shape[0]
     row_ref[...] = rows_on_sublanes(1.0 / (jnp.sum(sums_ref[...], axis=0) * total_rows))
-    total_ref[...] = rows_on_sublanes((1.0 / temp_student) / jnp.sum(student_ref[...], axis=0)[:, rows:])
+    groups = rows // LANES
+    step = student_ref.shape[0] // groups
+    totals = jnp.concatenate([student_ref[group * step][:, rows:] for group in range(groups)], axis=1)
+    total_ref[...] = rows_on_sublanes((1.0 / temp_student) / totals)
     levels, depth_share = mine_ref.shape[:2]
     me = lax.axis_index("rows")
     core, level = me % 2, me // 2
@@ -243,11 +253,14 @@
         return 0
 
     lax.fori_loop(0, teacher_exp_ref.shape[1] // TILE, one_tile, 0, unroll=2)
-    sum_ref[...] = jnp.dot(score_ref[...], back_ref[...], preferred_element_type=f32)
+    sum_ref[...] = lax.dot_general(
+        score_ref[...], unit_weight_ref[...], (((1,), (1,)), ((), ())), preferred_element_type=f32
+    )
     images, masked = mask_ref.shape
     width = unit_ref.shape[1]
-    patches = placed_ref.shape[0] * placed_ref.shape[1] // images
-    share = patches // shares
+    shares = placed_ref.shape[0]
+    share = placed_ref.shape[1] // images
+    patch = lax.broadcasted_iota(jnp.int32, (shares * share, masked), 0)
 
     def one_image(image, _):
         rows = pl.ds(pl.multiple_of(image * masked, masked), masked)
@@ -255,22 +268,21 @@
         total = sum_ref[rows, :]
         projection = jnp.sum(unit * total, axis=1, keepdims=True)
         pieces = three_pieces((total - unit * projection) * spread(inverse_ref[rows, :], width))
-        chosen = selector(mask_ref, image, patches).astype(bf16)
+        chosen = (patch == mask_ref[pl.ds(image, 1), :]).astype(bf16)
         placed = sum(jnp.dot(chosen, piece, preferred_element_type=f32) for piece in pieces)
-        placed_ref[:, pl.ds(pl.multiple_of(image * share, share), share), :] = placed.reshape(
-            shares, share, width
-        )
+        where = pl.ds(pl.multiple_of(image * share, share), share)
+        placed_ref[:, where, :] = placed.reshape(shares, share, width)
         return 0
 
     lax.fori_loop(0, images, one_image, 0, unroll=2)
+
+
+def total_body(parts_ref, out_ref):
+    out_ref[...] = jnp.sum(parts_ref[...], axis=0)
 
 
 def everyones(copies, axis):
     return lax.all_to_all(copies, axis, 0, 0, tiled=True)
-
-
-def share_of_sum(parts, axis):
-    return jnp.sum(lax.all_to_all(parts, axis, 0, 0, tiled=True), axis=0)
 
 
 def send_rows(values, to):
@@ -287,7 +299,7 @@
     protos = student_weight.shape[1]
     work = 2 * rows * protos * depth
 
-    teacher_exp, column_part, student_exp, student_part, unit, inverse, turned, back, length = call(
+    teacher_exp, column_part, student_exp, student_part, unit, inverse, turned, unit_weight, length = call(
         first_body,
         [
             ((rows, protos), f32),
@@ -297,7 +309,7 @@
             ((rows, depth), f32),
             ((rows, LANES), f32),
             ((depth, rows), bf16),
-            ((protos, depth), bf16),
+            ((depth, protos), bf16),
             ((1, protos), f32),
         ],
         (teacher_patches, teacher_weight, student_patches, student_weight, mask_index),
@@ -306,41 +318,46 @@
             pltpu.VMEM(teacher_weight.shape, bf16),
             pltpu.VMEM(student_patches.shape, bf16),
             pltpu.VMEM(student_weight.shape, bf16),
+            pltpu.VMEM(mask_index.shape, jnp.int32),
             pltpu.VMEM((rows, depth), bf16),
             pltpu.VMEM((rows, depth), bf16),
             pltpu.VMEM((rows, LANES), f32),
-            pltpu.SemaphoreType.DMA((4,)),
+            pltpu.SemaphoreType.DMA((5,)),
         ],
-        limit=12, hbm=4, flops=2 * work, moved=2**23,
-    )
+        limit=12, hbm=5, flops=2 * work, moved=2**23,
+    )
+    rider = student_part
     for sweep in range(SK_ITERS):
         column_sums = everyones(column_part, "rows")
-        student = (student_part,) if sweep == 0 else ()
+        riders = [rider] if sweep < 2 else []
         col_scale, row_part = call(
             columns_body,
-            [((1, protos), f32), ((proto_devices, 1, rows * (1 + len(student))), f32)],
-            (column_sums, teacher_exp, *student),
+            [((1, protos), f32), ((proto_devices, 1, rows + LANES * len(riders)), f32)],
+            (column_sums, teacher_exp, *riders),
             [pltpu.VMEM((rows, LANES), f32)],
             flops=2 * rows * protos, moved=2**23,
         )
         row_sums = everyones(row_part, "protos")
-        if sweep == 0:
+        if sweep == 1:
             student_sums = row_sums
         if sweep < SK_ITERS - 1:
-            (column_part,) = call(
+            column_part, *riding = call(
                 functools.partial(rows_body, total_rows),
-                [((row_devices, 1, protos), f32)],
+                [((row_devices, 1, protos), f32)] + [((1, LANES), f32)] * (sweep == 0),
                 (row_sums, teacher_exp),
                 [pltpu.VMEM((rows, LANES), f32), pltpu.VMEM((8, protos), f32)],
                 flops=2 * rows * protos, moved=2**23,
             )
+            if sweep == 0:
+                (rider,) = riding
     share = patches // proto_devices
     levels = row_devices // 2
     placed, mine, other = call(
-        functools.partial(gradient_body, total_rows, proto_devices),
-        [((proto_devices, images * share, depth), f32)] + [((levels, depth // row_devices, protos), f32)] * 2,
+        functools.partial(gradient_body, total_rows),
+        [((proto_devices, images * share, depth), f32)]
+        + [((levels, depth // row_devices, protos), f32)] * 2,
         (
-            row_sums, student_sums, col_scale, teacher_exp, student_exp, back, turned, unit, inverse, mask_index,
+            row_sums, student_sums, col_scale, teacher_exp, student_exp, unit_weight, turned, unit, inverse, mask_index,
             student_weight, length,
         ),
         [
@@ -351,12 +368,13 @@
         ],
         limit=12, flops=2 * work, moved=2**24,
     )
-    levels_parts = mine + send_rows(other, lambda i: i ^ 1)
-    grad_weight = levels_parts[0]
+    parts = mine + send_rows(other, lambda i: i ^ 1)
+    grad_weight = parts[0]
     for ahead in range(1, levels):
-        grad_weight = grad_weight + send_rows(levels_parts[ahead], lambda i: (i + 2 * ahead) % row_devices)
-    grad_patches = share_of_sum(placed, "protos").reshape(images, share, depth)
-    return (grad_patches, grad_weight)
+        grad_weight = grad_weight + send_rows(parts[ahead], lambda i: (i + 2 * ahead) % row_devices)
+    arrived = everyones(placed, "protos")
+    (grad_patches,) = call(total_body, [(arrived.shape[1:], f32)], (arrived,))
+    return (grad_patches.reshape(images, share, depth), grad_weight)
 
 
 def solution(mesh):

time: 177 us -> 171 us (0.966)
  Pallas kernels: 23.2 us -> 19.9 us
  other arithmetic: 3.18 us -> 0.83 us
  local copies, waits for them, and re-layouts: 0.75 us -> 3.01 us
  blocking collectives: 94.7 us -> 92.5 us
    pallas_call x7 -> x8, Pallas kernels: 23.2 us -> 19.9 us  [call(): pl.pallas_call(body, out_shape=[pltpu.VMEM(s, d) for s, d in outs], in_sp...]
    reduce_sum x1 -> x0, other arithmetic: 2.35 us -> none  [share_of_sum(): return jnp.sum(lax.all_to_all(parts, axis, 0, 0, tiled=True), axis=0)]
    unnamed x6 -> x9, local copies, waits for them, and re-layouts: 0.69 us -> 2.95 us
    all_to_all x6, blocking collectives: 94.7 us -> 92.5 us  [everyones(): return lax.all_to_all(copies, axis, 0, 0, tiled=True)]
where the time goes in v4:
time: 171 us; the launch traced here: 169 us
  blocking collectives  92.5 us (54%)
  starting transfers between devices  31.3 us (18%)
  waiting for transfers between devices  20.9 us (12%)
  Pallas kernels  19.9 us (12%)
  local copies, waits for them, and re-layouts  3.01 us (2%)
    all_to_all x6, blocking collectives, everyones(): return lax.all_to_all(copies, axis, 0, 0, tiled=True)  92.5 us
    ppermute x8, starting transfers between devices, send_rows(): lax.ppermute(values, 'rows', [(i, to(i)) for i in range(lax.axis_size('ro...  26.7 us
    pallas_call x8, Pallas kernels, call(): pl.pallas_call(body, out_shape=[pltpu.VMEM(s, d) for s, d in outs], in_sp...  19.9 us
    ppermute x8, waiting for transfers between devices, send_rows(): lax.ppermute(values, 'rows', [(i, to(i)) for i in range(lax.axis_size('ro...  16.3 us
    all_to_all x1, waiting for transfers between devices, everyones(): return lax.all_to_all(copies, axis, 0, 0, tiled=True)  4.6 us
    all_to_all x1, starting transfers between devices, everyones(): return lax.all_to_all(copies, axis, 0, 0, tiled=True)  4.55 us
  transfers between devices with their start and end apart: 9, of which 5 were waited for; matrix products, arithmetic and copies ran while one was open for 1% of the time, Pallas kernels for 0%

profile of v4, /device:TPU:1, one launch (start us, length us, event | category | flops | bytes accessed | tf_op | source)
XLA Modules:
  0.0 169.3 jit_solution(2663927133315191433)
XLA Ops:
  0.6 7.2 %shard_map.68 = (f32[1024,2048]{1,0:T(8,128)S(1)}, f32[16,1,2048]{2,1,0:T(1,128)S(1)}, f32[1024,2048]{1,0:T(8,128)S(1)}, f32[1,1024]{1,0:T(1,128)S(1)}, f32[1024...) custom-call(bf16[8,256,256]{2,1,0:T(8,128)(2,1)} %teacher_hbm.1, ...), custom_call_target="tpu_custom_call" | custom-call | flops 2147483648 | bytes 8388608 | tf_op jit(solution)/shard_map/pallas_call | solution.py:26
  7.8 20.8 %all_to_all.35.sums_ref = f32[16,1,2048]{2,1,0:T(1,128)S(1)} all-to-all(f32[16,1,2048]{2,1,0:T(1,128)S(1)} %get-tuple-element.20), channel_id=1, replica_groups=mesh['rows'=16,'protos'=32] {'rows'}, dimensions={0} | all-to-all | bytes 262144 | tf_op jit(solution)/shard_map/all_to_all | solution.py:285
  28.6 1.2 shard_map.69
  29.8 19.0 %all_to_all.36.sums_ref = f32[32,1,1152]{2,1,0:T(1,128)S(1)} all-to-all(f32[32,1,1152]{2,1,0:T(1,128)S(1)} %get-tuple-element.23), channel_id=1, replica_groups=mesh['rows'=16,'protos'=32] {'protos'}, dimensions={0} | all-to-all | bytes 294912 | tf_op jit(solution)/shard_map/all_to_all | solution.py:285
  49.8 13.3 %all_to_all.37.sums_ref = f32[16,1,2048]{2,1,0:T(1,128)S(1)} all-to-all(f32[16,1,2048]{2,1,0:T(1,128)S(1)} %get-tuple-element.24), channel_id=1, replica_groups=mesh['rows'=16,'protos'=32] {'rows'}, dimensions={0} | all-to-all | bytes 262144 | tf_op jit(solution)/shard_map/all_to_all | solution.py:285
  64.4 13.2 %all_to_all.38.sums_ref.student_ref = f32[32,1,1152]{2,1,0:T(1,128)S(1)} all-to-all(f32[32,1,1152]{2,1,0:T(1,128)S(1)} %get-tuple-element.26), channel_id=1, replica_groups=mesh['rows'=16,'protos'=32] {'protos'}, dimensions={0} | all-to-all | bytes 294912 | tf_op jit(solution)/shard_map/all_to_all | solution.py:285
  78.6 13.4 %all_to_all.39.sums_ref = f32[16,1,2048]{2,1,0:T(1,128)S(1)} all-to-all(f32[16,1,2048]{2,1,0:T(1,128)S(1)} %shard_map.72), channel_id=1, replica_groups=mesh['rows'=16,'protos'=32] {'rows'}, dimensions={0} | all-to-all | bytes 262144 | tf_op jit(solution)/shard_map/all_to_all | solution.py:285
  92.9 13.0 %all_to_all.40.sums_ref = f32[32,1,1024]{2,1,0:T(1,128)S(1)} all-to-all(f32[32,1,1024]{2,1,0:T(1,128)S(1)} %get-tuple-element.27), channel_id=1, replica_groups=mesh['rows'=16,'protos'=32] {'protos'}, dimensions={0} | all-to-all | bytes 262144 | tf_op jit(solution)/shard_map/all_to_all | solution.py:285
  105.9 7.1 %shard_map.74 = (f32[32,64,256]{2,1,0:T(8,128)S(1)}, f32[8,16,2048]{2,1,0:T(8,128)S(1)}, f32[8,16,2048]{2,1,0:T(8,128)S(1)}) custom-call(f32[32,1,1024]{2,1,0:T(1,128)S(1)} %all_to_all.40.sums_ref, f32[32,1,1152]{2,1,0:T(1,128)S(1)} %all_to_all.38.sums_ref.student_ref, f32[1,2048]{1,0:T(1,128)S(1)} %get-tuple-element.28.cols_ref, ...), custom_call_target="tpu_custom_call" | custom-call | flops 2147483648 | bytes 16777216 | tf_op jit(solution)/shard_map/pallas_call | solution.py:26
  113.0 1.3 copy-done
  115.3 4.6 %all-to-all-start.6 = ((f32[32,64,256]{2,1,0:T(8,128)}), f32[32,64,256]{2,1,0:T(8,128)S(1)}, u32[]{:S(2)}, u32[]{:S(2)}) async-start(f32[32,64,256]{2,1,0:T(8,128)} %copy-done), calls=%async_computation.6 | async-start | bytes 4194304 | tf_op jit(solution)/shard_map/all_to_all | solution.py:285
  119.9 3.2 %collective-permute-start = (f32[8,16,2048]{2,1,0:T(8,128)}, f32[8,16,2048]{2,1,0:T(8,128)S(1)}, u32[]{:S(2)}, u32[]{:S(2)}) collective-permute-start(f32[8,16,2048]{2,1,0:T(8,128)} %copy-done.3), channel_id=1, source_target_pairs={{0,32},{32,0},{64,96},{96,64},{128,160},{160,128},{192,224},{224,1... | collective-permute-start | bytes 3145736 | tf_op jit(solution)/shard_map/ppermute | solution.py:289
  123.0 2.5 %collective-permute-done = f32[8,16,2048]{2,1,0:T(8,128)S(1)} collective-permute-done((f32[8,16,2048]{2,1,0:T(8,128)}, f32[8,16,2048]{2,1,0:T(8,128)S(1)}, u32[]{:S(2)}, u32[]{:S(2)}) %collective-permute-start) | collective-permute-done | bytes 1048608 | tf_op jit(solution)/shard_map/ppermute | solution.py:289
  125.7 2.0 %collective-permute-start.1 = (f32[16,2048]{1,0:T(8,128)S(1)}, f32[16,2048]{1,0:T(8,128)S(1)}, u32[]{:S(2)}, u32[]{:S(2)}) collective-permute-start(f32[16,2048]{1,0:T(8,128)S(1)} %get-tuple-element.38), channel_id=1, source_target_pairs={{0,64},{32,96},{64,128},{96,160},{128,192},{160,224},{192,256},{22... | collective-permute-start | bytes 393224 | tf_op jit(solution)/shard_map/ppermute | solution.py:289
  127.7 4.5 %collective-permute-start.7 = (f32[16,2048]{1,0:T(8,128)S(1)}, f32[16,2048]{1,0:T(8,128)S(1)}, u32[]{:S(2)}, u32[]{:S(2)}) collective-permute-start(f32[16,2048]{1,0:T(8,128)S(1)} %get-tuple-element.39), channel_id=1, source_target_pairs={{0,448},{32,480},{64,0},{96,32},{128,64},{160,96},{192,128},{224,1... | collective-permute-start | bytes 393224 | tf_op jit(solution)/shard_map/ppermute | solution.py:289
  132.2 1.9 %collective-permute-start.6 = (f32[16,2048]{1,0:T(8,128)S(1)}, f32[16,2048]{1,0:T(8,128)S(1)}, u32[]{:S(2)}, u32[]{:S(2)}) collective-permute-start(f32[16,2048]{1,0:T(8,128)S(1)} %get-tuple-element.40), channel_id=1, source_target_pairs={{0,384},{32,416},{64,448},{96,480},{128,0},{160,32},{192,64},{224,... | collective-permute-start | bytes 393224 | tf_op jit(solution)/shard_map/ppermute | solution.py:289
  134.2 3.6 %collective-permute-start.5 = (f32[16,2048]{1,0:T(8,128)S(1)}, f32[16,2048]{1,0:T(8,128)S(1)}, u32[]{:S(2)}, u32[]{:S(2)}) collective-permute-start(f32[16,2048]{1,0:T(8,128)S(1)} %get-tuple-element.41), channel_id=1, source_target_pairs={{0,320},{32,352},{64,384},{96,416},{128,448},{160,480},{192,0},{22... | collective-permute-start | bytes 393224 | tf_op jit(solution)/shard_map/ppermute | solution.py:289
  137.8 5.5 %collective-permute-start.4 = (f32[16,2048]{1,0:T(8,128)S(1)}, f32[16,2048]{1,0:T(8,128)S(1)}, u32[]{:S(2)}, u32[]{:S(2)}) collective-permute-start(f32[16,2048]{1,0:T(8,128)S(1)} %get-tuple-element.42), channel_id=1, source_target_pairs={{0,256},{32,288},{64,320},{96,352},{128,384},{160,416},{192,448},{... | collective-permute-start | bytes 393224 | tf_op jit(solution)/shard_map/ppermute | solution.py:289
  143.4 2.2 %collective-permute-start.3 = (f32[16,2048]{1,0:T(8,128)S(1)}, f32[16,2048]{1,0:T(8,128)S(1)}, u32[]{:S(2)}, u32[]{:S(2)}) collective-permute-start(f32[16,2048]{1,0:T(8,128)S(1)} %get-tuple-element.43), channel_id=1, source_target_pairs={{0,192},{32,224},{64,256},{96,288},{128,320},{160,352},{192,384},{... | collective-permute-start | bytes 393224 | tf_op jit(solution)/shard_map/ppermute | solution.py:289
  145.6 3.8 %collective-permute-start.2 = (f32[16,2048]{1,0:T(8,128)S(1)}, f32[16,2048]{1,0:T(8,128)S(1)}, u32[]{:S(2)}, u32[]{:S(2)}) collective-permute-start(f32[16,2048]{1,0:T(8,128)S(1)} %get-tuple-element.44), channel_id=1, source_target_pairs={{0,128},{32,160},{64,192},{96,224},{128,256},{160,288},{192,320},{... | collective-permute-start | bytes 393224 | tf_op jit(solution)/shard_map/ppermute | solution.py:289
  149.4 1.3 collective-permute-done.4
  150.7 6.2 %collective-permute-done.3 = f32[16,2048]{1,0:T(8,128)S(1)} collective-permute-done((f32[16,2048]{1,0:T(8,128)S(1)}, f32[16,2048]{1,0:T(8,128)S(1)}, u32[]{:S(2)}, u32[]{:S(2)}) %collective-permute-start.3) | collective-permute-done | bytes 131104 | tf_op jit(solution)/shard_map/ppermute | solution.py:289
  156.9 6.3 %collective-permute-done.2 = f32[16,2048]{1,0:T(8,128)S(1)} collective-permute-done((f32[16,2048]{1,0:T(8,128)S(1)}, f32[16,2048]{1,0:T(8,128)S(1)}, u32[]{:S(2)}, u32[]{:S(2)}) %collective-permute-start.2) | collective-permute-done | bytes 131104 | tf_op jit(solution)/shard_map/ppermute | solution.py:289
  163.9 4.6 %all-to-all-done.6.parts_ref = f32[32,64,256]{2,1,0:T(8,128)S(1)} async-done(((f32[32,64,256]{2,1,0:T(8,128)}), f32[32,64,256]{2,1,0:T(8,128)S(1)}, u32[]{:S(2)}, u32[]{:S(2)}) %all-to-all-start.6) | async-done | bytes 2097184 | tf_op jit(solution)/shard_map/all_to_all | solution.py:285
  (20 shorter events, 6.9 us)
Async XLA Ops:
  77.5 28.4 %copy-start.1 = (bf16[256,2048]{1,0:T(8,128)(2,1)S(1)}, bf16[256,2048]{1,0:T(8,128)(2,1)}, u32[]{:S(2)}) copy-start(bf16[256,2048]{1,0:T(8,128)(2,1)} %weight_ref.1) | copy-start | bytes 3145732
  77.5 28.4 %copy-start.2 = (s32[8,128]{1,0:T(8,128)S(1)}, s32[8,128]{1,0:T(8,128)}, u32[]{:S(2)}) copy-start(s32[8,128]{1,0:T(8,128)} %mask_ref.1) | copy-start | bytes 12292
  113.0 1.3 copy-start
  114.3 1.0 copy-start.3
  115.3 53.2 %all-to-all-start.6 = ((f32[32,64,256]{2,1,0:T(8,128)}), f32[32,64,256]{2,1,0:T(8,128)S(1)}, u32[]{:S(2)}, u32[]{:S(2)}) async-start(f32[32,64,256]{2,1,0:T(8,128)} %copy-done), calls=%async_computation.6 | async-start | bytes 4194304 | tf_op jit(solution)/shard_map/all_to_all | solution.py:285
  119.9 5.7 %collective-permute-start = (f32[8,16,2048]{2,1,0:T(8,128)}, f32[8,16,2048]{2,1,0:T(8,128)S(1)}, u32[]{:S(2)}, u32[]{:S(2)}) collective-permute-start(f32[8,16,2048]{2,1,0:T(8,128)} %copy-done.3), channel_id=1, source_target_pairs={{0,32},{32,0},{64,96},{96,64},{128,160},{160,128},{192,224},{224,1... | collective-permute-start | bytes 3145736 | tf_op jit(solution)/shard_map/ppermute | solution.py:289
  125.7 17.6 %collective-permute-start.1 = (f32[16,2048]{1,0:T(8,128)S(1)}, f32[16,2048]{1,0:T(8,128)S(1)}, u32[]{:S(2)}, u32[]{:S(2)}) collective-permute-start(f32[16,2048]{1,0:T(8,128)S(1)} %get-tuple-element.38), channel_id=1, source_target_pairs={{0,64},{32,96},{64,128},{96,160},{128,192},{160,224},{192,256},{22... | collective-permute-start | bytes 393224 | tf_op jit(solution)/shard_map/ppermute | solution.py:289
  127.7 17.9 %collective-permute-start.7 = (f32[16,2048]{1,0:T(8,128)S(1)}, f32[16,2048]{1,0:T(8,128)S(1)}, u32[]{:S(2)}, u32[]{:S(2)}) collective-permute-start(f32[16,2048]{1,0:T(8,128)S(1)} %get-tuple-element.39), channel_id=1, source_target_pairs={{0,448},{32,480},{64,0},{96,32},{128,64},{160,96},{192,128},{224,1... | collective-permute-start | bytes 393224 | tf_op jit(solution)/shard_map/ppermute | solution.py:289
  132.2 17.1 %collective-permute-start.6 = (f32[16,2048]{1,0:T(8,128)S(1)}, f32[16,2048]{1,0:T(8,128)S(1)}, u32[]{:S(2)}, u32[]{:S(2)}) collective-permute-start(f32[16,2048]{1,0:T(8,128)S(1)} %get-tuple-element.40), channel_id=1, source_target_pairs={{0,384},{32,416},{64,448},{96,480},{128,0},{160,32},{192,64},{224,... | collective-permute-start | bytes 393224 | tf_op jit(solution)/shard_map/ppermute | solution.py:289
  134.2 15.2 %collective-permute-start.5 = (f32[16,2048]{1,0:T(8,128)S(1)}, f32[16,2048]{1,0:T(8,128)S(1)}, u32[]{:S(2)}, u32[]{:S(2)}) collective-permute-start(f32[16,2048]{1,0:T(8,128)S(1)} %get-tuple-element.41), channel_id=1, source_target_pairs={{0,320},{32,352},{64,384},{96,416},{128,448},{160,480},{192,0},{22... | collective-permute-start | bytes 393224 | tf_op jit(solution)/shard_map/ppermute | solution.py:289
  137.8 12.8 %collective-permute-start.4 = (f32[16,2048]{1,0:T(8,128)S(1)}, f32[16,2048]{1,0:T(8,128)S(1)}, u32[]{:S(2)}, u32[]{:S(2)}) collective-permute-start(f32[16,2048]{1,0:T(8,128)S(1)} %get-tuple-element.42), channel_id=1, source_target_pairs={{0,256},{32,288},{64,320},{96,352},{128,384},{160,416},{192,448},{... | collective-permute-start | bytes 393224 | tf_op jit(solution)/shard_map/ppermute | solution.py:289
  143.4 13.5 %collective-permute-start.3 = (f32[16,2048]{1,0:T(8,128)S(1)}, f32[16,2048]{1,0:T(8,128)S(1)}, u32[]{:S(2)}, u32[]{:S(2)}) collective-permute-start(f32[16,2048]{1,0:T(8,128)S(1)} %get-tuple-element.43), channel_id=1, source_target_pairs={{0,192},{32,224},{64,256},{96,288},{128,320},{160,352},{192,384},{... | collective-permute-start | bytes 393224 | tf_op jit(solution)/shard_map/ppermute | solution.py:289
  145.6 17.6 %collective-permute-start.2 = (f32[16,2048]{1,0:T(8,128)S(1)}, f32[16,2048]{1,0:T(8,128)S(1)}, u32[]{:S(2)}, u32[]{:S(2)}) collective-permute-start(f32[16,2048]{1,0:T(8,128)S(1)} %get-tuple-element.44), channel_id=1, source_target_pairs={{0,128},{32,160},{64,192},{96,224},{128,256},{160,288},{192,320},{... | collective-permute-start | bytes 393224 | tf_op jit(solution)/shard_map/ppermute | solution.py:289

commit v5 on v4

--- a/solution.py
+++ b/solution.py
@@ -25,9 +25,14 @@
     spaces = [pltpu.HBM] * hbm + [pltpu.VMEM] * (len(ins) - hbm)
     return pl.pallas_call(
         body,
-        out_shape=[pltpu.VMEM(s, d) for s, d in outs],
+        out_shape=[
+            (space[0] if space else pltpu.VMEM)(shape, dtype) for shape, dtype, *space in outs
+        ],
         in_specs=[pl.BlockSpec(memory_space=space) for space in spaces],
-        out_specs=[pl.BlockSpec(memory_space=pltpu.VMEM)] * len(outs),
+        out_specs=[
+            pl.BlockSpec(memory_space=pltpu.HBM if space and space[0] is pltpu.HBM else pltpu.VMEM)
+            for _, _, *space in outs
+        ],
         scratch_shapes=list(scratch),
         compiler_params=pltpu.CompilerParams(vmem_limit_bytes=limit * 2**20),
         cost_estimate=pl.CostEstimate(flops=flops, bytes_accessed=moved, transcendentals=0),
@@ -61,9 +66,10 @@
 
 
 def rows_on_sublanes(line):
-    groups = line.shape[1] // LANES
-    table = jnp.concatenate([line[:, g * LANES : (g + 1) * LANES] for g in range(groups)], axis=0).T
-    pieces = [jnp.broadcast_to(table[:, g : g + 1], (LANES, LANES)) for g in range(groups)]
+    pieces = [
+        jnp.broadcast_to(line[:, s : s + LANES], (LANES, LANES)).T
+        for s in range(0, line.shape[1], LANES)
+    ]
     return jnp.concatenate(pieces, axis=0)
 
 
@@ -218,12 +224,11 @@
     return high, middle, (rest - middle.astype(f32)).astype(bf16)
 
 
-def gradient_body(
+def feature_body(
     total_rows,
-    sums_ref, student_ref, cols_ref, teacher_exp_ref, student_exp_ref, unit_weight_ref, turned_ref, unit_ref, inverse_ref,
-    mask_ref, weight_ref, length_ref,
-    placed_ref, mine_ref, other_ref,
-    row_ref, total_ref, sum_ref, score_ref,
+    sums_ref, student_ref, cols_ref, teacher_exp_ref, student_exp_ref, unit_weight_ref, unit_ref, inverse_ref,
+    mask_ref,
+    placed_ref, score_hbm, row_ref, total_ref, sum_ref, score_ref, sem,
 ):
     rows = teacher_exp_ref.shape[0]
     row_ref[...] = rows_on_sublanes(1.0 / (jnp.sum(sums_ref[...], axis=0) * total_rows))
@@ -231,28 +236,18 @@
     step = student_ref.shape[0] // groups
     totals = jnp.concatenate([student_ref[group * step][:, rows:] for group in range(groups)], axis=1)
     total_ref[...] = rows_on_sublanes((1.0 / temp_student) / totals)
-    levels, depth_share = mine_ref.shape[:2]
-    me = lax.axis_index("rows")
-    core, level = me % 2, me // 2
 
     def one_tile(tile, _):
         cols = pl.ds(pl.multiple_of(tile * TILE, TILE), TILE)
         target = teacher_exp_ref[:, cols] * spread(row_ref[...], TILE)
         target = target * (cols_ref[:, cols] * (total_rows / temp_student))
         score = (student_exp_ref[:, cols] * spread(total_ref[...], TILE) - target).astype(bf16)
-        total = jnp.dot(turned_ref[...], score, preferred_element_type=f32)
-        inverse = 1.0 / length_ref[:, cols]
-        unit = weight_ref[:, cols].astype(f32) * inverse
-        dots = jnp.sum(unit * total, axis=0, keepdims=True)
-        gradient = ((total - unit * dots) * inverse).reshape(levels, 2, depth_share, TILE)
-        for z in range(levels):
-            place = pl.ds((z + levels - level) % levels, 1)
-            mine_ref[place, :, cols] = jnp.where(core == 0, gradient[z, 0], gradient[z, 1])[None]
-            other_ref[place, :, cols] = jnp.where(core == 0, gradient[z, 1], gradient[z, 0])[None]
         score_ref[:, cols] = score
         return 0
 
     lax.fori_loop(0, teacher_exp_ref.shape[1] // TILE, one_tile, 0, unroll=2)
+    store = pltpu.make_async_copy(score_ref, score_hbm, sem)
+    store.start()
     sum_ref[...] = lax.dot_general(
         score_ref[...], unit_weight_ref[...], (((1,), (1,)), ((), ())), preferred_element_type=f32
     )
@@ -275,10 +270,58 @@
         return 0
 
     lax.fori_loop(0, images, one_image, 0, unroll=2)
-
-
-def total_body(parts_ref, out_ref):
-    out_ref[...] = jnp.sum(parts_ref[...], axis=0)
+    store.wait()
+
+
+def weight_body(
+    score_hbm, weight_hbm, turned_ref, length_ref, mine_ref, other_ref, score_ref, weight_ref, sems
+):
+    levels, share = mine_ref.shape[:2]
+    me = lax.axis_index("rows")
+    core, level = me % 2, me // 2
+    tiles = weight_ref.shape[1] // TILE
+    weight_load = pltpu.make_async_copy(weight_hbm, weight_ref, sems.at[tiles])
+    weight_load.start()
+    loads = [
+        pltpu.make_async_copy(
+            score_hbm.at[:, pl.ds(tile * TILE, TILE)], score_ref.at[:, pl.ds(tile * TILE, TILE)], sems.at[tile]
+        )
+        for tile in range(tiles)
+    ]
+    for load in loads:
+        load.start()
+    weight_load.wait()
+    for tile in range(tiles):
+        cols = slice(tile * TILE, (tile + 1) * TILE)
+        loads[tile].wait()
+        total = jnp.dot(turned_ref[...], score_ref[:, cols], preferred_element_type=f32)
+        inverse = 1.0 / length_ref[:, cols]
+        unit = weight_ref[:, cols].astype(f32) * inverse
+        dots = jnp.sum(unit * total, axis=0, keepdims=True)
+        gradient = ((total - unit * dots) * inverse).reshape(levels, 2, share, TILE)
+        for z in range(levels):
+            place = pl.ds((z + levels - level) % levels, 1)
+            mine_ref[place, :, cols] = jnp.where(core == 0, gradient[z, 0], gradient[z, 1])[None]
+            other_ref[place, :, cols] = jnp.where(core == 0, gradient[z, 1], gradient[z, 0])[None]
+
+
+def total_body(parts_hbm, out_ref, parts_ref, sems):
+    pieces = sems.shape[0]
+    size = parts_ref.shape[0] // pieces
+    loads = [
+        pltpu.make_async_copy(
+            parts_hbm.at[pl.ds(piece * size, size)], parts_ref.at[pl.ds(piece * size, size)], sems.at[piece]
+        )
+        for piece in range(pieces)
+    ]
+    for load in loads:
+        load.start()
+    total = None
+    for piece in range(pieces):
+        loads[piece].wait()
+        part = jnp.sum(parts_ref[piece * size : (piece + 1) * size], axis=0)
+        total = part if total is None else total + part
+    out_ref[...] = total
 
 
 def everyones(copies, axis):
@@ -287,6 +330,25 @@
 
 def send_rows(values, to):
     return lax.ppermute(values, "rows", [(i, to(i)) for i in range(lax.axis_size("rows"))])
+
+
+def ring_share(parts, levels):
+    def along(values, by):
+        return send_rows(values, lambda i: (i + 2 * by) % (2 * levels))
+
+    last = levels // 2
+    total = parts[0]
+    if levels > 1:
+        up = parts[last]
+        for k in range(last - 1, 0, -1):
+            up = along(up, 1) + parts[k]
+        total = total + along(up, 1)
+    if levels > 2:
+        down = parts[last + 1]
+        for k in range(last + 2, levels):
+            down = along(down, -1) + parts[k]
+        total = total + along(down, -1)
+    return total
 
 
 def local(student_patches, teacher_patches, mask_index, student_weight, teacher_weight):
@@ -352,28 +414,39 @@
                 (rider,) = riding
     share = patches // proto_devices
     levels = row_devices // 2
-    placed, mine, other = call(
-        functools.partial(gradient_body, total_rows),
-        [((proto_devices, images * share, depth), f32)]
-        + [((levels, depth // row_devices, protos), f32)] * 2,
-        (
-            row_sums, student_sums, col_scale, teacher_exp, student_exp, unit_weight, turned, unit, inverse, mask_index,
-            student_weight, length,
-        ),
+    placed, score = call(
+        functools.partial(feature_body, total_rows),
+        [((proto_devices, images * share, depth), f32), ((rows, protos), bf16, pltpu.HBM)],
+        (row_sums, student_sums, col_scale, teacher_exp, student_exp, unit_weight, unit, inverse, mask_index),
         [
             pltpu.VMEM((rows, LANES), f32),
             pltpu.VMEM((rows, LANES), f32),
             pltpu.VMEM((rows, depth), f32),
             pltpu.VMEM((rows, protos), bf16),
-        ],
-        limit=12, flops=2 * work, moved=2**24,
-    )
-    parts = mine + send_rows(other, lambda i: i ^ 1)
-    grad_weight = parts[0]
-    for ahead in range(1, levels):
-        grad_weight = grad_weight + send_rows(parts[ahead], lambda i: (i + 2 * ahead) % row_devices)
+            pltpu.SemaphoreType.DMA,
+        ],
+        limit=12, flops=work, moved=2**24,
+    )
     arrived = everyones(placed, "protos")
-    (grad_patches,) = call(total_body, [(arrived.shape[1:], f32)], (arrived,))
+    mine, other = call(
+        weight_body,
+        [((levels, depth // row_devices, protos), f32)] * 2,
+        (score, student_weight, turned, length),
+        [
+            pltpu.VMEM((rows, protos), bf16),
+            pltpu.VMEM(student_weight.shape, bf16),
+            pltpu.SemaphoreType.DMA((protos // TILE + 1,)),
+        ],
+        limit=12, hbm=2,
+    )
+    grad_weight = ring_share(mine + send_rows(other, lambda i: i ^ 1), levels)
+    (grad_patches,) = call(
+        total_body,
+        [(arrived.shape[1:], f32, jax.ShapeDtypeStruct)],
+        (arrived,),
+        [pltpu.VMEM(arrived.shape, f32), pltpu.SemaphoreType.DMA((4 if proto_devices % 4 == 0 else 1,))],
+        hbm=1,
+    )
     return (grad_patches.reshape(images, share, depth), grad_weight)
 
 

time: 171 us -> 171 us (level)
  Pallas kernels: 19.9 us -> 26.9 us
  waiting for transfers between devices: 20.9 us -> 16.9 us
    pallas_call x8 -> x9, Pallas kernels: 19.9 us -> 26.9 us  [call(): pl.pallas_call(body, out_shape=[(space[0] if space else pltpu.VMEM)(shape...]
    ppermute x8, waiting for transfers between devices: 16.3 us -> 12.7 us  [send_rows(): lax.ppermute(values, 'rows', [(i, to(i)) for i in range(lax.axis_size('ro...]
  transfers between devices with their start and end apart: 9 -> 9, of which waited for: 5 -> 8; matrix products, arithmetic and copies ran while one was open for 1% -> 1% of each run, Pallas kernels for 0% -> 3%
where the time goes in v5:
time: 171 us; the launch traced here: 170 us
  blocking collectives  92.6 us (54%)
  starting transfers between devices  30 us (18%)
  Pallas kernels  26.9 us (16%)
  waiting for transfers between devices  16.9 us (10%)
    all_to_all x6, blocking collectives, everyones(): return lax.all_to_all(copies, axis, 0, 0, tiled=True)  92.6 us
    pallas_call x9, Pallas kernels, call(): pl.pallas_call(body, out_shape=[(space[0] if space else pltpu.VMEM)(shape...  26.9 us
    ppermute x8, starting transfers between devices, send_rows(): lax.ppermute(values, 'rows', [(i, to(i)) for i in range(lax.axis_size('ro...  25.3 us
    ppermute x8, waiting for transfers between devices, send_rows(): lax.ppermute(values, 'rows', [(i, to(i)) for i in range(lax.axis_size('ro...  12.7 us
    all_to_all x1, starting transfers between devices, everyones(): return lax.all_to_all(copies, axis, 0, 0, tiled=True)  4.76 us
    all_to_all x1, waiting for transfers between devices, everyones(): return lax.all_to_all(copies, axis, 0, 0, tiled=True)  4.21 us
  transfers between devices with their start and end apart: 9, of which 8 were waited for; matrix products, arithmetic and copies ran while one was open for 1% of the time, Pallas kernels for 3%

profile of v5, /device:TPU:1, one launch (start us, length us, event | category | flops | bytes accessed | tf_op | source)
XLA Modules:
  0.0 169.6 jit_solution(1722450100537834179)
XLA Ops:
  0.6 7.2 %shard_map.68 = (f32[1024,2048]{1,0:T(8,128)S(1)}, f32[16,1,2048]{2,1,0:T(1,128)S(1)}, f32[1024,2048]{1,0:T(8,128)S(1)}, f32[1,1024]{1,0:T(1,128)S(1)}, f32[1024...) custom-call(bf16[8,256,256]{2,1,0:T(8,128)(2,1)} %teacher_hbm.1, ...), custom_call_target="tpu_custom_call" | custom-call | flops 2147483648 | bytes 8388608 | tf_op jit(solution)/shard_map/pallas_call | solution.py:26
  7.8 20.8 %all_to_all.35.sums_ref = f32[16,1,2048]{2,1,0:T(1,128)S(1)} all-to-all(f32[16,1,2048]{2,1,0:T(1,128)S(1)} %get-tuple-element.21), channel_id=1, replica_groups=mesh['rows'=16,'protos'=32] {'rows'}, dimensions={0} | all-to-all | bytes 262144 | tf_op jit(solution)/shard_map/all_to_all | solution.py:328
  29.8 19.0 %all_to_all.36.sums_ref = f32[32,1,1152]{2,1,0:T(1,128)S(1)} all-to-all(f32[32,1,1152]{2,1,0:T(1,128)S(1)} %get-tuple-element.24), channel_id=1, replica_groups=mesh['rows'=16,'protos'=32] {'protos'}, dimensions={0} | all-to-all | bytes 294912 | tf_op jit(solution)/shard_map/all_to_all | solution.py:328
  49.7 13.3 %all_to_all.37.sums_ref = f32[16,1,2048]{2,1,0:T(1,128)S(1)} all-to-all(f32[16,1,2048]{2,1,0:T(1,128)S(1)} %get-tuple-element.25), channel_id=1, replica_groups=mesh['rows'=16,'protos'=32] {'rows'}, dimensions={0} | all-to-all | bytes 262144 | tf_op jit(solution)/shard_map/all_to_all | solution.py:328
  64.3 13.2 %all_to_all.38.sums_ref.student_ref = f32[32,1,1152]{2,1,0:T(1,128)S(1)} all-to-all(f32[32,1,1152]{2,1,0:T(1,128)S(1)} %get-tuple-element.27), channel_id=1, replica_groups=mesh['rows'=16,'protos'=32] {'protos'}, dimensions={0} | all-to-all | bytes 294912 | tf_op jit(solution)/shard_map/all_to_all | solution.py:328
  78.4 13.4 %all_to_all.39.sums_ref = f32[16,1,2048]{2,1,0:T(1,128)S(1)} all-to-all(f32[16,1,2048]{2,1,0:T(1,128)S(1)} %shard_map.72), channel_id=1, replica_groups=mesh['rows'=16,'protos'=32] {'rows'}, dimensions={0} | all-to-all | bytes 262144 | tf_op jit(solution)/shard_map/all_to_all | solution.py:328
  92.7 13.0 %all_to_all.40.sums_ref = f32[32,1,1024]{2,1,0:T(1,128)S(1)} all-to-all(f32[32,1,1024]{2,1,0:T(1,128)S(1)} %get-tuple-element.28), channel_id=1, replica_groups=mesh['rows'=16,'protos'=32] {'protos'}, dimensions={0} | all-to-all | bytes 262144 | tf_op jit(solution)/shard_map/all_to_all | solution.py:328
  105.7 6.9 %shard_map.74 = (f32[32,64,256]{2,1,0:T(8,128)}, bf16[1024,2048]{1,0:T(8,128)(2,1)}) custom-call(f32[32,1,1024]{2,1,0:T(1,128)S(1)} %all_to_all.40.sums_ref, f32[32,1,1152]{2,1,0:T(1,128)S(1)} %all_to_all.38.sums_ref.student_ref, f32[1,2048]{1,0:T(1,128)S(1)} %get-tuple-element.29.cols_ref, f32[1024,2048]{1,0:T(8,128)S(1)} %get-tuple-element.22.exp_ref.teacher_exp_ref, ...), custom_call_target="tpu_custom_call" | custom-call | flops 1073741824 | bytes 16777216 | tf_op jit(solution)/shard_map/pallas_call | solution.py:26
  112.6 4.8 %all-to-all-start.6 = ((f32[32,64,256]{2,1,0:T(8,128)}), f32[32,64,256]{2,1,0:T(8,128)S(1)}, u32[]{:S(2)}, u32[]{:S(2)}) async-start(f32[32,64,256]{2,1,0:T(8,128)} %get-tuple-element.34), calls=%async_computation.6 | async-start | bytes 4194304 | tf_op jit(solution)/shard_map/all_to_all | solution.py:328
  117.4 5.2 %shard_map.76 = (f32[8,16,2048]{2,1,0:T(8,128)S(1)}, f32[8,16,2048]{2,1,0:T(8,128)S(1)}) custom-call(bf16[1024,2048]{1,0:T(8,128)(2,1)} %get-tuple-element.35.score_hbm, bf16[256,2048]{1,0:T(8,128)(2,1)} %weight_hbm.1, bf16[256,1024]{1,0:T(8,128)(2,1)S(1)} %get-tuple-element.36.turned_ref, f32[1,2048]{1,0:T(1,128)S(1)} %get-tuple-element.37.length_ref), custom_call_target="tpu_custom_call" | custom-call | tf_op jit(solution)/shard_map/pallas_call | solution.py:26
  122.7 3.2 %collective-permute-start = (f32[8,16,2048]{2,1,0:T(8,128)S(1)}, f32[8,16,2048]{2,1,0:T(8,128)S(1)}, u32[]{:S(2)}, u32[]{:S(2)}) collective-permute-start(f32[8,16,2048]{2,1,0:T(8,128)S(1)} %get-tuple-element.39), channel_id=1, source_target_pairs={{0,32},{32,0},{64,96},{96,64},{128,160},{160,128},{192,224},{224,1... | collective-permute-start | bytes 3145736 | tf_op jit(solution)/shard_map/ppermute | solution.py:332
  125.8 2.3 %collective-permute-done = f32[8,16,2048]{2,1,0:T(8,128)S(1)} collective-permute-done((f32[8,16,2048]{2,1,0:T(8,128)S(1)}, f32[8,16,2048]{2,1,0:T(8,128)S(1)}, u32[]{:S(2)}, u32[]{:S(2)}) %collective-permute-start) | collective-permute-done | bytes 1048608 | tf_op jit(solution)/shard_map/ppermute | solution.py:332
  128.3 2.0 %collective-permute-start.1 = (f32[16,2048]{1,0:T(8,128)S(1)}, f32[16,2048]{1,0:T(8,128)S(1)}, u32[]{:S(2)}, u32[]{:S(2)}) collective-permute-start(f32[16,2048]{1,0:T(8,128)S(1)} %get-tuple-element.44), channel_id=1, source_target_pairs={{0,64},{32,96},{64,128},{96,160},{128,192},{160,224},{192,256},{22... | collective-permute-start | bytes 393224 | tf_op jit(solution)/shard_map/ppermute | solution.py:332
  130.2 4.5 %collective-permute-start.5 = (f32[16,2048]{1,0:T(8,128)S(1)}, f32[16,2048]{1,0:T(8,128)S(1)}, u32[]{:S(2)}, u32[]{:S(2)}) collective-permute-start(f32[16,2048]{1,0:T(8,128)S(1)} %get-tuple-element.45), channel_id=1, source_target_pairs={{0,448},{32,480},{64,0},{96,32},{128,64},{160,96},{192,128},{224,1... | collective-permute-start | bytes 393224 | tf_op jit(solution)/shard_map/ppermute | solution.py:332
  134.8 1.3 collective-permute-done.1
  136.1 1.9 %collective-permute-start.2 = (f32[16,2048]{1,0:T(8,128)S(1)}, f32[16,2048]{1,0:T(8,128)S(1)}, u32[]{:S(2)}, u32[]{:S(2)}) collective-permute-start(f32[16,2048]{1,0:T(8,128)S(1)} %fusion.4), channel_id=1, source_target_pairs={{0,64},{32,96},{64,128},{96,160},{128,192},{160,224},{192,256},{22... | collective-permute-start | bytes 393224 | tf_op jit(solution)/shard_map/ppermute | solution.py:332
  138.0 5.3 %collective-permute-done.2 = f32[16,2048]{1,0:T(8,128)S(1)} collective-permute-done((f32[16,2048]{1,0:T(8,128)S(1)}, f32[16,2048]{1,0:T(8,128)S(1)}, u32[]{:S(2)}, u32[]{:S(2)}) %collective-permute-start.2) | collective-permute-done | bytes 131104 | tf_op jit(solution)/shard_map/ppermute | solution.py:332
  143.4 1.9 %collective-permute-start.3 = (f32[16,2048]{1,0:T(8,128)S(1)}, f32[16,2048]{1,0:T(8,128)S(1)}, u32[]{:S(2)}, u32[]{:S(2)}) collective-permute-start(f32[16,2048]{1,0:T(8,128)S(1)} %get-tuple-element.42), channel_id=1, source_target_pairs={{0,64},{32,96},{64,128},{96,160},{128,192},{160,224},{192,256},{22... | collective-permute-start | bytes 393224 | tf_op jit(solution)/shard_map/ppermute | solution.py:332
  145.3 4.6 %collective-permute-start.6 = (f32[16,2048]{1,0:T(8,128)S(1)}, f32[16,2048]{1,0:T(8,128)S(1)}, u32[]{:S(2)}, u32[]{:S(2)}) collective-permute-start(f32[16,2048]{1,0:T(8,128)S(1)} %get-tuple-element.43), channel_id=1, source_target_pairs={{0,448},{32,480},{64,0},{96,32},{128,64},{160,96},{192,128},{224,1... | collective-permute-start | bytes 393224 | tf_op jit(solution)/shard_map/ppermute | solution.py:332
  151.8 1.9 %collective-permute-start.4 = (f32[16,2048]{1,0:T(8,128)S(1)}, f32[16,2048]{1,0:T(8,128)S(1)}, u32[]{:S(2)}, u32[]{:S(2)}) collective-permute-start(f32[16,2048]{1,0:T(8,128)S(1)} %get-tuple-element.40), channel_id=1, source_target_pairs={{0,64},{32,96},{64,128},{96,160},{128,192},{160,224},{192,256},{22... | collective-permute-start | bytes 393224 | tf_op jit(solution)/shard_map/ppermute | solution.py:332
  153.8 5.3 %collective-permute-start.7 = (f32[16,2048]{1,0:T(8,128)S(1)}, f32[16,2048]{1,0:T(8,128)S(1)}, u32[]{:S(2)}, u32[]{:S(2)}) collective-permute-start(f32[16,2048]{1,0:T(8,128)S(1)} %get-tuple-element.41), channel_id=1, source_target_pairs={{0,448},{32,480},{64,0},{96,32},{128,64},{160,96},{192,128},{224,1... | collective-permute-start | bytes 393224 | tf_op jit(solution)/shard_map/ppermute | solution.py:332
  161.7 4.2 %all-to-all-done.6.parts_hbm = f32[32,64,256]{2,1,0:T(8,128)S(1)} async-done(((f32[32,64,256]{2,1,0:T(8,128)}), f32[32,64,256]{2,1,0:T(8,128)S(1)}, u32[]{:S(2)}, u32[]{:S(2)}) %all-to-all-start.6) | async-done | bytes 2097184 | tf_op jit(solution)/shard_map/all_to_all | solution.py:328
  165.9 1.3 copy-done.1
  167.2 2.2 %shard_map.75 = f32[64,256]{1,0:T(8,128)} custom-call(f32[32,64,256]{2,1,0:T(8,128)} %copy-done.1), custom_call_target="tpu_custom_call" | custom-call | tf_op jit(solution)/shard_map/pallas_call | solution.py:26
  (19 shorter events, 10.1 us)
Async XLA Ops:
  91.7 14.0 %copy-start = (s32[8,128]{1,0:T(8,128)S(1)}, s32[8,128]{1,0:T(8,128)}, u32[]{:S(2)}) copy-start(s32[8,128]{1,0:T(8,128)} %mask_ref.1) | copy-start | bytes 12292
  112.6 53.2 %all-to-all-start.6 = ((f32[32,64,256]{2,1,0:T(8,128)}), f32[32,64,256]{2,1,0:T(8,128)S(1)}, u32[]{:S(2)}, u32[]{:S(2)}) async-start(f32[32,64,256]{2,1,0:T(8,128)} %get-tuple-element.34), calls=%async_computation.6 | async-start | bytes 4194304 | tf_op jit(solution)/shard_map/all_to_all | solution.py:328
  122.7 5.4 %collective-permute-start = (f32[8,16,2048]{2,1,0:T(8,128)S(1)}, f32[8,16,2048]{2,1,0:T(8,128)S(1)}, u32[]{:S(2)}, u32[]{:S(2)}) collective-permute-start(f32[8,16,2048]{2,1,0:T(8,128)S(1)} %get-tuple-element.39), channel_id=1, source_target_pairs={{0,32},{32,0},{64,96},{96,64},{128,160},{160,128},{192,224},{224,1... | collective-permute-start | bytes 3145736 | tf_op jit(solution)/shard_map/ppermute | solution.py:332
  128.3 7.8 %collective-permute-start.1 = (f32[16,2048]{1,0:T(8,128)S(1)}, f32[16,2048]{1,0:T(8,128)S(1)}, u32[]{:S(2)}, u32[]{:S(2)}) collective-permute-start(f32[16,2048]{1,0:T(8,128)S(1)} %get-tuple-element.44), channel_id=1, source_target_pairs={{0,64},{32,96},{64,128},{96,160},{128,192},{160,224},{192,256},{22... | collective-permute-start | bytes 393224 | tf_op jit(solution)/shard_map/ppermute | solution.py:332
  130.2 7.8 %collective-permute-start.5 = (f32[16,2048]{1,0:T(8,128)S(1)}, f32[16,2048]{1,0:T(8,128)S(1)}, u32[]{:S(2)}, u32[]{:S(2)}) collective-permute-start(f32[16,2048]{1,0:T(8,128)S(1)} %get-tuple-element.45), channel_id=1, source_target_pairs={{0,448},{32,480},{64,0},{96,32},{128,64},{160,96},{192,128},{224,1... | collective-permute-start | bytes 393224 | tf_op jit(solution)/shard_map/ppermute | solution.py:332
  136.1 7.2 %collective-permute-start.2 = (f32[16,2048]{1,0:T(8,128)S(1)}, f32[16,2048]{1,0:T(8,128)S(1)}, u32[]{:S(2)}, u32[]{:S(2)}) collective-permute-start(f32[16,2048]{1,0:T(8,128)S(1)} %fusion.4), channel_id=1, source_target_pairs={{0,64},{32,96},{64,128},{96,160},{128,192},{160,224},{192,256},{22... | collective-permute-start | bytes 393224 | tf_op jit(solution)/shard_map/ppermute | solution.py:332
  143.4 7.2 %collective-permute-start.3 = (f32[16,2048]{1,0:T(8,128)S(1)}, f32[16,2048]{1,0:T(8,128)S(1)}, u32[]{:S(2)}, u32[]{:S(2)}) collective-permute-start(f32[16,2048]{1,0:T(8,128)S(1)} %get-tuple-element.42), channel_id=1, source_target_pairs={{0,64},{32,96},{64,128},{96,160},{128,192},{160,224},{192,256},{22... | collective-permute-start | bytes 393224 | tf_op jit(solution)/shard_map/ppermute | solution.py:332
  145.3 6.5 %collective-permute-start.6 = (f32[16,2048]{1,0:T(8,128)S(1)}, f32[16,2048]{1,0:T(8,128)S(1)}, u32[]{:S(2)}, u32[]{:S(2)}) collective-permute-start(f32[16,2048]{1,0:T(8,128)S(1)} %get-tuple-element.43), channel_id=1, source_target_pairs={{0,448},{32,480},{64,0},{96,32},{128,64},{160,96},{192,128},{224,1... | collective-permute-start | bytes 393224 | tf_op jit(solution)/shard_map/ppermute | solution.py:332
  151.8 7.9 %collective-permute-start.4 = (f32[16,2048]{1,0:T(8,128)S(1)}, f32[16,2048]{1,0:T(8,128)S(1)}, u32[]{:S(2)}, u32[]{:S(2)}) collective-permute-start(f32[16,2048]{1,0:T(8,128)S(1)} %get-tuple-element.40), channel_id=1, source_target_pairs={{0,64},{32,96},{64,128},{96,160},{128,192},{160,224},{192,256},{22... | collective-permute-start | bytes 393224 | tf_op jit(solution)/shard_map/ppermute | solution.py:332
  153.8 7.2 %collective-permute-start.7 = (f32[16,2048]{1,0:T(8,128)S(1)}, f32[16,2048]{1,0:T(8,128)S(1)}, u32[]{:S(2)}, u32[]{:S(2)}) collective-permute-start(f32[16,2048]{1,0:T(8,128)S(1)} %get-tuple-element.41), channel_id=1, source_target_pairs={{0,448},{32,480},{64,0},{96,32},{128,64},{160,96},{192,128},{224,1... | collective-permute-start | bytes 393224 | tf_op jit(solution)/shard_map/ppermute | solution.py:332
  165.9 1.3 copy-start.1

commit v6 on v5

--- a/solution.py
+++ b/solution.py
@@ -217,13 +217,6 @@
     store_copies(cols_ref, jnp.sum(parts_ref[...], axis=0, keepdims=True))
 
 
-def three_pieces(values):
-    high = values.astype(bf16)
-    rest = values - high.astype(f32)
-    middle = rest.astype(bf16)
-    return high, middle, (rest - middle.astype(f32)).astype(bf16)
-
-
 def feature_body(
     total_rows,
     sums_ref, student_ref, cols_ref, teacher_exp_ref, student_exp_ref, unit_weight_ref, unit_ref, inverse_ref,
@@ -255,21 +248,24 @@
     width = unit_ref.shape[1]
     shares = placed_ref.shape[0]
     share = placed_ref.shape[1] // images
-    patch = lax.broadcasted_iota(jnp.int32, (shares * share, masked), 0)
+    patch = lax.broadcasted_iota(jnp.int32, (shares * share, 2 * masked), 0)
 
     def one_image(image, _):
         rows = pl.ds(pl.multiple_of(image * masked, masked), masked)
         unit = unit_ref[rows, :]
         total = sum_ref[rows, :]
         projection = jnp.sum(unit * total, axis=1, keepdims=True)
-        pieces = three_pieces((total - unit * projection) * spread(inverse_ref[rows, :], width))
-        chosen = (patch == mask_ref[pl.ds(image, 1), :]).astype(bf16)
-        placed = sum(jnp.dot(chosen, piece, preferred_element_type=f32) for piece in pieces)
+        gradient = (total - unit * projection) * spread(inverse_ref[rows, :], width)
+        high = gradient.astype(bf16)
+        low = (gradient - high.astype(f32)).astype(bf16)
+        positions = mask_ref[pl.ds(image, 1), :]
+        chosen = (patch == jnp.concatenate([positions, positions], axis=1)).astype(bf16)
+        placed = jnp.dot(chosen, jnp.concatenate([high, low], axis=0), preferred_element_type=f32)
         where = pl.ds(pl.multiple_of(image * share, share), share)
         placed_ref[:, where, :] = placed.reshape(shares, share, width)
         return 0
 
-    lax.fori_loop(0, images, one_image, 0, unroll=2)
+    lax.fori_loop(0, images, one_image, 0, unroll=4)
     store.wait()
 
 
@@ -305,23 +301,8 @@
             other_ref[place, :, cols] = jnp.where(core == 0, gradient[z, 1], gradient[z, 0])[None]
 
 
-def total_body(parts_hbm, out_ref, parts_ref, sems):
-    pieces = sems.shape[0]
-    size = parts_ref.shape[0] // pieces
-    loads = [
-        pltpu.make_async_copy(
-            parts_hbm.at[pl.ds(piece * size, size)], parts_ref.at[pl.ds(piece * size, size)], sems.at[piece]
-        )
-        for piece in range(pieces)
-    ]
-    for load in loads:
-        load.start()
-    total = None
-    for piece in range(pieces):
-        loads[piece].wait()
-        part = jnp.sum(parts_ref[piece * size : (piece + 1) * size], axis=0)
-        total = part if total is None else total + part
-    out_ref[...] = total
+def total_body(parts_ref, out_ref):
+    out_ref[...] = jnp.sum(parts_ref[...], axis=0)
 
 
 def everyones(copies, axis):
@@ -444,8 +425,6 @@
         total_body,
         [(arrived.shape[1:], f32, jax.ShapeDtypeStruct)],
         (arrived,),
-        [pltpu.VMEM(arrived.shape, f32), pltpu.SemaphoreType.DMA((4 if proto_devices % 4 == 0 else 1,))],
-        hbm=1,
     )
     return (grad_patches.reshape(images, share, depth), grad_weight)
 

time: 171 us -> 168 us (0.982)
  Pallas kernels: 26.9 us -> 23.5 us
    pallas_call x9, Pallas kernels: 26.9 us -> 23.5 us  [call(): pl.pallas_call(body, out_shape=[(space[0] if space else pltpu.VMEM)(shape...]
where the time goes in v6:
time: 168 us; the launch traced here: 166 us
  blocking collectives  92.6 us (55%)
  starting transfers between devices  30 us (18%)
  Pallas kernels  23.5 us (14%)
  waiting for transfers between devices  16.9 us (10%)
    all_to_all x6, blocking collectives, everyones(): return lax.all_to_all(copies, axis, 0, 0, tiled=True)  92.6 us
    ppermute x8, starting transfers between devices, send_rows(): lax.ppermute(values, 'rows', [(i, to(i)) for i in range(lax.axis_size('ro...  25.3 us
    pallas_call x9, Pallas kernels, call(): pl.pallas_call(body, out_shape=[(space[0] if space else pltpu.VMEM)(shape...  23.5 us
    ppermute x8, waiting for transfers between devices, send_rows(): lax.ppermute(values, 'rows', [(i, to(i)) for i in range(lax.axis_size('ro...  12.7 us
    all_to_all x1, starting transfers between devices, everyones(): return lax.all_to_all(copies, axis, 0, 0, tiled=True)  4.74 us
    all_to_all x1, waiting for transfers between devices, everyones(): return lax.all_to_all(copies, axis, 0, 0, tiled=True)  4.22 us
  transfers between devices with their start and end apart: 9, of which 8 were waited for; matrix products, arithmetic and copies ran while one was open for 1% of the time, Pallas kernels for 3%

profile of v6, /device:TPU:1, one launch (start us, length us, event | category | flops | bytes accessed | tf_op | source)
XLA Modules:
  0.0 166.1 jit_solution(18299278912575953097)
XLA Ops:
  0.6 7.2 %shard_map.68 = (f32[1024,2048]{1,0:T(8,128)S(1)}, f32[16,1,2048]{2,1,0:T(1,128)S(1)}, f32[1024,2048]{1,0:T(8,128)S(1)}, f32[1,1024]{1,0:T(1,128)S(1)}, f32[1024...) custom-call(bf16[8,256,256]{2,1,0:T(8,128)(2,1)} %teacher_hbm.1, ...), custom_call_target="tpu_custom_call" | custom-call | flops 2147483648 | bytes 8388608 | tf_op jit(solution)/shard_map/pallas_call | solution.py:26
  7.8 20.8 %all_to_all.35.sums_ref = f32[16,1,2048]{2,1,0:T(1,128)S(1)} all-to-all(f32[16,1,2048]{2,1,0:T(1,128)S(1)} %get-tuple-element.21), channel_id=1, replica_groups=mesh['rows'=16,'protos'=32] {'rows'}, dimensions={0} | all-to-all | bytes 262144 | tf_op jit(solution)/shard_map/all_to_all | solution.py:309
  29.8 19.0 %all_to_all.36.sums_ref = f32[32,1,1152]{2,1,0:T(1,128)S(1)} all-to-all(f32[32,1,1152]{2,1,0:T(1,128)S(1)} %get-tuple-element.24), channel_id=1, replica_groups=mesh['rows'=16,'protos'=32] {'protos'}, dimensions={0} | all-to-all | bytes 294912 | tf_op jit(solution)/shard_map/all_to_all | solution.py:309
  49.7 13.3 %all_to_all.37.sums_ref = f32[16,1,2048]{2,1,0:T(1,128)S(1)} all-to-all(f32[16,1,2048]{2,1,0:T(1,128)S(1)} %get-tuple-element.25), channel_id=1, replica_groups=mesh['rows'=16,'protos'=32] {'rows'}, dimensions={0} | all-to-all | bytes 262144 | tf_op jit(solution)/shard_map/all_to_all | solution.py:309
  63.0 1.3 shard_map.71
  64.3 13.2 %all_to_all.38.sums_ref.student_ref = f32[32,1,1152]{2,1,0:T(1,128)S(1)} all-to-all(f32[32,1,1152]{2,1,0:T(1,128)S(1)} %get-tuple-element.27), channel_id=1, replica_groups=mesh['rows'=16,'protos'=32] {'protos'}, dimensions={0} | all-to-all | bytes 294912 | tf_op jit(solution)/shard_map/all_to_all | solution.py:309
  78.4 13.4 %all_to_all.39.sums_ref = f32[16,1,2048]{2,1,0:T(1,128)S(1)} all-to-all(f32[16,1,2048]{2,1,0:T(1,128)S(1)} %shard_map.72), channel_id=1, replica_groups=mesh['rows'=16,'protos'=32] {'rows'}, dimensions={0} | all-to-all | bytes 262144 | tf_op jit(solution)/shard_map/all_to_all | solution.py:309
  92.7 13.0 %all_to_all.40.sums_ref = f32[32,1,1024]{2,1,0:T(1,128)S(1)} all-to-all(f32[32,1,1024]{2,1,0:T(1,128)S(1)} %get-tuple-element.28), channel_id=1, replica_groups=mesh['rows'=16,'protos'=32] {'protos'}, dimensions={0} | all-to-all | bytes 262144 | tf_op jit(solution)/shard_map/all_to_all | solution.py:309
  105.7 5.0 %shard_map.74 = (f32[32,64,256]{2,1,0:T(8,128)S(1)}, bf16[1024,2048]{1,0:T(8,128)(2,1)}) custom-call(f32[32,1,1024]{2,1,0:T(1,128)S(1)} %all_to_all.40.sums_ref, f32[32,1,1152]{2,1,0:T(1,128)S(1)} %all_to_all.38.sums_ref.student_ref, f32[1,2048]{1,0:T(1,128)S(1)} %get-tuple-element.29.cols_ref, f32[1024,2048]{1,0:T(8,128)S(1)} %get-tuple-element.22.exp_ref.teacher_exp_ref, ...), custom_call_target="tpu_custom_call" | custom-call | flops 1073741824 | bytes 16777216 | tf_op jit(solution)/shard_map/pallas_call | solution.py:26
  110.8 1.3 copy-done
  112.1 4.7 %all-to-all-start.6 = ((f32[32,64,256]{2,1,0:T(8,128)}), f32[32,64,256]{2,1,0:T(8,128)S(1)}, u32[]{:S(2)}, u32[]{:S(2)}) async-start(f32[32,64,256]{2,1,0:T(8,128)} %copy-done), calls=%async_computation.6 | async-start | bytes 4194304 | tf_op jit(solution)/shard_map/all_to_all | solution.py:309
  116.8 5.2 %shard_map.76 = (f32[8,16,2048]{2,1,0:T(8,128)S(1)}, f32[8,16,2048]{2,1,0:T(8,128)S(1)}) custom-call(bf16[1024,2048]{1,0:T(8,128)(2,1)} %get-tuple-element.35.score_hbm, bf16[256,2048]{1,0:T(8,128)(2,1)} %weight_hbm.1, bf16[256,1024]{1,0:T(8,128)(2,1)S(1)} %get-tuple-element.36.turned_ref, f32[1,2048]{1,0:T(1,128)S(1)} %get-tuple-element.37.length_ref), custom_call_target="tpu_custom_call" | custom-call | tf_op jit(solution)/shard_map/pallas_call | solution.py:26
  122.1 3.2 %collective-permute-start = (f32[8,16,2048]{2,1,0:T(8,128)S(1)}, f32[8,16,2048]{2,1,0:T(8,128)S(1)}, u32[]{:S(2)}, u32[]{:S(2)}) collective-permute-start(f32[8,16,2048]{2,1,0:T(8,128)S(1)} %get-tuple-element.39), channel_id=1, source_target_pairs={{0,32},{32,0},{64,96},{96,64},{128,160},{160,128},{192,224},{224,1... | collective-permute-start | bytes 3145736 | tf_op jit(solution)/shard_map/ppermute | solution.py:313
  125.3 2.3 %collective-permute-done = f32[8,16,2048]{2,1,0:T(8,128)S(1)} collective-permute-done((f32[8,16,2048]{2,1,0:T(8,128)S(1)}, f32[8,16,2048]{2,1,0:T(8,128)S(1)}, u32[]{:S(2)}, u32[]{:S(2)}) %collective-permute-start) | collective-permute-done | bytes 1048608 | tf_op jit(solution)/shard_map/ppermute | solution.py:313
  127.7 2.0 %collective-permute-start.1 = (f32[16,2048]{1,0:T(8,128)S(1)}, f32[16,2048]{1,0:T(8,128)S(1)}, u32[]{:S(2)}, u32[]{:S(2)}) collective-permute-start(f32[16,2048]{1,0:T(8,128)S(1)} %get-tuple-element.44), channel_id=1, source_target_pairs={{0,64},{32,96},{64,128},{96,160},{128,192},{160,224},{192,256},{22... | collective-permute-start | bytes 393224 | tf_op jit(solution)/shard_map/ppermute | solution.py:313
  129.7 4.5 %collective-permute-start.5 = (f32[16,2048]{1,0:T(8,128)S(1)}, f32[16,2048]{1,0:T(8,128)S(1)}, u32[]{:S(2)}, u32[]{:S(2)}) collective-permute-start(f32[16,2048]{1,0:T(8,128)S(1)} %get-tuple-element.45), channel_id=1, source_target_pairs={{0,448},{32,480},{64,0},{96,32},{128,64},{160,96},{192,128},{224,1... | collective-permute-start | bytes 393224 | tf_op jit(solution)/shard_map/ppermute | solution.py:313
  134.2 1.3 collective-permute-done.1
  135.5 1.9 %collective-permute-start.2 = (f32[16,2048]{1,0:T(8,128)S(1)}, f32[16,2048]{1,0:T(8,128)S(1)}, u32[]{:S(2)}, u32[]{:S(2)}) collective-permute-start(f32[16,2048]{1,0:T(8,128)S(1)} %fusion.4), channel_id=1, source_target_pairs={{0,64},{32,96},{64,128},{96,160},{128,192},{160,224},{192,256},{22... | collective-permute-start | bytes 393224 | tf_op jit(solution)/shard_map/ppermute | solution.py:313
  137.5 5.3 %collective-permute-done.2 = f32[16,2048]{1,0:T(8,128)S(1)} collective-permute-done((f32[16,2048]{1,0:T(8,128)S(1)}, f32[16,2048]{1,0:T(8,128)S(1)}, u32[]{:S(2)}, u32[]{:S(2)}) %collective-permute-start.2) | collective-permute-done | bytes 131104 | tf_op jit(solution)/shard_map/ppermute | solution.py:313
  142.8 1.9 %collective-permute-start.3 = (f32[16,2048]{1,0:T(8,128)S(1)}, f32[16,2048]{1,0:T(8,128)S(1)}, u32[]{:S(2)}, u32[]{:S(2)}) collective-permute-start(f32[16,2048]{1,0:T(8,128)S(1)} %get-tuple-element.42), channel_id=1, source_target_pairs={{0,64},{32,96},{64,128},{96,160},{128,192},{160,224},{192,256},{22... | collective-permute-start | bytes 393224 | tf_op jit(solution)/shard_map/ppermute | solution.py:313
  144.7 4.6 %collective-permute-start.6 = (f32[16,2048]{1,0:T(8,128)S(1)}, f32[16,2048]{1,0:T(8,128)S(1)}, u32[]{:S(2)}, u32[]{:S(2)}) collective-permute-start(f32[16,2048]{1,0:T(8,128)S(1)} %get-tuple-element.43), channel_id=1, source_target_pairs={{0,448},{32,480},{64,0},{96,32},{128,64},{160,96},{192,128},{224,1... | collective-permute-start | bytes 393224 | tf_op jit(solution)/shard_map/ppermute | solution.py:313
  151.3 1.9 %collective-permute-start.4 = (f32[16,2048]{1,0:T(8,128)S(1)}, f32[16,2048]{1,0:T(8,128)S(1)}, u32[]{:S(2)}, u32[]{:S(2)}) collective-permute-start(f32[16,2048]{1,0:T(8,128)S(1)} %get-tuple-element.40), channel_id=1, source_target_pairs={{0,64},{32,96},{64,128},{96,160},{128,192},{160,224},{192,256},{22... | collective-permute-start | bytes 393224 | tf_op jit(solution)/shard_map/ppermute | solution.py:313
  153.2 5.3 %collective-permute-start.7 = (f32[16,2048]{1,0:T(8,128)S(1)}, f32[16,2048]{1,0:T(8,128)S(1)}, u32[]{:S(2)}, u32[]{:S(2)}) collective-permute-start(f32[16,2048]{1,0:T(8,128)S(1)} %get-tuple-element.41), channel_id=1, source_target_pairs={{0,448},{32,480},{64,0},{96,32},{128,64},{160,96},{192,128},{224,1... | collective-permute-start | bytes 393224 | tf_op jit(solution)/shard_map/ppermute | solution.py:313
  161.1 4.2 %all-to-all-done.6.parts_ref = f32[32,64,256]{2,1,0:T(8,128)S(1)} async-done(((f32[32,64,256]{2,1,0:T(8,128)}), f32[32,64,256]{2,1,0:T(8,128)S(1)}, u32[]{:S(2)}, u32[]{:S(2)}) %all-to-all-start.6) | async-done | bytes 2097184 | tf_op jit(solution)/shard_map/all_to_all | solution.py:309
  (19 shorter events, 9.6 us)
Async XLA Ops:
  91.7 14.0 %copy-start.1 = (s32[8,128]{1,0:T(8,128)S(1)}, s32[8,128]{1,0:T(8,128)}, u32[]{:S(2)}) copy-start(s32[8,128]{1,0:T(8,128)} %mask_ref.1) | copy-start | bytes 12292
  110.7 1.3 copy-start
  112.1 53.2 %all-to-all-start.6 = ((f32[32,64,256]{2,1,0:T(8,128)}), f32[32,64,256]{2,1,0:T(8,128)S(1)}, u32[]{:S(2)}, u32[]{:S(2)}) async-start(f32[32,64,256]{2,1,0:T(8,128)} %copy-done), calls=%async_computation.6 | async-start | bytes 4194304 | tf_op jit(solution)/shard_map/all_to_all | solution.py:309
  122.1 5.4 %collective-permute-start = (f32[8,16,2048]{2,1,0:T(8,128)S(1)}, f32[8,16,2048]{2,1,0:T(8,128)S(1)}, u32[]{:S(2)}, u32[]{:S(2)}) collective-permute-start(f32[8,16,2048]{2,1,0:T(8,128)S(1)} %get-tuple-element.39), channel_id=1, source_target_pairs={{0,32},{32,0},{64,96},{96,64},{128,160},{160,128},{192,224},{224,1... | collective-permute-start | bytes 3145736 | tf_op jit(solution)/shard_map/ppermute | solution.py:313
  127.7 7.8 %collective-permute-start.1 = (f32[16,2048]{1,0:T(8,128)S(1)}, f32[16,2048]{1,0:T(8,128)S(1)}, u32[]{:S(2)}, u32[]{:S(2)}) collective-permute-start(f32[16,2048]{1,0:T(8,128)S(1)} %get-tuple-element.44), channel_id=1, source_target_pairs={{0,64},{32,96},{64,128},{96,160},{128,192},{160,224},{192,256},{22... | collective-permute-start | bytes 393224 | tf_op jit(solution)/shard_map/ppermute | solution.py:313
  129.7 7.8 %collective-permute-start.5 = (f32[16,2048]{1,0:T(8,128)S(1)}, f32[16,2048]{1,0:T(8,128)S(1)}, u32[]{:S(2)}, u32[]{:S(2)}) collective-permute-start(f32[16,2048]{1,0:T(8,128)S(1)} %get-tuple-element.45), channel_id=1, source_target_pairs={{0,448},{32,480},{64,0},{96,32},{128,64},{160,96},{192,128},{224,1... | collective-permute-start | bytes 393224 | tf_op jit(solution)/shard_map/ppermute | solution.py:313
  135.5 7.2 %collective-permute-start.2 = (f32[16,2048]{1,0:T(8,128)S(1)}, f32[16,2048]{1,0:T(8,128)S(1)}, u32[]{:S(2)}, u32[]{:S(2)}) collective-permute-start(f32[16,2048]{1,0:T(8,128)S(1)} %fusion.4), channel_id=1, source_target_pairs={{0,64},{32,96},{64,128},{96,160},{128,192},{160,224},{192,256},{22... | collective-permute-start | bytes 393224 | tf_op jit(solution)/shard_map/ppermute | solution.py:313
  142.8 7.2 %collective-permute-start.3 = (f32[16,2048]{1,0:T(8,128)S(1)}, f32[16,2048]{1,0:T(8,128)S(1)}, u32[]{:S(2)}, u32[]{:S(2)}) collective-permute-start(f32[16,2048]{1,0:T(8,128)S(1)} %get-tuple-element.42), channel_id=1, source_target_pairs={{0,64},{32,96},{64,128},{96,160},{128,192},{160,224},{192,256},{22... | collective-permute-start | bytes 393224 | tf_op jit(solution)/shard_map/ppermute | solution.py:313
  144.7 6.5 %collective-permute-start.6 = (f32[16,2048]{1,0:T(8,128)S(1)}, f32[16,2048]{1,0:T(8,128)S(1)}, u32[]{:S(2)}, u32[]{:S(2)}) collective-permute-start(f32[16,2048]{1,0:T(8,128)S(1)} %get-tuple-element.43), channel_id=1, source_target_pairs={{0,448},{32,480},{64,0},{96,32},{128,64},{160,96},{192,128},{224,1... | collective-permute-start | bytes 393224 | tf_op jit(solution)/shard_map/ppermute | solution.py:313
  151.3 7.9 %collective-permute-start.4 = (f32[16,2048]{1,0:T(8,128)S(1)}, f32[16,2048]{1,0:T(8,128)S(1)}, u32[]{:S(2)}, u32[]{:S(2)}) collective-permute-start(f32[16,2048]{1,0:T(8,128)S(1)} %get-tuple-element.40), channel_id=1, source_target_pairs={{0,64},{32,96},{64,128},{96,160},{128,192},{160,224},{192,256},{22... | collective-permute-start | bytes 393224 | tf_op jit(solution)/shard_map/ppermute | solution.py:313
  153.2 7.2 %collective-permute-start.7 = (f32[16,2048]{1,0:T(8,128)S(1)}, f32[16,2048]{1,0:T(8,128)S(1)}, u32[]{:S(2)}, u32[]{:S(2)}) collective-permute-start(f32[16,2048]{1,0:T(8,128)S(1)} %get-tuple-element.41), channel_id=1, source_target_pairs={{0,448},{32,480},{64,0},{96,32},{128,64},{160,96},{192,128},{224,1... | collective-permute-start | bytes 393224 | tf_op jit(solution)/shard_map/ppermute | solution.py:313

commit v7 on v6

--- a/solution.py
+++ b/solution.py
@@ -95,29 +95,36 @@
 ):
     images, masked = mask_ref.shape
     protos = teacher_exp_ref.shape[1]
-    loads = [
+    mask_load, teacher_weight_load, student_load, student_weight_load = [
         pltpu.make_async_copy(source, target, sems.at[index])
         for index, (source, target) in enumerate(
             (
                 (mask_hbm, mask_ref),
-                (teacher_hbm, teacher_ref),
                 (teacher_weight_hbm, teacher_weight_ref),
                 (student_hbm, student_ref),
                 (student_weight_hbm, student_weight_ref),
             )
         )
     ]
-    for load in loads:
+    teacher_loads = [
+        pltpu.make_async_copy(teacher_hbm.at[image], teacher_ref.at[image], sems.at[4 + image])
+        for image in range(images)
+    ]
+    mask_load.start()
+    for load in teacher_loads:
         load.start()
-    loads[0].wait()
+    teacher_weight_load.start()
+    mask_load.wait()
     positions = mask_ref[...].astype(f32).T
-    loads[1].wait()
     for image in range(images):
+        teacher_loads[image].wait()
         picked = pick(teacher_ref, positions, image)
         length = jnp.sqrt(jnp.sum(picked * picked, axis=1, keepdims=True) + epsilon)
         rows = slice(image * masked, (image + 1) * masked)
         teacher_bf_ref[rows, :] = (picked * (1.0 / length)).astype(bf16)
-    loads[2].wait()
+    student_load.start()
+    student_weight_load.start()
+    teacher_weight_load.wait()
 
     def teacher_tile(tile, _):
         cols = pl.ds(pl.multiple_of(tile * TILE, TILE), TILE)
@@ -130,7 +137,7 @@
         return 0
 
     lax.fori_loop(0, protos // TILE, teacher_tile, 0, unroll=4)
-    loads[3].wait()
+    student_load.wait()
 
     for image in range(images):
         picked = pick(student_ref, positions, image)
@@ -142,7 +149,7 @@
         turned_ref[:, rows] = unit.T.astype(bf16)
         inverse_ref[rows, :] = jnp.broadcast_to(inverse, (masked, LANES))
     parts_ref[...] = jnp.zeros_like(parts_ref)
-    loads[4].wait()
+    student_weight_load.wait()
 
     def student_tile(tile, _):
         cols = pl.ds(pl.multiple_of(tile * TILE, TILE), TILE)
@@ -221,7 +228,7 @@
     total_rows,
     sums_ref, student_ref, cols_ref, teacher_exp_ref, student_exp_ref, unit_weight_ref, unit_ref, inverse_ref,
     mask_ref,
-    placed_ref, score_hbm, row_ref, total_ref, sum_ref, score_ref, sem,
+    placed_hbm, score_hbm, row_ref, total_ref, sum_ref, score_ref, placed_ref, sems,
 ):
     rows = teacher_exp_ref.shape[0]
     row_ref[...] = rows_on_sublanes(1.0 / (jnp.sum(sums_ref[...], axis=0) * total_rows))
@@ -230,43 +237,58 @@
     totals = jnp.concatenate([student_ref[group * step][:, rows:] for group in range(groups)], axis=1)
     total_ref[...] = rows_on_sublanes((1.0 / temp_student) / totals)
 
-    def one_tile(tile, _):
-        cols = pl.ds(pl.multiple_of(tile * TILE, TILE), TILE)
-        target = teacher_exp_ref[:, cols] * spread(row_ref[...], TILE)
-        target = target * (cols_ref[:, cols] * (total_rows / temp_student))
-        score = (student_exp_ref[:, cols] * spread(total_ref[...], TILE) - target).astype(bf16)
-        score_ref[:, cols] = score
-        return 0
-
-    lax.fori_loop(0, teacher_exp_ref.shape[1] // TILE, one_tile, 0, unroll=2)
-    store = pltpu.make_async_copy(score_ref, score_hbm, sem)
-    store.start()
-    sum_ref[...] = lax.dot_general(
-        score_ref[...], unit_weight_ref[...], (((1,), (1,)), ((), ())), preferred_element_type=f32
-    )
+    protos = teacher_exp_ref.shape[1]
+    halves = [slice(0, protos // 2), slice(protos // 2, protos)]
+    stores = [
+        pltpu.make_async_copy(score_ref.at[:, half], score_hbm.at[:, half], sems.at[index])
+        for index, half in enumerate(halves)
+    ]
+
+    def score_of(half):
+        for start in range(half.start, half.stop, TILE):
+            cols = slice(start, start + TILE)
+            target = teacher_exp_ref[:, cols] * spread(row_ref[...], TILE)
+            target = target * (cols_ref[:, cols] * (total_rows / temp_student))
+            score = (student_exp_ref[:, cols] * spread(total_ref[...], TILE) - target).astype(bf16)
+            score_ref[:, cols] = score
+
+    def product(half):
+        return lax.dot_general(
+            score_ref[:, half], unit_weight_ref[:, half], (((1,), (1,)), ((), ())), preferred_element_type=f32
+        )
+
+    score_of(halves[0])
+    stores[0].start()
+    sum_ref[...] = product(halves[0])
+    score_of(halves[1])
+    stores[1].start()
+    sum_ref[...] += product(halves[1])
     images, masked = mask_ref.shape
     width = unit_ref.shape[1]
     shares = placed_ref.shape[0]
     share = placed_ref.shape[1] // images
     patch = lax.broadcasted_iota(jnp.int32, (shares * share, 2 * masked), 0)
 
-    def one_image(image, _):
-        rows = pl.ds(pl.multiple_of(image * masked, masked), masked)
+    placed_stores = []
+    for image in range(images):
+        rows = slice(image * masked, (image + 1) * masked)
         unit = unit_ref[rows, :]
         total = sum_ref[rows, :]
         projection = jnp.sum(unit * total, axis=1, keepdims=True)
         gradient = (total - unit * projection) * spread(inverse_ref[rows, :], width)
         high = gradient.astype(bf16)
         low = (gradient - high.astype(f32)).astype(bf16)
-        positions = mask_ref[pl.ds(image, 1), :]
+        positions = mask_ref[image : image + 1, :]
         chosen = (patch == jnp.concatenate([positions, positions], axis=1)).astype(bf16)
         placed = jnp.dot(chosen, jnp.concatenate([high, low], axis=0), preferred_element_type=f32)
-        where = pl.ds(pl.multiple_of(image * share, share), share)
+        where = pl.ds(image * share, share)
         placed_ref[:, where, :] = placed.reshape(shares, share, width)
-        return 0
-
-    lax.fori_loop(0, images, one_image, 0, unroll=4)
-    store.wait()
+        placed_stores.append(
+            pltpu.make_async_copy(placed_ref.at[:, where], placed_hbm.at[:, where], sems.at[2 + image])
+        )
+        placed_stores[-1].start()
+    for store in stores + placed_stores:
+        store.wait()
 
 
 def weight_body(
@@ -365,7 +387,7 @@
             pltpu.VMEM((rows, depth), bf16),
             pltpu.VMEM((rows, depth), bf16),
             pltpu.VMEM((rows, LANES), f32),
-            pltpu.SemaphoreType.DMA((5,)),
+            pltpu.SemaphoreType.DMA((4 + images,)),
         ],
         limit=12, hbm=5, flops=2 * work, moved=2**23,
     )
@@ -397,16 +419,17 @@
     levels = row_devices // 2
     placed, score = call(
         functools.partial(feature_body, total_rows),
-        [((proto_devices, images * share, depth), f32), ((rows, protos), bf16, pltpu.HBM)],
+        [((proto_devices, images * share, depth), f32, pltpu.HBM), ((rows, protos), bf16, pltpu.HBM)],
         (row_sums, student_sums, col_scale, teacher_exp, student_exp, unit_weight, unit, inverse, mask_index),
         [
             pltpu.VMEM((rows, LANES), f32),
             pltpu.VMEM((rows, LANES), f32),
             pltpu.VMEM((rows, depth), f32),
             pltpu.VMEM((rows, protos), bf16),
-            pltpu.SemaphoreType.DMA,
-        ],
-        limit=12, flops=work, moved=2**24,
+            pltpu.VMEM((proto_devices, images * share, depth), f32),
+            pltpu.SemaphoreType.DMA((2 + images,)),
+        ],
+        limit=16, flops=work, moved=2**24,
     )
     arrived = everyones(placed, "protos")
     mine, other = call(

time: 168 us -> 167 us (level)
  no operation moved by 1% of the time
where the time goes in v7:
time: 167 us; the launch traced here: 165 us
  blocking collectives  92.5 us (55%)
  starting transfers between devices  30 us (18%)
  Pallas kernels  24.2 us (14%)
  waiting for transfers between devices  16.9 us (10%)
    all_to_all x6, blocking collectives, everyones(): return lax.all_to_all(copies, axis, 0, 0, tiled=True)  92.5 us
    ppermute x8, starting transfers between devices, send_rows(): lax.ppermute(values, 'rows', [(i, to(i)) for i in range(lax.axis_size('ro...  25.3 us
    pallas_call x9, Pallas kernels, call(): pl.pallas_call(body, out_shape=[(space[0] if space else pltpu.VMEM)(shape...  24.2 us
    ppermute x8, waiting for transfers between devices, send_rows(): lax.ppermute(values, 'rows', [(i, to(i)) for i in range(lax.axis_size('ro...  12.7 us
    all_to_all x1, starting transfers between devices, everyones(): return lax.all_to_all(copies, axis, 0, 0, tiled=True)  4.76 us
    all_to_all x1, waiting for transfers between devices, everyones(): return lax.all_to_all(copies, axis, 0, 0, tiled=True)  4.21 us
  transfers between devices with their start and end apart: 9, of which 8 were waited for; matrix products, arithmetic and copies ran while one was open for 1% of the time, Pallas kernels for 3%

profile of v7, /device:TPU:1, one launch (start us, length us, event | category | flops | bytes accessed | tf_op | source)
XLA Modules:
  0.0 165.4 jit_solution(11006389833733383184)
XLA Ops:
  0.6 8.7 %shard_map.68 = (f32[1024,2048]{1,0:T(8,128)S(1)}, f32[16,1,2048]{2,1,0:T(1,128)S(1)}, f32[1024,2048]{1,0:T(8,128)S(1)}, f32[1,1024]{1,0:T(1,128)S(1)}, f32[1024...) custom-call(bf16[8,256,256]{2,1,0:T(8,128)(2,1)} %teacher_hbm.1, ...), custom_call_target="tpu_custom_call" | custom-call | flops 2147483648 | bytes 8388608 | tf_op jit(solution)/shard_map/pallas_call | solution.py:26
  9.3 20.8 %all_to_all.35.sums_ref = f32[16,1,2048]{2,1,0:T(1,128)S(1)} all-to-all(f32[16,1,2048]{2,1,0:T(1,128)S(1)} %get-tuple-element.21), channel_id=1, replica_groups=mesh['rows'=16,'protos'=32] {'rows'}, dimensions={0} | all-to-all | bytes 262144 | tf_op jit(solution)/shard_map/all_to_all | solution.py:331
  30.1 1.3 shard_map.69
  31.3 19.0 %all_to_all.36.sums_ref = f32[32,1,1152]{2,1,0:T(1,128)S(1)} all-to-all(f32[32,1,1152]{2,1,0:T(1,128)S(1)} %get-tuple-element.24), channel_id=1, replica_groups=mesh['rows'=16,'protos'=32] {'protos'}, dimensions={0} | all-to-all | bytes 294912 | tf_op jit(solution)/shard_map/all_to_all | solution.py:331
  51.2 13.3 %all_to_all.37.sums_ref = f32[16,1,2048]{2,1,0:T(1,128)S(1)} all-to-all(f32[16,1,2048]{2,1,0:T(1,128)S(1)} %get-tuple-element.25), channel_id=1, replica_groups=mesh['rows'=16,'protos'=32] {'rows'}, dimensions={0} | all-to-all | bytes 262144 | tf_op jit(solution)/shard_map/all_to_all | solution.py:331
  64.5 1.3 shard_map.71
  65.8 13.2 %all_to_all.38.sums_ref.student_ref = f32[32,1,1152]{2,1,0:T(1,128)S(1)} all-to-all(f32[32,1,1152]{2,1,0:T(1,128)S(1)} %get-tuple-element.27), channel_id=1, replica_groups=mesh['rows'=16,'protos'=32] {'protos'}, dimensions={0} | all-to-all | bytes 294912 | tf_op jit(solution)/shard_map/all_to_all | solution.py:331
  79.9 13.4 %all_to_all.39.sums_ref = f32[16,1,2048]{2,1,0:T(1,128)S(1)} all-to-all(f32[16,1,2048]{2,1,0:T(1,128)S(1)} %shard_map.72), channel_id=1, replica_groups=mesh['rows'=16,'protos'=32] {'rows'}, dimensions={0} | all-to-all | bytes 262144 | tf_op jit(solution)/shard_map/all_to_all | solution.py:331
  94.2 13.0 %all_to_all.40.sums_ref = f32[32,1,1024]{2,1,0:T(1,128)S(1)} all-to-all(f32[32,1,1024]{2,1,0:T(1,128)S(1)} %get-tuple-element.28), channel_id=1, replica_groups=mesh['rows'=16,'protos'=32] {'protos'}, dimensions={0} | all-to-all | bytes 262144 | tf_op jit(solution)/shard_map/all_to_all | solution.py:331
  107.2 4.2 %shard_map.74 = (f32[32,64,256]{2,1,0:T(8,128)}, bf16[1024,2048]{1,0:T(8,128)(2,1)}) custom-call(f32[32,1,1024]{2,1,0:T(1,128)S(1)} %all_to_all.40.sums_ref, f32[32,1,1152]{2,1,0:T(1,128)S(1)} %all_to_all.38.sums_ref.student_ref, f32[1,2048]{1,0:T(1,128)S(1)} %get-tuple-element.29.cols_ref, f32[1024,2048]{1,0:T(8,128)S(1)} %get-tuple-element.22.exp_ref.teacher_exp_ref, ...), custom_call_target="tpu_custom_call" | custom-call | flops 1073741824 | bytes 16777216 | tf_op jit(solution)/shard_map/pallas_call | solution.py:26
  111.4 4.8 %all-to-all-start.6 = ((f32[32,64,256]{2,1,0:T(8,128)}), f32[32,64,256]{2,1,0:T(8,128)S(1)}, u32[]{:S(2)}, u32[]{:S(2)}) async-start(f32[32,64,256]{2,1,0:T(8,128)} %get-tuple-element.34), calls=%async_computation.6 | async-start | bytes 4194304 | tf_op jit(solution)/shard_map/all_to_all | solution.py:331
  116.2 5.2 %shard_map.76 = (f32[8,16,2048]{2,1,0:T(8,128)S(1)}, f32[8,16,2048]{2,1,0:T(8,128)S(1)}) custom-call(bf16[1024,2048]{1,0:T(8,128)(2,1)} %get-tuple-element.35.score_hbm, bf16[256,2048]{1,0:T(8,128)(2,1)} %weight_hbm.1, bf16[256,1024]{1,0:T(8,128)(2,1)S(1)} %get-tuple-element.36.turned_ref, f32[1,2048]{1,0:T(1,128)S(1)} %get-tuple-element.37.length_ref), custom_call_target="tpu_custom_call" | custom-call | tf_op jit(solution)/shard_map/pallas_call | solution.py:26
  121.4 3.2 %collective-permute-start = (f32[8,16,2048]{2,1,0:T(8,128)S(1)}, f32[8,16,2048]{2,1,0:T(8,128)S(1)}, u32[]{:S(2)}, u32[]{:S(2)}) collective-permute-start(f32[8,16,2048]{2,1,0:T(8,128)S(1)} %get-tuple-element.39), channel_id=1, source_target_pairs={{0,32},{32,0},{64,96},{96,64},{128,160},{160,128},{192,224},{224,1... | collective-permute-start | bytes 3145736 | tf_op jit(solution)/shard_map/ppermute | solution.py:335
  124.6 2.3 %collective-permute-done = f32[8,16,2048]{2,1,0:T(8,128)S(1)} collective-permute-done((f32[8,16,2048]{2,1,0:T(8,128)S(1)}, f32[8,16,2048]{2,1,0:T(8,128)S(1)}, u32[]{:S(2)}, u32[]{:S(2)}) %collective-permute-start) | collective-permute-done | bytes 1048608 | tf_op jit(solution)/shard_map/ppermute | solution.py:335
  127.0 2.0 %collective-permute-start.1 = (f32[16,2048]{1,0:T(8,128)S(1)}, f32[16,2048]{1,0:T(8,128)S(1)}, u32[]{:S(2)}, u32[]{:S(2)}) collective-permute-start(f32[16,2048]{1,0:T(8,128)S(1)} %get-tuple-element.44), channel_id=1, source_target_pairs={{0,64},{32,96},{64,128},{96,160},{128,192},{160,224},{192,256},{22... | collective-permute-start | bytes 393224 | tf_op jit(solution)/shard_map/ppermute | solution.py:335
  129.0 4.5 %collective-permute-start.5 = (f32[16,2048]{1,0:T(8,128)S(1)}, f32[16,2048]{1,0:T(8,128)S(1)}, u32[]{:S(2)}, u32[]{:S(2)}) collective-permute-start(f32[16,2048]{1,0:T(8,128)S(1)} %get-tuple-element.45), channel_id=1, source_target_pairs={{0,448},{32,480},{64,0},{96,32},{128,64},{160,96},{192,128},{224,1... | collective-permute-start | bytes 393224 | tf_op jit(solution)/shard_map/ppermute | solution.py:335
  133.5 1.3 collective-permute-done.1
  134.9 1.9 %collective-permute-start.2 = (f32[16,2048]{1,0:T(8,128)S(1)}, f32[16,2048]{1,0:T(8,128)S(1)}, u32[]{:S(2)}, u32[]{:S(2)}) collective-permute-start(f32[16,2048]{1,0:T(8,128)S(1)} %fusion.4), channel_id=1, source_target_pairs={{0,64},{32,96},{64,128},{96,160},{128,192},{160,224},{192,256},{22... | collective-permute-start | bytes 393224 | tf_op jit(solution)/shard_map/ppermute | solution.py:335
  136.8 5.3 %collective-permute-done.2 = f32[16,2048]{1,0:T(8,128)S(1)} collective-permute-done((f32[16,2048]{1,0:T(8,128)S(1)}, f32[16,2048]{1,0:T(8,128)S(1)}, u32[]{:S(2)}, u32[]{:S(2)}) %collective-permute-start.2) | collective-permute-done | bytes 131104 | tf_op jit(solution)/shard_map/ppermute | solution.py:335
  142.1 1.9 %collective-permute-start.3 = (f32[16,2048]{1,0:T(8,128)S(1)}, f32[16,2048]{1,0:T(8,128)S(1)}, u32[]{:S(2)}, u32[]{:S(2)}) collective-permute-start(f32[16,2048]{1,0:T(8,128)S(1)} %get-tuple-element.42), channel_id=1, source_target_pairs={{0,64},{32,96},{64,128},{96,160},{128,192},{160,224},{192,256},{22... | collective-permute-start | bytes 393224 | tf_op jit(solution)/shard_map/ppermute | solution.py:335
  144.1 4.6 %collective-permute-start.6 = (f32[16,2048]{1,0:T(8,128)S(1)}, f32[16,2048]{1,0:T(8,128)S(1)}, u32[]{:S(2)}, u32[]{:S(2)}) collective-permute-start(f32[16,2048]{1,0:T(8,128)S(1)} %get-tuple-element.43), channel_id=1, source_target_pairs={{0,448},{32,480},{64,0},{96,32},{128,64},{160,96},{192,128},{224,1... | collective-permute-start | bytes 393224 | tf_op jit(solution)/shard_map/ppermute | solution.py:335
  150.6 1.9 %collective-permute-start.4 = (f32[16,2048]{1,0:T(8,128)S(1)}, f32[16,2048]{1,0:T(8,128)S(1)}, u32[]{:S(2)}, u32[]{:S(2)}) collective-permute-start(f32[16,2048]{1,0:T(8,128)S(1)} %get-tuple-element.40), channel_id=1, source_target_pairs={{0,64},{32,96},{64,128},{96,160},{128,192},{160,224},{192,256},{22... | collective-permute-start | bytes 393224 | tf_op jit(solution)/shard_map/ppermute | solution.py:335
  152.5 5.3 %collective-permute-start.7 = (f32[16,2048]{1,0:T(8,128)S(1)}, f32[16,2048]{1,0:T(8,128)S(1)}, u32[]{:S(2)}, u32[]{:S(2)}) collective-permute-start(f32[16,2048]{1,0:T(8,128)S(1)} %get-tuple-element.41), channel_id=1, source_target_pairs={{0,448},{32,480},{64,0},{96,32},{128,64},{160,96},{192,128},{224,1... | collective-permute-start | bytes 393224 | tf_op jit(solution)/shard_map/ppermute | solution.py:335
  160.4 4.2 %all-to-all-done.6.parts_ref = f32[32,64,256]{2,1,0:T(8,128)S(1)} async-done(((f32[32,64,256]{2,1,0:T(8,128)}), f32[32,64,256]{2,1,0:T(8,128)S(1)}, u32[]{:S(2)}, u32[]{:S(2)}) %all-to-all-start.6) | async-done | bytes 2097184 | tf_op jit(solution)/shard_map/all_to_all | solution.py:331
  (17 shorter events, 8.4 us)
Async XLA Ops:
  93.2 14.0 %copy-start = (s32[8,128]{1,0:T(8,128)S(1)}, s32[8,128]{1,0:T(8,128)}, u32[]{:S(2)}) copy-start(s32[8,128]{1,0:T(8,128)} %mask_ref.1) | copy-start | bytes 12292
  111.4 53.2 %all-to-all-start.6 = ((f32[32,64,256]{2,1,0:T(8,128)}), f32[32,64,256]{2,1,0:T(8,128)S(1)}, u32[]{:S(2)}, u32[]{:S(2)}) async-start(f32[32,64,256]{2,1,0:T(8,128)} %get-tuple-element.34), calls=%async_computation.6 | async-start | bytes 4194304 | tf_op jit(solution)/shard_map/all_to_all | solution.py:331
  121.4 5.4 %collective-permute-start = (f32[8,16,2048]{2,1,0:T(8,128)S(1)}, f32[8,16,2048]{2,1,0:T(8,128)S(1)}, u32[]{:S(2)}, u32[]{:S(2)}) collective-permute-start(f32[8,16,2048]{2,1,0:T(8,128)S(1)} %get-tuple-element.39), channel_id=1, source_target_pairs={{0,32},{32,0},{64,96},{96,64},{128,160},{160,128},{192,224},{224,1... | collective-permute-start | bytes 3145736 | tf_op jit(solution)/shard_map/ppermute | solution.py:335
  127.0 7.8 %collective-permute-start.1 = (f32[16,2048]{1,0:T(8,128)S(1)}, f32[16,2048]{1,0:T(8,128)S(1)}, u32[]{:S(2)}, u32[]{:S(2)}) collective-permute-start(f32[16,2048]{1,0:T(8,128)S(1)} %get-tuple-element.44), channel_id=1, source_target_pairs={{0,64},{32,96},{64,128},{96,160},{128,192},{160,224},{192,256},{22... | collective-permute-start | bytes 393224 | tf_op jit(solution)/shard_map/ppermute | solution.py:335
  129.0 7.8 %collective-permute-start.5 = (f32[16,2048]{1,0:T(8,128)S(1)}, f32[16,2048]{1,0:T(8,128)S(1)}, u32[]{:S(2)}, u32[]{:S(2)}) collective-permute-start(f32[16,2048]{1,0:T(8,128)S(1)} %get-tuple-element.45), channel_id=1, source_target_pairs={{0,448},{32,480},{64,0},{96,32},{128,64},{160,96},{192,128},{224,1... | collective-permute-start | bytes 393224 | tf_op jit(solution)/shard_map/ppermute | solution.py:335
  134.9 7.2 %collective-permute-start.2 = (f32[16,2048]{1,0:T(8,128)S(1)}, f32[16,2048]{1,0:T(8,128)S(1)}, u32[]{:S(2)}, u32[]{:S(2)}) collective-permute-start(f32[16,2048]{1,0:T(8,128)S(1)} %fusion.4), channel_id=1, source_target_pairs={{0,64},{32,96},{64,128},{96,160},{128,192},{160,224},{192,256},{22... | collective-permute-start | bytes 393224 | tf_op jit(solution)/shard_map/ppermute | solution.py:335
  142.1 7.2 %collective-permute-start.3 = (f32[16,2048]{1,0:T(8,128)S(1)}, f32[16,2048]{1,0:T(8,128)S(1)}, u32[]{:S(2)}, u32[]{:S(2)}) collective-permute-start(f32[16,2048]{1,0:T(8,128)S(1)} %get-tuple-element.42), channel_id=1, source_target_pairs={{0,64},{32,96},{64,128},{96,160},{128,192},{160,224},{192,256},{22... | collective-permute-start | bytes 393224 | tf_op jit(solution)/shard_map/ppermute | solution.py:335
  144.1 6.5 %collective-permute-start.6 = (f32[16,2048]{1,0:T(8,128)S(1)}, f32[16,2048]{1,0:T(8,128)S(1)}, u32[]{:S(2)}, u32[]{:S(2)}) collective-permute-start(f32[16,2048]{1,0:T(8,128)S(1)} %get-tuple-element.43), channel_id=1, source_target_pairs={{0,448},{32,480},{64,0},{96,32},{128,64},{160,96},{192,128},{224,1... | collective-permute-start | bytes 393224 | tf_op jit(solution)/shard_map/ppermute | solution.py:335
  150.6 7.9 %collective-permute-start.4 = (f32[16,2048]{1,0:T(8,128)S(1)}, f32[16,2048]{1,0:T(8,128)S(1)}, u32[]{:S(2)}, u32[]{:S(2)}) collective-permute-start(f32[16,2048]{1,0:T(8,128)S(1)} %get-tuple-element.40), channel_id=1, source_target_pairs={{0,64},{32,96},{64,128},{96,160},{128,192},{160,224},{192,256},{22... | collective-permute-start | bytes 393224 | tf_op jit(solution)/shard_map/ppermute | solution.py:335
  152.5 7.2 %collective-permute-start.7 = (f32[16,2048]{1,0:T(8,128)S(1)}, f32[16,2048]{1,0:T(8,128)S(1)}, u32[]{:S(2)}, u32[]{:S(2)}) collective-permute-start(f32[16,2048]{1,0:T(8,128)S(1)} %get-tuple-element.41), channel_id=1, source_target_pairs={{0,448},{32,480},{64,0},{96,32},{128,64},{160,96},{192,128},{224,1... | collective-permute-start | bytes 393224 | tf_op jit(solution)/shard_map/ppermute | solution.py:335

commit v8 on v7

--- a/solution.py
+++ b/solution.py
@@ -95,36 +95,29 @@
 ):
     images, masked = mask_ref.shape
     protos = teacher_exp_ref.shape[1]
-    mask_load, teacher_weight_load, student_load, student_weight_load = [
+    loads = [
         pltpu.make_async_copy(source, target, sems.at[index])
         for index, (source, target) in enumerate(
             (
                 (mask_hbm, mask_ref),
+                (teacher_hbm, teacher_ref),
                 (teacher_weight_hbm, teacher_weight_ref),
                 (student_hbm, student_ref),
                 (student_weight_hbm, student_weight_ref),
             )
         )
     ]
-    teacher_loads = [
-        pltpu.make_async_copy(teacher_hbm.at[image], teacher_ref.at[image], sems.at[4 + image])
-        for image in range(images)
-    ]
-    mask_load.start()
-    for load in teacher_loads:
+    for load in loads:
         load.start()
-    teacher_weight_load.start()
-    mask_load.wait()
+    loads[0].wait()
     positions = mask_ref[...].astype(f32).T
+    loads[1].wait()
     for image in range(images):
-        teacher_loads[image].wait()
         picked = pick(teacher_ref, positions, image)
         length = jnp.sqrt(jnp.sum(picked * picked, axis=1, keepdims=True) + epsilon)
         rows = slice(image * masked, (image + 1) * masked)
         teacher_bf_ref[rows, :] = (picked * (1.0 / length)).astype(bf16)
-    student_load.start()
-    student_weight_load.start()
-    teacher_weight_load.wait()
+    loads[2].wait()
 
     def teacher_tile(tile, _):
         cols = pl.ds(pl.multiple_of(tile * TILE, TILE), TILE)
@@ -137,7 +130,7 @@
         return 0
 
     lax.fori_loop(0, protos // TILE, teacher_tile, 0, unroll=4)
-    student_load.wait()
+    loads[3].wait()
 
     for image in range(images):
         picked = pick(student_ref, positions, image)
@@ -149,7 +142,7 @@
         turned_ref[:, rows] = unit.T.astype(bf16)
         inverse_ref[rows, :] = jnp.broadcast_to(inverse, (masked, LANES))
     parts_ref[...] = jnp.zeros_like(parts_ref)
-    student_weight_load.wait()
+    loads[4].wait()
 
     def student_tile(tile, _):
         cols = pl.ds(pl.multiple_of(tile * TILE, TILE), TILE)
@@ -297,21 +290,22 @@
     levels, share = mine_ref.shape[:2]
     me = lax.axis_index("rows")
     core, level = me % 2, me // 2
-    tiles = weight_ref.shape[1] // TILE
-    weight_load = pltpu.make_async_copy(weight_hbm, weight_ref, sems.at[tiles])
-    weight_load.start()
+    protos = weight_ref.shape[1]
+    half = protos // 2
+    weight_load = pltpu.make_async_copy(weight_hbm, weight_ref, sems.at[2])
     loads = [
         pltpu.make_async_copy(
-            score_hbm.at[:, pl.ds(tile * TILE, TILE)], score_ref.at[:, pl.ds(tile * TILE, TILE)], sems.at[tile]
+            score_hbm.at[:, pl.ds(start, half)], score_ref.at[:, pl.ds(start, half)], sems.at[index]
         )
-        for tile in range(tiles)
+        for index, start in enumerate((0, half))
     ]
-    for load in loads:
+    for load in (loads[0], weight_load, loads[1]):
         load.start()
     weight_load.wait()
-    for tile in range(tiles):
-        cols = slice(tile * TILE, (tile + 1) * TILE)
-        loads[tile].wait()
+    for start in range(0, protos, TILE):
+        cols = slice(start, start + TILE)
+        if start % half == 0:
+            loads[start // half].wait()
         total = jnp.dot(turned_ref[...], score_ref[:, cols], preferred_element_type=f32)
         inverse = 1.0 / length_ref[:, cols]
         unit = weight_ref[:, cols].astype(f32) * inverse
@@ -387,7 +381,7 @@
             pltpu.VMEM((rows, depth), bf16),
             pltpu.VMEM((rows, depth), bf16),
             pltpu.VMEM((rows, LANES), f32),
-            pltpu.SemaphoreType.DMA((4 + images,)),
+            pltpu.SemaphoreType.DMA((5,)),
         ],
         limit=12, hbm=5, flops=2 * work, moved=2**23,
     )
@@ -439,7 +433,7 @@
         [
             pltpu.VMEM((rows, protos), bf16),
             pltpu.VMEM(student_weight.shape, bf16),
-            pltpu.SemaphoreType.DMA((protos // TILE + 1,)),
+            pltpu.SemaphoreType.DMA((3,)),
         ],
         limit=12, hbm=2,
     )

time: 167 us -> 165 us (0.988)
  Pallas kernels: 24.2 us -> 21.2 us
  waiting for transfers between devices: 16.9 us -> 18.6 us
    pallas_call x9, Pallas kernels: 24.2 us -> 21.2 us  [call(): pl.pallas_call(body, out_shape=[(space[0] if space else pltpu.VMEM)(shape...]
    all_to_all x1, waiting for transfers between devices: 4.21 us -> 5.92 us  [everyones(): return lax.all_to_all(copies, axis, 0, 0, tiled=True)]
  transfers between devices with their start and end apart: 9 -> 9, of which waited for: 8 -> 8; matrix products, arithmetic and copies ran while one was open for 1% -> 1% of each run, Pallas kernels for 3% -> 2%
where the time goes in v8:
time: 165 us; the launch traced here: 164 us
  blocking collectives  92.5 us (56%)
  starting transfers between devices  29.9 us (18%)
  Pallas kernels  21.2 us (13%)
  waiting for transfers between devices  18.6 us (11%)
    all_to_all x6, blocking collectives, everyones(): return lax.all_to_all(copies, axis, 0, 0, tiled=True)  92.5 us
    ppermute x8, starting transfers between devices, send_rows(): lax.ppermute(values, 'rows', [(i, to(i)) for i in range(lax.axis_size('ro...  25.3 us
    pallas_call x9, Pallas kernels, call(): pl.pallas_call(body, out_shape=[(space[0] if space else pltpu.VMEM)(shape...  21.2 us
    ppermute x8, waiting for transfers between devices, send_rows(): lax.ppermute(values, 'rows', [(i, to(i)) for i in range(lax.axis_size('ro...  12.7 us
    all_to_all x1, waiting for transfers between devices, everyones(): return lax.all_to_all(copies, axis, 0, 0, tiled=True)  5.92 us
    all_to_all x1, starting transfers between devices, everyones(): return lax.all_to_all(copies, axis, 0, 0, tiled=True)  4.58 us
  transfers between devices with their start and end apart: 9, of which 8 were waited for; matrix products, arithmetic and copies ran while one was open for 1% of the time, Pallas kernels for 2%

profile of v8, /device:TPU:1, one launch (start us, length us, event | category | flops | bytes accessed | tf_op | source)
XLA Modules:
  0.0 163.9 jit_solution(16966953653651827139)
XLA Ops:
  0.6 7.2 %shard_map.68 = (f32[1024,2048]{1,0:T(8,128)S(1)}, f32[16,1,2048]{2,1,0:T(1,128)S(1)}, f32[1024,2048]{1,0:T(8,128)S(1)}, f32[1,1024]{1,0:T(1,128)S(1)}, f32[1024...) custom-call(bf16[8,256,256]{2,1,0:T(8,128)(2,1)} %teacher_hbm.1, ...), custom_call_target="tpu_custom_call" | custom-call | flops 2147483648 | bytes 8388608 | tf_op jit(solution)/shard_map/pallas_call | solution.py:26
  7.8 20.8 %all_to_all.35.sums_ref = f32[16,1,2048]{2,1,0:T(1,128)S(1)} all-to-all(f32[16,1,2048]{2,1,0:T(1,128)S(1)} %get-tuple-element.21), channel_id=1, replica_groups=mesh['rows'=16,'protos'=32] {'rows'}, dimensions={0} | all-to-all | bytes 262144 | tf_op jit(solution)/shard_map/all_to_all | solution.py:325
  28.6 1.3 shard_map.69
  29.9 19.0 %all_to_all.36.sums_ref = f32[32,1,1152]{2,1,0:T(1,128)S(1)} all-to-all(f32[32,1,1152]{2,1,0:T(1,128)S(1)} %get-tuple-element.24), channel_id=1, replica_groups=mesh['rows'=16,'protos'=32] {'protos'}, dimensions={0} | all-to-all | bytes 294912 | tf_op jit(solution)/shard_map/all_to_all | solution.py:325
  49.7 13.3 %all_to_all.37.sums_ref = f32[16,1,2048]{2,1,0:T(1,128)S(1)} all-to-all(f32[16,1,2048]{2,1,0:T(1,128)S(1)} %get-tuple-element.25), channel_id=1, replica_groups=mesh['rows'=16,'protos'=32] {'rows'}, dimensions={0} | all-to-all | bytes 262144 | tf_op jit(solution)/shard_map/all_to_all | solution.py:325
  63.0 1.3 shard_map.71
  64.3 13.2 %all_to_all.38.sums_ref.student_ref = f32[32,1,1152]{2,1,0:T(1,128)S(1)} all-to-all(f32[32,1,1152]{2,1,0:T(1,128)S(1)} %get-tuple-element.27), channel_id=1, replica_groups=mesh['rows'=16,'protos'=32] {'protos'}, dimensions={0} | all-to-all | bytes 294912 | tf_op jit(solution)/shard_map/all_to_all | solution.py:325
  78.4 13.4 %all_to_all.39.sums_ref = f32[16,1,2048]{2,1,0:T(1,128)S(1)} all-to-all(f32[16,1,2048]{2,1,0:T(1,128)S(1)} %shard_map.72), channel_id=1, replica_groups=mesh['rows'=16,'protos'=32] {'rows'}, dimensions={0} | all-to-all | bytes 262144 | tf_op jit(solution)/shard_map/all_to_all | solution.py:325
  92.7 13.0 %all_to_all.40.sums_ref = f32[32,1,1024]{2,1,0:T(1,128)S(1)} all-to-all(f32[32,1,1024]{2,1,0:T(1,128)S(1)} %get-tuple-element.28), channel_id=1, replica_groups=mesh['rows'=16,'protos'=32] {'protos'}, dimensions={0} | all-to-all | bytes 262144 | tf_op jit(solution)/shard_map/all_to_all | solution.py:325
  105.7 4.2 %shard_map.74 = (f32[32,64,256]{2,1,0:T(8,128)}, bf16[1024,2048]{1,0:T(8,128)(2,1)}) custom-call(f32[32,1,1024]{2,1,0:T(1,128)S(1)} %all_to_all.40.sums_ref, f32[32,1,1152]{2,1,0:T(1,128)S(1)} %all_to_all.38.sums_ref.student_ref, f32[1,2048]{1,0:T(1,128)S(1)} %get-tuple-element.29.cols_ref, f32[1024,2048]{1,0:T(8,128)S(1)} %get-tuple-element.22.exp_ref.teacher_exp_ref, ...), custom_call_target="tpu_custom_call" | custom-call | flops 1073741824 | bytes 16777216 | tf_op jit(solution)/shard_map/pallas_call | solution.py:26
  109.9 4.6 %all-to-all-start.6 = ((f32[32,64,256]{2,1,0:T(8,128)}), f32[32,64,256]{2,1,0:T(8,128)S(1)}, u32[]{:S(2)}, u32[]{:S(2)}) async-start(f32[32,64,256]{2,1,0:T(8,128)} %get-tuple-element.34), calls=%async_computation.6 | async-start | bytes 4194304 | tf_op jit(solution)/shard_map/all_to_all | solution.py:325
  114.5 3.7 %shard_map.76 = (f32[8,16,2048]{2,1,0:T(8,128)S(1)}, f32[8,16,2048]{2,1,0:T(8,128)S(1)}) custom-call(bf16[1024,2048]{1,0:T(8,128)(2,1)} %get-tuple-element.35.score_hbm, bf16[256,2048]{1,0:T(8,128)(2,1)} %weight_hbm.1, bf16[256,1024]{1,0:T(8,128)(2,1)S(1)} %get-tuple-element.36.turned_ref, f32[1,2048]{1,0:T(1,128)S(1)} %get-tuple-element.37.length_ref), custom_call_target="tpu_custom_call" | custom-call | tf_op jit(solution)/shard_map/pallas_call | solution.py:26
  118.2 3.2 %collective-permute-start = (f32[8,16,2048]{2,1,0:T(8,128)S(1)}, f32[8,16,2048]{2,1,0:T(8,128)S(1)}, u32[]{:S(2)}, u32[]{:S(2)}) collective-permute-start(f32[8,16,2048]{2,1,0:T(8,128)S(1)} %get-tuple-element.39), channel_id=1, source_target_pairs={{0,32},{32,0},{64,96},{96,64},{128,160},{160,128},{192,224},{224,1... | collective-permute-start | bytes 3145736 | tf_op jit(solution)/shard_map/ppermute | solution.py:329
  121.4 2.3 %collective-permute-done = f32[8,16,2048]{2,1,0:T(8,128)S(1)} collective-permute-done((f32[8,16,2048]{2,1,0:T(8,128)S(1)}, f32[8,16,2048]{2,1,0:T(8,128)S(1)}, u32[]{:S(2)}, u32[]{:S(2)}) %collective-permute-start) | collective-permute-done | bytes 1048608 | tf_op jit(solution)/shard_map/ppermute | solution.py:329
  123.8 2.0 %collective-permute-start.1 = (f32[16,2048]{1,0:T(8,128)S(1)}, f32[16,2048]{1,0:T(8,128)S(1)}, u32[]{:S(2)}, u32[]{:S(2)}) collective-permute-start(f32[16,2048]{1,0:T(8,128)S(1)} %get-tuple-element.44), channel_id=1, source_target_pairs={{0,64},{32,96},{64,128},{96,160},{128,192},{160,224},{192,256},{22... | collective-permute-start | bytes 393224 | tf_op jit(solution)/shard_map/ppermute | solution.py:329
  125.8 4.5 %collective-permute-start.5 = (f32[16,2048]{1,0:T(8,128)S(1)}, f32[16,2048]{1,0:T(8,128)S(1)}, u32[]{:S(2)}, u32[]{:S(2)}) collective-permute-start(f32[16,2048]{1,0:T(8,128)S(1)} %get-tuple-element.45), channel_id=1, source_target_pairs={{0,448},{32,480},{64,0},{96,32},{128,64},{160,96},{192,128},{224,1... | collective-permute-start | bytes 393224 | tf_op jit(solution)/shard_map/ppermute | solution.py:329
  130.4 1.3 collective-permute-done.1
  131.7 1.9 %collective-permute-start.2 = (f32[16,2048]{1,0:T(8,128)S(1)}, f32[16,2048]{1,0:T(8,128)S(1)}, u32[]{:S(2)}, u32[]{:S(2)}) collective-permute-start(f32[16,2048]{1,0:T(8,128)S(1)} %fusion.4), channel_id=1, source_target_pairs={{0,64},{32,96},{64,128},{96,160},{128,192},{160,224},{192,256},{22... | collective-permute-start | bytes 393224 | tf_op jit(solution)/shard_map/ppermute | solution.py:329
  133.6 5.3 %collective-permute-done.2 = f32[16,2048]{1,0:T(8,128)S(1)} collective-permute-done((f32[16,2048]{1,0:T(8,128)S(1)}, f32[16,2048]{1,0:T(8,128)S(1)}, u32[]{:S(2)}, u32[]{:S(2)}) %collective-permute-start.2) | collective-permute-done | bytes 131104 | tf_op jit(solution)/shard_map/ppermute | solution.py:329
  138.9 1.9 %collective-permute-start.3 = (f32[16,2048]{1,0:T(8,128)S(1)}, f32[16,2048]{1,0:T(8,128)S(1)}, u32[]{:S(2)}, u32[]{:S(2)}) collective-permute-start(f32[16,2048]{1,0:T(8,128)S(1)} %get-tuple-element.42), channel_id=1, source_target_pairs={{0,64},{32,96},{64,128},{96,160},{128,192},{160,224},{192,256},{22... | collective-permute-start | bytes 393224 | tf_op jit(solution)/shard_map/ppermute | solution.py:329
  140.9 4.6 %collective-permute-start.6 = (f32[16,2048]{1,0:T(8,128)S(1)}, f32[16,2048]{1,0:T(8,128)S(1)}, u32[]{:S(2)}, u32[]{:S(2)}) collective-permute-start(f32[16,2048]{1,0:T(8,128)S(1)} %get-tuple-element.43), channel_id=1, source_target_pairs={{0,448},{32,480},{64,0},{96,32},{128,64},{160,96},{192,128},{224,1... | collective-permute-start | bytes 393224 | tf_op jit(solution)/shard_map/ppermute | solution.py:329
  147.4 1.9 %collective-permute-start.4 = (f32[16,2048]{1,0:T(8,128)S(1)}, f32[16,2048]{1,0:T(8,128)S(1)}, u32[]{:S(2)}, u32[]{:S(2)}) collective-permute-start(f32[16,2048]{1,0:T(8,128)S(1)} %get-tuple-element.40), channel_id=1, source_target_pairs={{0,64},{32,96},{64,128},{96,160},{128,192},{160,224},{192,256},{22... | collective-permute-start | bytes 393224 | tf_op jit(solution)/shard_map/ppermute | solution.py:329
  149.4 5.3 %collective-permute-start.7 = (f32[16,2048]{1,0:T(8,128)S(1)}, f32[16,2048]{1,0:T(8,128)S(1)}, u32[]{:S(2)}, u32[]{:S(2)}) collective-permute-start(f32[16,2048]{1,0:T(8,128)S(1)} %get-tuple-element.41), channel_id=1, source_target_pairs={{0,448},{32,480},{64,0},{96,32},{128,64},{160,96},{192,128},{224,1... | collective-permute-start | bytes 393224 | tf_op jit(solution)/shard_map/ppermute | solution.py:329
  157.3 5.9 %all-to-all-done.6.parts_ref = f32[32,64,256]{2,1,0:T(8,128)S(1)} async-done(((f32[32,64,256]{2,1,0:T(8,128)}), f32[32,64,256]{2,1,0:T(8,128)S(1)}, u32[]{:S(2)}, u32[]{:S(2)}) %all-to-all-start.6) | async-done | bytes 2097184 | tf_op jit(solution)/shard_map/all_to_all | solution.py:325
  (17 shorter events, 8.4 us)
Async XLA Ops:
  91.7 14.0 %copy-start = (s32[8,128]{1,0:T(8,128)S(1)}, s32[8,128]{1,0:T(8,128)}, u32[]{:S(2)}) copy-start(s32[8,128]{1,0:T(8,128)} %mask_ref.1) | copy-start | bytes 12292
  109.9 53.2 %all-to-all-start.6 = ((f32[32,64,256]{2,1,0:T(8,128)}), f32[32,64,256]{2,1,0:T(8,128)S(1)}, u32[]{:S(2)}, u32[]{:S(2)}) async-start(f32[32,64,256]{2,1,0:T(8,128)} %get-tuple-element.34), calls=%async_computation.6 | async-start | bytes 4194304 | tf_op jit(solution)/shard_map/all_to_all | solution.py:325
  118.2 5.4 %collective-permute-start = (f32[8,16,2048]{2,1,0:T(8,128)S(1)}, f32[8,16,2048]{2,1,0:T(8,128)S(1)}, u32[]{:S(2)}, u32[]{:S(2)}) collective-permute-start(f32[8,16,2048]{2,1,0:T(8,128)S(1)} %get-tuple-element.39), channel_id=1, source_target_pairs={{0,32},{32,0},{64,96},{96,64},{128,160},{160,128},{192,224},{224,1... | collective-permute-start | bytes 3145736 | tf_op jit(solution)/shard_map/ppermute | solution.py:329
  123.8 7.8 %collective-permute-start.1 = (f32[16,2048]{1,0:T(8,128)S(1)}, f32[16,2048]{1,0:T(8,128)S(1)}, u32[]{:S(2)}, u32[]{:S(2)}) collective-permute-start(f32[16,2048]{1,0:T(8,128)S(1)} %get-tuple-element.44), channel_id=1, source_target_pairs={{0,64},{32,96},{64,128},{96,160},{128,192},{160,224},{192,256},{22... | collective-permute-start | bytes 393224 | tf_op jit(solution)/shard_map/ppermute | solution.py:329
  125.8 7.8 %collective-permute-start.5 = (f32[16,2048]{1,0:T(8,128)S(1)}, f32[16,2048]{1,0:T(8,128)S(1)}, u32[]{:S(2)}, u32[]{:S(2)}) collective-permute-start(f32[16,2048]{1,0:T(8,128)S(1)} %get-tuple-element.45), channel_id=1, source_target_pairs={{0,448},{32,480},{64,0},{96,32},{128,64},{160,96},{192,128},{224,1... | collective-permute-start | bytes 393224 | tf_op jit(solution)/shard_map/ppermute | solution.py:329
  131.7 7.2 %collective-permute-start.2 = (f32[16,2048]{1,0:T(8,128)S(1)}, f32[16,2048]{1,0:T(8,128)S(1)}, u32[]{:S(2)}, u32[]{:S(2)}) collective-permute-start(f32[16,2048]{1,0:T(8,128)S(1)} %fusion.4), channel_id=1, source_target_pairs={{0,64},{32,96},{64,128},{96,160},{128,192},{160,224},{192,256},{22... | collective-permute-start | bytes 393224 | tf_op jit(solution)/shard_map/ppermute | solution.py:329
  138.9 7.2 %collective-permute-start.3 = (f32[16,2048]{1,0:T(8,128)S(1)}, f32[16,2048]{1,0:T(8,128)S(1)}, u32[]{:S(2)}, u32[]{:S(2)}) collective-permute-start(f32[16,2048]{1,0:T(8,128)S(1)} %get-tuple-element.42), channel_id=1, source_target_pairs={{0,64},{32,96},{64,128},{96,160},{128,192},{160,224},{192,256},{22... | collective-permute-start | bytes 393224 | tf_op jit(solution)/shard_map/ppermute | solution.py:329
  140.9 6.5 %collective-permute-start.6 = (f32[16,2048]{1,0:T(8,128)S(1)}, f32[16,2048]{1,0:T(8,128)S(1)}, u32[]{:S(2)}, u32[]{:S(2)}) collective-permute-start(f32[16,2048]{1,0:T(8,128)S(1)} %get-tuple-element.43), channel_id=1, source_target_pairs={{0,448},{32,480},{64,0},{96,32},{128,64},{160,96},{192,128},{224,1... | collective-permute-start | bytes 393224 | tf_op jit(solution)/shard_map/ppermute | solution.py:329
  147.4 7.9 %collective-permute-start.4 = (f32[16,2048]{1,0:T(8,128)S(1)}, f32[16,2048]{1,0:T(8,128)S(1)}, u32[]{:S(2)}, u32[]{:S(2)}) collective-permute-start(f32[16,2048]{1,0:T(8,128)S(1)} %get-tuple-element.40), channel_id=1, source_target_pairs={{0,64},{32,96},{64,128},{96,160},{128,192},{160,224},{192,256},{22... | collective-permute-start | bytes 393224 | tf_op jit(solution)/shard_map/ppermute | solution.py:329
  149.4 7.2 %collective-permute-start.7 = (f32[16,2048]{1,0:T(8,128)S(1)}, f32[16,2048]{1,0:T(8,128)S(1)}, u32[]{:S(2)}, u32[]{:S(2)}) collective-permute-start(f32[16,2048]{1,0:T(8,128)S(1)} %get-tuple-element.41), channel_id=1, source_target_pairs={{0,448},{32,480},{64,0},{96,32},{128,64},{160,96},{192,128},{224,1... | collective-permute-start | bytes 393224 | tf_op jit(solution)/shard_map/ppermute | solution.py:329

commit v9 on v8

--- a/solution.py
+++ b/solution.py
@@ -129,7 +129,7 @@
         cols_ref[:, :, cols] = jnp.broadcast_to(line[None], (cols_ref.shape[0], 1, TILE))
         return 0
 
-    lax.fori_loop(0, protos // TILE, teacher_tile, 0, unroll=4)
+    lax.fori_loop(0, protos // TILE, teacher_tile, 0, unroll=8)
     loads[3].wait()
 
     for image in range(images):
@@ -156,7 +156,7 @@
         parts_ref[...] += fold_lanes(exps)
         return 0
 
-    lax.fori_loop(0, protos // TILE, student_tile, 0, unroll=4)
+    lax.fori_loop(0, protos // TILE, student_tile, 0, unroll=8)
     student_rows_ref[...] = lanes_of_rows(parts_ref[...])
 
 
@@ -178,7 +178,7 @@
         parts_ref[rows, :] = total
         return 0
 
-    lax.fori_loop(0, exp_ref.shape[0] // step, block, 0, unroll=2)
+    lax.fori_loop(0, exp_ref.shape[0] // step, block, 0, unroll=4)
     line = lanes_of_rows(parts_ref[...])
     peers, _, width = rows_ref.shape
     rows = line.shape[1]
@@ -213,7 +213,7 @@
             parts_ref[:, start : start + LANES] += total
         return 0
 
-    lax.fori_loop(0, exp_ref.shape[0] // step, block, 0, unroll=2)
+    lax.fori_loop(0, exp_ref.shape[0] // step, block, 0, unroll=4)
     store_copies(cols_ref, jnp.sum(parts_ref[...], axis=0, keepdims=True))
 
 

time: 165 us -> 164 us (level)
  no operation moved by 1% of the time
where the time goes in v9:
time: 164 us; the launch traced here: 163 us
  blocking collectives  92.5 us (56%)
  starting transfers between devices  30 us (18%)
  Pallas kernels  19.8 us (12%)
  waiting for transfers between devices  18.4 us (11%)
    all_to_all x6, blocking collectives, everyones(): return lax.all_to_all(copies, axis, 0, 0, tiled=True)  92.5 us
    ppermute x8, starting transfers between devices, send_rows(): lax.ppermute(values, 'rows', [(i, to(i)) for i in range(lax.axis_size('ro...  25.3 us
    pallas_call x9, Pallas kernels, call(): pl.pallas_call(body, out_shape=[(space[0] if space else pltpu.VMEM)(shape...  19.8 us
    ppermute x8, waiting for transfers between devices, send_rows(): lax.ppermute(values, 'rows', [(i, to(i)) for i in range(lax.axis_size('ro...  12.7 us
    all_to_all x1, waiting for transfers between devices, everyones(): return lax.all_to_all(copies, axis, 0, 0, tiled=True)  5.73 us
    all_to_all x1, starting transfers between devices, everyones(): return lax.all_to_all(copies, axis, 0, 0, tiled=True)  4.76 us
  transfers between devices with their start and end apart: 9, of which 8 were waited for; matrix products, arithmetic and copies ran while one was open for 1% of the time, Pallas kernels for 2%

profile of v9, /device:TPU:1, one launch (start us, length us, event | category | flops | bytes accessed | tf_op | source)
XLA Modules:
  0.0 162.6 jit_solution(376105681533912156)
XLA Ops:
  0.6 6.2 %shard_map.68 = (f32[1024,2048]{1,0:T(8,128)S(1)}, f32[16,1,2048]{2,1,0:T(1,128)S(1)}, f32[1024,2048]{1,0:T(8,128)S(1)}, f32[1,1024]{1,0:T(1,128)S(1)}, f32[1024...) custom-call(bf16[8,256,256]{2,1,0:T(8,128)(2,1)} %teacher_hbm.1, ...), custom_call_target="tpu_custom_call" | custom-call | flops 2147483648 | bytes 8388608 | tf_op jit(solution)/shard_map/pallas_call | solution.py:26
  6.8 20.8 %all_to_all.35.sums_ref = f32[16,1,2048]{2,1,0:T(1,128)S(1)} all-to-all(f32[16,1,2048]{2,1,0:T(1,128)S(1)} %get-tuple-element.21), channel_id=1, replica_groups=mesh['rows'=16,'protos'=32] {'rows'}, dimensions={0} | all-to-all | bytes 262144 | tf_op jit(solution)/shard_map/all_to_all | solution.py:325
  28.8 19.0 %all_to_all.36.sums_ref = f32[32,1,1152]{2,1,0:T(1,128)S(1)} all-to-all(f32[32,1,1152]{2,1,0:T(1,128)S(1)} %get-tuple-element.24), channel_id=1, replica_groups=mesh['rows'=16,'protos'=32] {'protos'}, dimensions={0} | all-to-all | bytes 294912 | tf_op jit(solution)/shard_map/all_to_all | solution.py:325
  48.6 13.3 %all_to_all.37.sums_ref = f32[16,1,2048]{2,1,0:T(1,128)S(1)} all-to-all(f32[16,1,2048]{2,1,0:T(1,128)S(1)} %get-tuple-element.25), channel_id=1, replica_groups=mesh['rows'=16,'protos'=32] {'rows'}, dimensions={0} | all-to-all | bytes 262144 | tf_op jit(solution)/shard_map/all_to_all | solution.py:325
  63.0 13.2 %all_to_all.38.sums_ref.student_ref = f32[32,1,1152]{2,1,0:T(1,128)S(1)} all-to-all(f32[32,1,1152]{2,1,0:T(1,128)S(1)} %get-tuple-element.27), channel_id=1, replica_groups=mesh['rows'=16,'protos'=32] {'protos'}, dimensions={0} | all-to-all | bytes 294912 | tf_op jit(solution)/shard_map/all_to_all | solution.py:325
  77.1 13.4 %all_to_all.39.sums_ref = f32[16,1,2048]{2,1,0:T(1,128)S(1)} all-to-all(f32[16,1,2048]{2,1,0:T(1,128)S(1)} %shard_map.72), channel_id=1, replica_groups=mesh['rows'=16,'protos'=32] {'rows'}, dimensions={0} | all-to-all | bytes 262144 | tf_op jit(solution)/shard_map/all_to_all | solution.py:325
  91.4 13.0 %all_to_all.40.sums_ref = f32[32,1,1024]{2,1,0:T(1,128)S(1)} all-to-all(f32[32,1,1024]{2,1,0:T(1,128)S(1)} %get-tuple-element.28), channel_id=1, replica_groups=mesh['rows'=16,'protos'=32] {'protos'}, dimensions={0} | all-to-all | bytes 262144 | tf_op jit(solution)/shard_map/all_to_all | solution.py:325
  104.4 4.2 %shard_map.74 = (f32[32,64,256]{2,1,0:T(8,128)}, bf16[1024,2048]{1,0:T(8,128)(2,1)}) custom-call(f32[32,1,1024]{2,1,0:T(1,128)S(1)} %all_to_all.40.sums_ref, f32[32,1,1152]{2,1,0:T(1,128)S(1)} %all_to_all.38.sums_ref.student_ref, f32[1,2048]{1,0:T(1,128)S(1)} %get-tuple-element.29.cols_ref, f32[1024,2048]{1,0:T(8,128)S(1)} %get-tuple-element.22.exp_ref.teacher_exp_ref, ...), custom_call_target="tpu_custom_call" | custom-call | flops 1073741824 | bytes 16777216 | tf_op jit(solution)/shard_map/pallas_call | solution.py:26
  108.6 4.8 %all-to-all-start.6 = ((f32[32,64,256]{2,1,0:T(8,128)}), f32[32,64,256]{2,1,0:T(8,128)S(1)}, u32[]{:S(2)}, u32[]{:S(2)}) async-start(f32[32,64,256]{2,1,0:T(8,128)} %get-tuple-element.34), calls=%async_computation.6 | async-start | bytes 4194304 | tf_op jit(solution)/shard_map/all_to_all | solution.py:325
  113.4 3.7 %shard_map.76 = (f32[8,16,2048]{2,1,0:T(8,128)S(1)}, f32[8,16,2048]{2,1,0:T(8,128)S(1)}) custom-call(bf16[1024,2048]{1,0:T(8,128)(2,1)} %get-tuple-element.35.score_hbm, bf16[256,2048]{1,0:T(8,128)(2,1)} %weight_hbm.1, bf16[256,1024]{1,0:T(8,128)(2,1)S(1)} %get-tuple-element.36.turned_ref, f32[1,2048]{1,0:T(1,128)S(1)} %get-tuple-element.37.length_ref), custom_call_target="tpu_custom_call" | custom-call | tf_op jit(solution)/shard_map/pallas_call | solution.py:26
  117.1 3.2 %collective-permute-start = (f32[8,16,2048]{2,1,0:T(8,128)S(1)}, f32[8,16,2048]{2,1,0:T(8,128)S(1)}, u32[]{:S(2)}, u32[]{:S(2)}) collective-permute-start(f32[8,16,2048]{2,1,0:T(8,128)S(1)} %get-tuple-element.39), channel_id=1, source_target_pairs={{0,32},{32,0},{64,96},{96,64},{128,160},{160,128},{192,224},{224,1... | collective-permute-start | bytes 3145736 | tf_op jit(solution)/shard_map/ppermute | solution.py:329
  120.3 2.3 %collective-permute-done = f32[8,16,2048]{2,1,0:T(8,128)S(1)} collective-permute-done((f32[8,16,2048]{2,1,0:T(8,128)S(1)}, f32[8,16,2048]{2,1,0:T(8,128)S(1)}, u32[]{:S(2)}, u32[]{:S(2)}) %collective-permute-start) | collective-permute-done | bytes 1048608 | tf_op jit(solution)/shard_map/ppermute | solution.py:329
  122.7 2.0 %collective-permute-start.1 = (f32[16,2048]{1,0:T(8,128)S(1)}, f32[16,2048]{1,0:T(8,128)S(1)}, u32[]{:S(2)}, u32[]{:S(2)}) collective-permute-start(f32[16,2048]{1,0:T(8,128)S(1)} %get-tuple-element.44), channel_id=1, source_target_pairs={{0,64},{32,96},{64,128},{96,160},{128,192},{160,224},{192,256},{22... | collective-permute-start | bytes 393224 | tf_op jit(solution)/shard_map/ppermute | solution.py:329
  124.7 4.5 %collective-permute-start.5 = (f32[16,2048]{1,0:T(8,128)S(1)}, f32[16,2048]{1,0:T(8,128)S(1)}, u32[]{:S(2)}, u32[]{:S(2)}) collective-permute-start(f32[16,2048]{1,0:T(8,128)S(1)} %get-tuple-element.45), channel_id=1, source_target_pairs={{0,448},{32,480},{64,0},{96,32},{128,64},{160,96},{192,128},{224,1... | collective-permute-start | bytes 393224 | tf_op jit(solution)/shard_map/ppermute | solution.py:329
  129.2 1.3 collective-permute-done.1
  130.5 1.9 %collective-permute-start.2 = (f32[16,2048]{1,0:T(8,128)S(1)}, f32[16,2048]{1,0:T(8,128)S(1)}, u32[]{:S(2)}, u32[]{:S(2)}) collective-permute-start(f32[16,2048]{1,0:T(8,128)S(1)} %fusion.4), channel_id=1, source_target_pairs={{0,64},{32,96},{64,128},{96,160},{128,192},{160,224},{192,256},{22... | collective-permute-start | bytes 393224 | tf_op jit(solution)/shard_map/ppermute | solution.py:329
  132.5 5.3 %collective-permute-done.2 = f32[16,2048]{1,0:T(8,128)S(1)} collective-permute-done((f32[16,2048]{1,0:T(8,128)S(1)}, f32[16,2048]{1,0:T(8,128)S(1)}, u32[]{:S(2)}, u32[]{:S(2)}) %collective-permute-start.2) | collective-permute-done | bytes 131104 | tf_op jit(solution)/shard_map/ppermute | solution.py:329
  137.8 1.9 %collective-permute-start.3 = (f32[16,2048]{1,0:T(8,128)S(1)}, f32[16,2048]{1,0:T(8,128)S(1)}, u32[]{:S(2)}, u32[]{:S(2)}) collective-permute-start(f32[16,2048]{1,0:T(8,128)S(1)} %get-tuple-element.42), channel_id=1, source_target_pairs={{0,64},{32,96},{64,128},{96,160},{128,192},{160,224},{192,256},{22... | collective-permute-start | bytes 393224 | tf_op jit(solution)/shard_map/ppermute | solution.py:329
  139.7 4.6 %collective-permute-start.6 = (f32[16,2048]{1,0:T(8,128)S(1)}, f32[16,2048]{1,0:T(8,128)S(1)}, u32[]{:S(2)}, u32[]{:S(2)}) collective-permute-start(f32[16,2048]{1,0:T(8,128)S(1)} %get-tuple-element.43), channel_id=1, source_target_pairs={{0,448},{32,480},{64,0},{96,32},{128,64},{160,96},{192,128},{224,1... | collective-permute-start | bytes 393224 | tf_op jit(solution)/shard_map/ppermute | solution.py:329
  145.0 1.2 collective-permute-done.6
  146.3 1.9 %collective-permute-start.4 = (f32[16,2048]{1,0:T(8,128)S(1)}, f32[16,2048]{1,0:T(8,128)S(1)}, u32[]{:S(2)}, u32[]{:S(2)}) collective-permute-start(f32[16,2048]{1,0:T(8,128)S(1)} %get-tuple-element.40), channel_id=1, source_target_pairs={{0,64},{32,96},{64,128},{96,160},{128,192},{160,224},{192,256},{22... | collective-permute-start | bytes 393224 | tf_op jit(solution)/shard_map/ppermute | solution.py:329
  148.2 5.3 %collective-permute-start.7 = (f32[16,2048]{1,0:T(8,128)S(1)}, f32[16,2048]{1,0:T(8,128)S(1)}, u32[]{:S(2)}, u32[]{:S(2)}) collective-permute-start(f32[16,2048]{1,0:T(8,128)S(1)} %get-tuple-element.41), channel_id=1, source_target_pairs={{0,448},{32,480},{64,0},{96,32},{128,64},{160,96},{192,128},{224,1... | collective-permute-start | bytes 393224 | tf_op jit(solution)/shard_map/ppermute | solution.py:329
  154.2 1.2 collective-permute-done.7
  156.1 5.7 %all-to-all-done.6.parts_ref = f32[32,64,256]{2,1,0:T(8,128)S(1)} async-done(((f32[32,64,256]{2,1,0:T(8,128)}), f32[32,64,256]{2,1,0:T(8,128)S(1)}, u32[]{:S(2)}, u32[]{:S(2)}) %all-to-all-start.6) | async-done | bytes 2097184 | tf_op jit(solution)/shard_map/all_to_all | solution.py:325
  (17 shorter events, 8.1 us)
Async XLA Ops:
  90.5 13.9 %copy-start = (s32[8,128]{1,0:T(8,128)S(1)}, s32[8,128]{1,0:T(8,128)}, u32[]{:S(2)}) copy-start(s32[8,128]{1,0:T(8,128)} %mask_ref.1) | copy-start | bytes 12292
  108.6 53.2 %all-to-all-start.6 = ((f32[32,64,256]{2,1,0:T(8,128)}), f32[32,64,256]{2,1,0:T(8,128)S(1)}, u32[]{:S(2)}, u32[]{:S(2)}) async-start(f32[32,64,256]{2,1,0:T(8,128)} %get-tuple-element.34), calls=%async_computation.6 | async-start | bytes 4194304 | tf_op jit(solution)/shard_map/all_to_all | solution.py:325
  117.1 5.4 %collective-permute-start = (f32[8,16,2048]{2,1,0:T(8,128)S(1)}, f32[8,16,2048]{2,1,0:T(8,128)S(1)}, u32[]{:S(2)}, u32[]{:S(2)}) collective-permute-start(f32[8,16,2048]{2,1,0:T(8,128)S(1)} %get-tuple-element.39), channel_id=1, source_target_pairs={{0,32},{32,0},{64,96},{96,64},{128,160},{160,128},{192,224},{224,1... | collective-permute-start | bytes 3145736 | tf_op jit(solution)/shard_map/ppermute | solution.py:329
  122.7 7.8 %collective-permute-start.1 = (f32[16,2048]{1,0:T(8,128)S(1)}, f32[16,2048]{1,0:T(8,128)S(1)}, u32[]{:S(2)}, u32[]{:S(2)}) collective-permute-start(f32[16,2048]{1,0:T(8,128)S(1)} %get-tuple-element.44), channel_id=1, source_target_pairs={{0,64},{32,96},{64,128},{96,160},{128,192},{160,224},{192,256},{22... | collective-permute-start | bytes 393224 | tf_op jit(solution)/shard_map/ppermute | solution.py:329
  124.7 7.8 %collective-permute-start.5 = (f32[16,2048]{1,0:T(8,128)S(1)}, f32[16,2048]{1,0:T(8,128)S(1)}, u32[]{:S(2)}, u32[]{:S(2)}) collective-permute-start(f32[16,2048]{1,0:T(8,128)S(1)} %get-tuple-element.45), channel_id=1, source_target_pairs={{0,448},{32,480},{64,0},{96,32},{128,64},{160,96},{192,128},{224,1... | collective-permute-start | bytes 393224 | tf_op jit(solution)/shard_map/ppermute | solution.py:329
  130.5 7.2 %collective-permute-start.2 = (f32[16,2048]{1,0:T(8,128)S(1)}, f32[16,2048]{1,0:T(8,128)S(1)}, u32[]{:S(2)}, u32[]{:S(2)}) collective-permute-start(f32[16,2048]{1,0:T(8,128)S(1)} %fusion.4), channel_id=1, source_target_pairs={{0,64},{32,96},{64,128},{96,160},{128,192},{160,224},{192,256},{22... | collective-permute-start | bytes 393224 | tf_op jit(solution)/shard_map/ppermute | solution.py:329
  137.8 7.2 %collective-permute-start.3 = (f32[16,2048]{1,0:T(8,128)S(1)}, f32[16,2048]{1,0:T(8,128)S(1)}, u32[]{:S(2)}, u32[]{:S(2)}) collective-permute-start(f32[16,2048]{1,0:T(8,128)S(1)} %get-tuple-element.42), channel_id=1, source_target_pairs={{0,64},{32,96},{64,128},{96,160},{128,192},{160,224},{192,256},{22... | collective-permute-start | bytes 393224 | tf_op jit(solution)/shard_map/ppermute | solution.py:329
  139.7 6.5 %collective-permute-start.6 = (f32[16,2048]{1,0:T(8,128)S(1)}, f32[16,2048]{1,0:T(8,128)S(1)}, u32[]{:S(2)}, u32[]{:S(2)}) collective-permute-start(f32[16,2048]{1,0:T(8,128)S(1)} %get-tuple-element.43), channel_id=1, source_target_pairs={{0,448},{32,480},{64,0},{96,32},{128,64},{160,96},{192,128},{224,1... | collective-permute-start | bytes 393224 | tf_op jit(solution)/shard_map/ppermute | solution.py:329
  146.3 7.9 %collective-permute-start.4 = (f32[16,2048]{1,0:T(8,128)S(1)}, f32[16,2048]{1,0:T(8,128)S(1)}, u32[]{:S(2)}, u32[]{:S(2)}) collective-permute-start(f32[16,2048]{1,0:T(8,128)S(1)} %get-tuple-element.40), channel_id=1, source_target_pairs={{0,64},{32,96},{64,128},{96,160},{128,192},{160,224},{192,256},{22... | collective-permute-start | bytes 393224 | tf_op jit(solution)/shard_map/ppermute | solution.py:329
  148.2 7.2 %collective-permute-start.7 = (f32[16,2048]{1,0:T(8,128)S(1)}, f32[16,2048]{1,0:T(8,128)S(1)}, u32[]{:S(2)}, u32[]{:S(2)}) collective-permute-start(f32[16,2048]{1,0:T(8,128)S(1)} %get-tuple-element.41), channel_id=1, source_target_pairs={{0,448},{32,480},{64,0},{96,32},{128,64},{160,96},{192,128},{224,1... | collective-permute-start | bytes 393224 | tf_op jit(solution)/shard_map/ppermute | solution.py:329

commit v10 on v9

--- a/solution.py
+++ b/solution.py
@@ -107,11 +107,13 @@
             )
         )
     ]
-    for load in loads:
+    for load in loads[:3]:
         load.start()
     loads[0].wait()
     positions = mask_ref[...].astype(f32).T
     loads[1].wait()
+    for load in loads[3:]:
+        load.start()
     for image in range(images):
         picked = pick(teacher_ref, positions, image)
         length = jnp.sqrt(jnp.sum(picked * picked, axis=1, keepdims=True) + epsilon)
@@ -178,7 +180,7 @@
         parts_ref[rows, :] = total
         return 0
 
-    lax.fori_loop(0, exp_ref.shape[0] // step, block, 0, unroll=4)
+    lax.fori_loop(0, exp_ref.shape[0] // step, block, 0, unroll=8)
     line = lanes_of_rows(parts_ref[...])
     peers, _, width = rows_ref.shape
     rows = line.shape[1]
@@ -213,7 +215,7 @@
             parts_ref[:, start : start + LANES] += total
         return 0
 
-    lax.fori_loop(0, exp_ref.shape[0] // step, block, 0, unroll=4)
+    lax.fori_loop(0, exp_ref.shape[0] // step, block, 0, unroll=8)
     store_copies(cols_ref, jnp.sum(parts_ref[...], axis=0, keepdims=True))
 
 

time: 164 us -> 164 us (level)
  no operation moved by 1% of the time
where the time goes in v10:
time: 164 us; the launch traced here: 162 us
  blocking collectives  92.6 us (56%)
  starting transfers between devices  29.9 us (18%)
  Pallas kernels  19.6 us (12%)
  waiting for transfers between devices  18.6 us (11%)
    all_to_all x6, blocking collectives, everyones(): return lax.all_to_all(copies, axis, 0, 0, tiled=True)  92.6 us
    ppermute x8, starting transfers between devices, send_rows(): lax.ppermute(values, 'rows', [(i, to(i)) for i in range(lax.axis_size('ro...  25.3 us
    pallas_call x9, Pallas kernels, call(): pl.pallas_call(body, out_shape=[(space[0] if space else pltpu.VMEM)(shape...  19.6 us
    ppermute x8, waiting for transfers between devices, send_rows(): lax.ppermute(values, 'rows', [(i, to(i)) for i in range(lax.axis_size('ro...  12.7 us
    all_to_all x1, waiting for transfers between devices, everyones(): return lax.all_to_all(copies, axis, 0, 0, tiled=True)  5.91 us
    all_to_all x1, starting transfers between devices, everyones(): return lax.all_to_all(copies, axis, 0, 0, tiled=True)  4.58 us
  transfers between devices with their start and end apart: 9, of which 8 were waited for; matrix products, arithmetic and copies ran while one was open for 1% of the time, Pallas kernels for 2%

profile of v10, /device:TPU:1, one launch (start us, length us, event | category | flops | bytes accessed | tf_op | source)
XLA Modules:
  0.0 162.4 jit_solution(17339380834424142232)
XLA Ops:
  0.6 6.2 %shard_map.68 = (f32[1024,2048]{1,0:T(8,128)S(1)}, f32[16,1,2048]{2,1,0:T(1,128)S(1)}, f32[1024,2048]{1,0:T(8,128)S(1)}, f32[1,1024]{1,0:T(1,128)S(1)}, f32[1024...) custom-call(bf16[8,256,256]{2,1,0:T(8,128)(2,1)} %teacher_hbm.1, ...), custom_call_target="tpu_custom_call" | custom-call | flops 2147483648 | bytes 8388608 | tf_op jit(solution)/shard_map/pallas_call | solution.py:26
  6.8 20.8 %all_to_all.35.sums_ref = f32[16,1,2048]{2,1,0:T(1,128)S(1)} all-to-all(f32[16,1,2048]{2,1,0:T(1,128)S(1)} %get-tuple-element.21), channel_id=1, replica_groups=mesh['rows'=16,'protos'=32] {'rows'}, dimensions={0} | all-to-all | bytes 262144 | tf_op jit(solution)/shard_map/all_to_all | solution.py:327
  28.7 19.0 %all_to_all.36.sums_ref = f32[32,1,1152]{2,1,0:T(1,128)S(1)} all-to-all(f32[32,1,1152]{2,1,0:T(1,128)S(1)} %get-tuple-element.24), channel_id=1, replica_groups=mesh['rows'=16,'protos'=32] {'protos'}, dimensions={0} | all-to-all | bytes 294912 | tf_op jit(solution)/shard_map/all_to_all | solution.py:327
  48.5 13.3 %all_to_all.37.sums_ref = f32[16,1,2048]{2,1,0:T(1,128)S(1)} all-to-all(f32[16,1,2048]{2,1,0:T(1,128)S(1)} %get-tuple-element.25), channel_id=1, replica_groups=mesh['rows'=16,'protos'=32] {'rows'}, dimensions={0} | all-to-all | bytes 262144 | tf_op jit(solution)/shard_map/all_to_all | solution.py:327
  62.9 13.2 %all_to_all.38.sums_ref.student_ref = f32[32,1,1152]{2,1,0:T(1,128)S(1)} all-to-all(f32[32,1,1152]{2,1,0:T(1,128)S(1)} %get-tuple-element.27), channel_id=1, replica_groups=mesh['rows'=16,'protos'=32] {'protos'}, dimensions={0} | all-to-all | bytes 294912 | tf_op jit(solution)/shard_map/all_to_all | solution.py:327
  76.9 13.4 %all_to_all.39.sums_ref = f32[16,1,2048]{2,1,0:T(1,128)S(1)} all-to-all(f32[16,1,2048]{2,1,0:T(1,128)S(1)} %shard_map.72), channel_id=1, replica_groups=mesh['rows'=16,'protos'=32] {'rows'}, dimensions={0} | all-to-all | bytes 262144 | tf_op jit(solution)/shard_map/all_to_all | solution.py:327
  91.2 13.0 %all_to_all.40.sums_ref = f32[32,1,1024]{2,1,0:T(1,128)S(1)} all-to-all(f32[32,1,1024]{2,1,0:T(1,128)S(1)} %get-tuple-element.28), channel_id=1, replica_groups=mesh['rows'=16,'protos'=32] {'protos'}, dimensions={0} | all-to-all | bytes 262144 | tf_op jit(solution)/shard_map/all_to_all | solution.py:327
  104.2 4.2 %shard_map.74 = (f32[32,64,256]{2,1,0:T(8,128)}, bf16[1024,2048]{1,0:T(8,128)(2,1)}) custom-call(f32[32,1,1024]{2,1,0:T(1,128)S(1)} %all_to_all.40.sums_ref, f32[32,1,1152]{2,1,0:T(1,128)S(1)} %all_to_all.38.sums_ref.student_ref, f32[1,2048]{1,0:T(1,128)S(1)} %get-tuple-element.29.cols_ref, f32[1024,2048]{1,0:T(8,128)S(1)} %get-tuple-element.22.exp_ref.teacher_exp_ref, ...), custom_call_target="tpu_custom_call" | custom-call | flops 1073741824 | bytes 16777216 | tf_op jit(solution)/shard_map/pallas_call | solution.py:26
  108.4 4.6 %all-to-all-start.6 = ((f32[32,64,256]{2,1,0:T(8,128)}), f32[32,64,256]{2,1,0:T(8,128)S(1)}, u32[]{:S(2)}, u32[]{:S(2)}) async-start(f32[32,64,256]{2,1,0:T(8,128)} %get-tuple-element.34), calls=%async_computation.6 | async-start | bytes 4194304 | tf_op jit(solution)/shard_map/all_to_all | solution.py:327
  113.0 3.7 %shard_map.76 = (f32[8,16,2048]{2,1,0:T(8,128)S(1)}, f32[8,16,2048]{2,1,0:T(8,128)S(1)}) custom-call(bf16[1024,2048]{1,0:T(8,128)(2,1)} %get-tuple-element.35.score_hbm, bf16[256,2048]{1,0:T(8,128)(2,1)} %weight_hbm.1, bf16[256,1024]{1,0:T(8,128)(2,1)S(1)} %get-tuple-element.36.turned_ref, f32[1,2048]{1,0:T(1,128)S(1)} %get-tuple-element.37.length_ref), custom_call_target="tpu_custom_call" | custom-call | tf_op jit(solution)/shard_map/pallas_call | solution.py:26
  116.7 3.2 %collective-permute-start = (f32[8,16,2048]{2,1,0:T(8,128)S(1)}, f32[8,16,2048]{2,1,0:T(8,128)S(1)}, u32[]{:S(2)}, u32[]{:S(2)}) collective-permute-start(f32[8,16,2048]{2,1,0:T(8,128)S(1)} %get-tuple-element.39), channel_id=1, source_target_pairs={{0,32},{32,0},{64,96},{96,64},{128,160},{160,128},{192,224},{224,1... | collective-permute-start | bytes 3145736 | tf_op jit(solution)/shard_map/ppermute | solution.py:331
  119.9 2.3 %collective-permute-done = f32[8,16,2048]{2,1,0:T(8,128)S(1)} collective-permute-done((f32[8,16,2048]{2,1,0:T(8,128)S(1)}, f32[8,16,2048]{2,1,0:T(8,128)S(1)}, u32[]{:S(2)}, u32[]{:S(2)}) %collective-permute-start) | collective-permute-done | bytes 1048608 | tf_op jit(solution)/shard_map/ppermute | solution.py:331
  122.3 2.0 %collective-permute-start.1 = (f32[16,2048]{1,0:T(8,128)S(1)}, f32[16,2048]{1,0:T(8,128)S(1)}, u32[]{:S(2)}, u32[]{:S(2)}) collective-permute-start(f32[16,2048]{1,0:T(8,128)S(1)} %get-tuple-element.44), channel_id=1, source_target_pairs={{0,64},{32,96},{64,128},{96,160},{128,192},{160,224},{192,256},{22... | collective-permute-start | bytes 393224 | tf_op jit(solution)/shard_map/ppermute | solution.py:331
  124.3 4.5 %collective-permute-start.5 = (f32[16,2048]{1,0:T(8,128)S(1)}, f32[16,2048]{1,0:T(8,128)S(1)}, u32[]{:S(2)}, u32[]{:S(2)}) collective-permute-start(f32[16,2048]{1,0:T(8,128)S(1)} %get-tuple-element.45), channel_id=1, source_target_pairs={{0,448},{32,480},{64,0},{96,32},{128,64},{160,96},{192,128},{224,1... | collective-permute-start | bytes 393224 | tf_op jit(solution)/shard_map/ppermute | solution.py:331
  128.8 1.3 collective-permute-done.1
  130.2 1.9 %collective-permute-start.2 = (f32[16,2048]{1,0:T(8,128)S(1)}, f32[16,2048]{1,0:T(8,128)S(1)}, u32[]{:S(2)}, u32[]{:S(2)}) collective-permute-start(f32[16,2048]{1,0:T(8,128)S(1)} %fusion.4), channel_id=1, source_target_pairs={{0,64},{32,96},{64,128},{96,160},{128,192},{160,224},{192,256},{22... | collective-permute-start | bytes 393224 | tf_op jit(solution)/shard_map/ppermute | solution.py:331
  132.1 5.3 %collective-permute-done.2 = f32[16,2048]{1,0:T(8,128)S(1)} collective-permute-done((f32[16,2048]{1,0:T(8,128)S(1)}, f32[16,2048]{1,0:T(8,128)S(1)}, u32[]{:S(2)}, u32[]{:S(2)}) %collective-permute-start.2) | collective-permute-done | bytes 131104 | tf_op jit(solution)/shard_map/ppermute | solution.py:331
  137.4 1.9 %collective-permute-start.3 = (f32[16,2048]{1,0:T(8,128)S(1)}, f32[16,2048]{1,0:T(8,128)S(1)}, u32[]{:S(2)}, u32[]{:S(2)}) collective-permute-start(f32[16,2048]{1,0:T(8,128)S(1)} %get-tuple-element.42), channel_id=1, source_target_pairs={{0,64},{32,96},{64,128},{96,160},{128,192},{160,224},{192,256},{22... | collective-permute-start | bytes 393224 | tf_op jit(solution)/shard_map/ppermute | solution.py:331
  139.3 4.6 %collective-permute-start.6 = (f32[16,2048]{1,0:T(8,128)S(1)}, f32[16,2048]{1,0:T(8,128)S(1)}, u32[]{:S(2)}, u32[]{:S(2)}) collective-permute-start(f32[16,2048]{1,0:T(8,128)S(1)} %get-tuple-element.43), channel_id=1, source_target_pairs={{0,448},{32,480},{64,0},{96,32},{128,64},{160,96},{192,128},{224,1... | collective-permute-start | bytes 393224 | tf_op jit(solution)/shard_map/ppermute | solution.py:331
  144.6 1.2 collective-permute-done.6
  145.9 1.9 %collective-permute-start.4 = (f32[16,2048]{1,0:T(8,128)S(1)}, f32[16,2048]{1,0:T(8,128)S(1)}, u32[]{:S(2)}, u32[]{:S(2)}) collective-permute-start(f32[16,2048]{1,0:T(8,128)S(1)} %get-tuple-element.40), channel_id=1, source_target_pairs={{0,64},{32,96},{64,128},{96,160},{128,192},{160,224},{192,256},{22... | collective-permute-start | bytes 393224 | tf_op jit(solution)/shard_map/ppermute | solution.py:331
  147.8 5.3 %collective-permute-start.7 = (f32[16,2048]{1,0:T(8,128)S(1)}, f32[16,2048]{1,0:T(8,128)S(1)}, u32[]{:S(2)}, u32[]{:S(2)}) collective-permute-start(f32[16,2048]{1,0:T(8,128)S(1)} %get-tuple-element.41), channel_id=1, source_target_pairs={{0,448},{32,480},{64,0},{96,32},{128,64},{160,96},{192,128},{224,1... | collective-permute-start | bytes 393224 | tf_op jit(solution)/shard_map/ppermute | solution.py:331
  153.8 1.2 collective-permute-done.7
  155.7 5.9 %all-to-all-done.6.parts_ref = f32[32,64,256]{2,1,0:T(8,128)S(1)} async-done(((f32[32,64,256]{2,1,0:T(8,128)}), f32[32,64,256]{2,1,0:T(8,128)S(1)}, u32[]{:S(2)}, u32[]{:S(2)}) %all-to-all-start.6) | async-done | bytes 2097184 | tf_op jit(solution)/shard_map/all_to_all | solution.py:327
  (17 shorter events, 7.9 us)
Async XLA Ops:
  90.3 13.9 %copy-start = (s32[8,128]{1,0:T(8,128)S(1)}, s32[8,128]{1,0:T(8,128)}, u32[]{:S(2)}) copy-start(s32[8,128]{1,0:T(8,128)} %mask_ref.1) | copy-start | bytes 12292
  108.4 53.2 %all-to-all-start.6 = ((f32[32,64,256]{2,1,0:T(8,128)}), f32[32,64,256]{2,1,0:T(8,128)S(1)}, u32[]{:S(2)}, u32[]{:S(2)}) async-start(f32[32,64,256]{2,1,0:T(8,128)} %get-tuple-element.34), calls=%async_computation.6 | async-start | bytes 4194304 | tf_op jit(solution)/shard_map/all_to_all | solution.py:327
  116.7 5.4 %collective-permute-start = (f32[8,16,2048]{2,1,0:T(8,128)S(1)}, f32[8,16,2048]{2,1,0:T(8,128)S(1)}, u32[]{:S(2)}, u32[]{:S(2)}) collective-permute-start(f32[8,16,2048]{2,1,0:T(8,128)S(1)} %get-tuple-element.39), channel_id=1, source_target_pairs={{0,32},{32,0},{64,96},{96,64},{128,160},{160,128},{192,224},{224,1... | collective-permute-start | bytes 3145736 | tf_op jit(solution)/shard_map/ppermute | solution.py:331
  122.3 7.8 %collective-permute-start.1 = (f32[16,2048]{1,0:T(8,128)S(1)}, f32[16,2048]{1,0:T(8,128)S(1)}, u32[]{:S(2)}, u32[]{:S(2)}) collective-permute-start(f32[16,2048]{1,0:T(8,128)S(1)} %get-tuple-element.44), channel_id=1, source_target_pairs={{0,64},{32,96},{64,128},{96,160},{128,192},{160,224},{192,256},{22... | collective-permute-start | bytes 393224 | tf_op jit(solution)/shard_map/ppermute | solution.py:331
  124.3 7.8 %collective-permute-start.5 = (f32[16,2048]{1,0:T(8,128)S(1)}, f32[16,2048]{1,0:T(8,128)S(1)}, u32[]{:S(2)}, u32[]{:S(2)}) collective-permute-start(f32[16,2048]{1,0:T(8,128)S(1)} %get-tuple-element.45), channel_id=1, source_target_pairs={{0,448},{32,480},{64,0},{96,32},{128,64},{160,96},{192,128},{224,1... | collective-permute-start | bytes 393224 | tf_op jit(solution)/shard_map/ppermute | solution.py:331
  130.2 7.2 %collective-permute-start.2 = (f32[16,2048]{1,0:T(8,128)S(1)}, f32[16,2048]{1,0:T(8,128)S(1)}, u32[]{:S(2)}, u32[]{:S(2)}) collective-permute-start(f32[16,2048]{1,0:T(8,128)S(1)} %fusion.4), channel_id=1, source_target_pairs={{0,64},{32,96},{64,128},{96,160},{128,192},{160,224},{192,256},{22... | collective-permute-start | bytes 393224 | tf_op jit(solution)/shard_map/ppermute | solution.py:331
  137.4 7.2 %collective-permute-start.3 = (f32[16,2048]{1,0:T(8,128)S(1)}, f32[16,2048]{1,0:T(8,128)S(1)}, u32[]{:S(2)}, u32[]{:S(2)}) collective-permute-start(f32[16,2048]{1,0:T(8,128)S(1)} %get-tuple-element.42), channel_id=1, source_target_pairs={{0,64},{32,96},{64,128},{96,160},{128,192},{160,224},{192,256},{22... | collective-permute-start | bytes 393224 | tf_op jit(solution)/shard_map/ppermute | solution.py:331
  139.3 6.5 %collective-permute-start.6 = (f32[16,2048]{1,0:T(8,128)S(1)}, f32[16,2048]{1,0:T(8,128)S(1)}, u32[]{:S(2)}, u32[]{:S(2)}) collective-permute-start(f32[16,2048]{1,0:T(8,128)S(1)} %get-tuple-element.43), channel_id=1, source_target_pairs={{0,448},{32,480},{64,0},{96,32},{128,64},{160,96},{192,128},{224,1... | collective-permute-start | bytes 393224 | tf_op jit(solution)/shard_map/ppermute | solution.py:331
  145.9 7.9 %collective-permute-start.4 = (f32[16,2048]{1,0:T(8,128)S(1)}, f32[16,2048]{1,0:T(8,128)S(1)}, u32[]{:S(2)}, u32[]{:S(2)}) collective-permute-start(f32[16,2048]{1,0:T(8,128)S(1)} %get-tuple-element.40), channel_id=1, source_target_pairs={{0,64},{32,96},{64,128},{96,160},{128,192},{160,224},{192,256},{22... | collective-permute-start | bytes 393224 | tf_op jit(solution)/shard_map/ppermute | solution.py:331
  147.8 7.2 %collective-permute-start.7 = (f32[16,2048]{1,0:T(8,128)S(1)}, f32[16,2048]{1,0:T(8,128)S(1)}, u32[]{:S(2)}, u32[]{:S(2)}) collective-permute-start(f32[16,2048]{1,0:T(8,128)S(1)} %get-tuple-element.41), channel_id=1, source_target_pairs={{0,448},{32,480},{64,0},{96,32},{128,64},{160,96},{192,128},{224,1... | collective-permute-start | bytes 393224 | tf_op jit(solution)/shard_map/ppermute | solution.py:331
